TPU v7x, 512 devices: a whole 4x8x8 slice. The times are simulated.
512 devices in a mesh: rep: 64 (over z_lo, y, x), fsdp: 8 (over z_hi, core).
Axes of the slice: x: 4, y: 8, z: 8 (z_hi: 4, z_lo: 2; z = z_hi * 2 + z_lo), core: 2. Of those that a mesh axis runs over, the one named last changes fastest.
Arguments:
- numerator: bfloat16 [64, 2560, 2560], P('rep', None, 'fsdp'), may hold values from -6 to 6
- push_weight: float32 [64], P('rep'), may hold values from 0.5 to 2
- norm_gain: float32 [2560], replicated, may hold values from 0.1 to 1.9
- activations: bfloat16 [2, 45056, 2560], P(None, ('rep', 'fsdp')), may hold values from -40 to 40, as said below
- cotangent: bfloat16 [2, 45056, 2560], P(None, ('rep', 'fsdp')), may hold values from -6 to 6
- step_index: int32 [], replicated, may hold values from 0 to 999
Outputs:
- mixed: bfloat16 [64, 2560, 2560], P('rep', None, 'fsdp')
- new_weight: float32 [64], P('rep')
Inputs may be any that keep to these rules, and one draw needn't show every extreme that they name: `activations`: Per-token and per-feature scales vary.
All inputs are finite; a program needn't handle non-finite values.
Results may differ from a plain program's by a relative error of at most 0.0075.
Values may be sent and summed in bfloat16 or wider, within the bound.
No kernel may reach another device: no remote copies, remote signals or barrier semaphores. Data moves between devices by JAX's collectives and lax.ppermute only.
A program may use at most 64 MiB of HBM per device.

v0:
```python
from functools import partial

import jax
import jax.numpy as jnp
from jax import lax
from jax.sharding import PartitionSpec as P

DW = 2560


LEARN_RATE = 1.5
EPSILON = 1e-05


def shifted(block, axis, distance):
    devices = range(lax.axis_size(axis))
    route = [((i - distance) % len(devices), i) for i in devices]
    return lax.ppermute(block, axis, route)


def silu_slope(pre_act):
    sig = jax.nn.sigmoid(pre_act)
    return sig * (1.0 + pre_act * (1.0 - sig))


def add_piece(total, piece, start, eff_weight, cot_block):
    scale = DW ** (-0.5)
    pre_act = scale * jnp.einsum(
        "mrd,dh->mrh", piece, eff_weight, preferred_element_type=jnp.float32
    )
    grad_out = (cot_block.astype(jnp.float32) * silu_slope(pre_act)).astype(jnp.bfloat16)
    return total + scale * jnp.einsum(
        "mrd,mrh->dh", piece, grad_out, preferred_element_type=jnp.float32
    )


def send_state(state, hop_size):
    return shifted(state, "rep", hop_size)


def to_partner(sender, state, step_index):
    bit_count = lax.axis_size("rep").bit_length() - 1
    branches = [partial(sender, hop_size=2**bit) for bit in range(bit_count)]
    return lax.switch(step_index % bit_count, branches, state)


def on_device(numerator, push_weight, norm_gain, activations, cotangent, step_index):
    wide = activations.astype(jnp.float32)
    mean_square = jnp.mean(wide * wide, axis=-1, keepdims=True)
    normed = (wide * lax.rsqrt(mean_square + EPSILON) * norm_gain).astype(jnp.bfloat16)
    eff_weight = (numerator[0].astype(jnp.float32) / push_weight[0]).astype(jnp.bfloat16)
    cot_cols = lax.all_to_all(cotangent, "fsdp", split_axis=2, concat_axis=1, tiled=True)
    total = jnp.zeros((normed.shape[2], eff_weight.shape[1]), jnp.float32)
    for micro in range(normed.shape[0]):
        folder = partial(add_piece, eff_weight=eff_weight, cot_block=cot_cols[micro : micro + 1])
        total = folder(
            total,
            lax.all_gather(normed[micro : micro + 1], "fsdp", axis=1, tiled=True),
            jnp.int32(0),
        )
    update = (LEARN_RATE * total).astype(jnp.bfloat16)[None]
    local = numerator.astype(jnp.float32) - update.astype(jnp.float32)
    partner_local, partner_weight = to_partner(send_state, (local, push_weight), step_index)
    mixed = (0.5 * local + 0.5 * partner_local).astype(jnp.bfloat16)
    new_weight = 0.5 * (push_weight + partner_weight)
    return (mixed, new_weight)


def solution(mesh):
    placed = (
        P("rep", None, "fsdp"),
        P("rep"),
        P(),
        P(None, ("rep", "fsdp"), None),
        P(None, ("rep", "fsdp"), None),
        P(),
    )
    return jax.shard_map(
        on_device,
        mesh=mesh,
        in_specs=placed,
        out_specs=(P("rep", None, "fsdp"), P("rep")),
        check_vma=False,
    )
```

profile of v0, /device:TPU:1, one launch (start us, length us, event | category | flops | bytes accessed | tf_op | source)
XLA Modules:
  0.0 241.5 jit_solution(3747886004429166590)
XLA Ops:
  7.2 0.0 all-gather.3.cloned.1.call-start
  7.2 1.5 fusion.12
  8.7 1.5 fusion.14
  10.2 1.0 fusion.43
  11.2 0.0 all-gather.5.cloned.1.call-start
  11.3 0.7 all-gather.5.cloned.1.call-update
  12.0 2.2 copy.26
  14.2 11.8 %all-to-all-start = ((bf16[2,88,2560]{1,0,2:T(2,128)(2,1)}), bf16[2,88,2560]{1,0,2:T(2,128)(2,1)S(1)}, u32[]{:S(2)}, u32[]{:S(2)}) async-start(bf16[2,88,2560]{1,0,2:T(2,128)(2,1)} %copy.26), calls=%async_computation | async-start | bytes 2621440 | tf_op jit(solution)/shard_map/all_to_all | solution.py:52
  27.3 36.4 %all-to-all-done = bf16[2,88,2560]{1,0,2:T(2,128)(2,1)S(1)} async-done(((bf16[2,88,2560]{1,0,2:T(2,128)(2,1)}), bf16[2,88,2560]{1,0,2:T(2,128)(2,1)S(1)}, u32[]{:S(2)}, u32[]{:S(2)}) %all-to-all-start) | async-done | bytes 901152 | tf_op jit(solution)/shard_map/all_to_all | solution.py:52
  63.6 1.4 copy.27
  65.1 0.1 fusion.42
  65.2 0.1 bitcast_convert_fusion.1
  65.3 0.3 copy.28
  65.7 0.1 bitcast_convert_fusion
  65.8 1.3 copy.29
  67.1 18.1 %all-gather.3.cloned.1.call-done = bf16[1,704,2560]{2,1,0:T(8,128)(2,1)} async-done(((bf16[1,88,2560]{2,1,0:T(8,128)(2,1)}), bf16[1,704,2560]{2,1,0:T(8,128)(2,1)}) %all-gather.3.cloned.1.call-update) | async-done | bytes 3604496 | tf_op jit(solution)/shard_map/all_gather | solution.py:58
  85.3 9.0 %fusion.7 = f32[2560,320]{0,1:T(8,128)} fusion(bf16[1,704,2560]{2,1,0:T(8,128)(2,1)} %all-gather.3.cloned.1.call-done, f32[704,320]{0,1:T(8,128)S(1)} %copy.28, bf16[1,2560,320]{1,2,0:T(8,128)(2,1)} %param.12, f32[]{:T(128)} %bitcast.44), kind=kOutput, calls=%fused_computation.10 | convolution fusion | flops 2311577600 | bytes 9420804 | tf_op jit(solution)/shard_map/mrd,mrh->dh/dot_general | solution.py:32
  94.3 47.1 %all-gather.5.cloned.1.call-done = bf16[1,704,2560]{2,1,0:T(8,128)(2,1)} async-done(((bf16[1,88,2560]{2,1,0:T(8,128)(2,1)}), bf16[1,704,2560]{2,1,0:T(8,128)(2,1)}) %all-gather.5.cloned.1.call-update) | async-done | bytes 3604496 | tf_op jit(solution)/shard_map/all_gather | solution.py:58
  141.4 9.0 %convert_subtract_fusion = f32[1,2560,320]{1,2,0:T(8,128)S(1)} fusion(bf16[1,2560,320]{1,2,0:T(8,128)(2,1)} %param.12, f32[2560,320]{0,1:T(8,128)} %fusion.7, bf16[1,704,2560]{2,1,0:T(8,128)(2,1)} %all-gather.5.cloned.1.call-done, f32[704,320]{0,1:T(8,128)} %copy.29, f32[]{:T(128)} %bitcast.45), kind=kOutput, calls=%fused_computation.2 | convolution fusion | flops 2316492800 | bytes 12697604 | tf_op jit(solution)/shard_map/mrd,mrh->dh/dot_general | solution.py:32
  150.4 78.8 %conditional.1 = (f32[1,2560,320]{1,2,0:T(8,128)}, f32[1]{0:T(128)}) conditional(s32[]{:T(128)} %clamp.3, (f32[1,2560,320]{1,2,0:T(8,128)S(1)}, f32[1]{0:T(128)}) %tuple.32, (f32[1,2560,320]{1,2,0:T(8,128)S(1)}, f32[1]{0:T(128)}) %tuple.32, (f32[1,2560,320]{1,2,0:T(8,128)S(1)}, f32[1]{0:T(128)}) %tuple.32, ...), branch_computations={%region_1.2_spmd, %region_2.3_spmd, %region_3.4_spmd, %region_4.5_... | conditional | bytes 13107312 | solution.py:44
  150.4 4.7 %collective-permute-start.2 = (f32[1,2560,320]{1,2,0:T(8,128)S(1)}, f32[1,2560,320]{1,2,0:T(8,128)}, u32[]{:S(2)}, u32[]{:S(2)}) collective-permute-start(f32[1,2560,320]{1,2,0:T(8,128)S(1)} %get-tuple-element.26), channel_id=1, source_target_pairs={{496,0},{504,8},{0,16},{8,24},{16,32},{24,40},{32,48},{40,56},{48,... | collective-permute-start | bytes 9830408 | tf_op jit(solution)/shard_map/cond/branch_1_fun/ppermute | solution.py:18
  155.0 3.1 %collective-permute-start.3 = (f32[1]{0:T(128)}, f32[1]{0:T(128)}, u32[]{:S(2)}, u32[]{:S(2)}) collective-permute-start(f32[1]{0:T(128)} %get-tuple-element.27), channel_id=1, source_target_pairs={{496,0},{504,8},{0,16},{8,24},{16,32},{24,40},{32,48},{40,56},{48,... | collective-permute-start | bytes 20 | tf_op jit(solution)/shard_map/cond/branch_1_fun/ppermute | solution.py:18
  158.1 71.0 %collective-permute-done.3 = f32[1]{0:T(128)} collective-permute-done((f32[1]{0:T(128)}, f32[1]{0:T(128)}, u32[]{:S(2)}, u32[]{:S(2)}) %collective-permute-start.3) | collective-permute-done | bytes 36 | tf_op jit(solution)/shard_map/cond/branch_1_fun/ppermute | solution.py:18
  229.1 3.8 %multiply_convert_fusion = bf16[1,2560,320]{1,2,0:T(8,128)(2,1)} fusion(f32[1,2560,320]{1,2,0:T(8,128)S(1)} %convert_subtract_fusion, f32[1,2560,320]{1,2,0:T(8,128)} %get-tuple-element.40), kind=kLoop, calls=%fused_computation.15 | loop fusion | flops 2457600 | bytes 8192000 | tf_op jit(solution)/shard_map/convert_element_type | solution.py:64
  (5 shorter events, 0.0 us)
Async XLA Ops:
  7.2 4.8 %copy-start = (bf16[2,88,2560]{2,1,0:T(8,128)(2,1)S(1)}, bf16[2,88,2560]{2,1,0:T(8,128)(2,1)}, u32[]{:S(2)}) copy-start(bf16[2,88,2560]{2,1,0:T(8,128)(2,1)} %param.16) | copy-start | bytes 2703364
  7.2 78.1 %all-gather.3.cloned.1.call-start = ((), (), s32[]{:S(2)}) async-start(), calls=%async_computation.1 | async-start | bytes 4055040 | tf_op jit(solution)/shard_map/all_gather | solution.py:58
  11.2 130.2 %all-gather.5.cloned.1.call-start = ((), (), s32[]{:S(2)}) async-start(), calls=%async_computation.2 | async-start | bytes 4055040 | tf_op jit(solution)/shard_map/all_gather | solution.py:58
  14.2 49.5 %all-to-all-start = ((bf16[2,88,2560]{1,0,2:T(2,128)(2,1)}), bf16[2,88,2560]{1,0,2:T(2,128)(2,1)S(1)}, u32[]{:S(2)}, u32[]{:S(2)}) async-start(bf16[2,88,2560]{1,0,2:T(2,128)(2,1)} %copy.26), calls=%async_computation | async-start | bytes 2621440 | tf_op jit(solution)/shard_map/all_to_all | solution.py:52
  150.4 78.8 %collective-permute-start.2 = (f32[1,2560,320]{1,2,0:T(8,128)S(1)}, f32[1,2560,320]{1,2,0:T(8,128)}, u32[]{:S(2)}, u32[]{:S(2)}) collective-permute-start(f32[1,2560,320]{1,2,0:T(8,128)S(1)} %get-tuple-element.26), channel_id=1, source_target_pairs={{496,0},{504,8},{0,16},{8,24},{16,32},{24,40},{32,48},{40,56},{48,... | collective-permute-start | bytes 9830408 | tf_op jit(solution)/shard_map/cond/branch_1_fun/ppermute | solution.py:18
  155.0 74.1 %collective-permute-start.3 = (f32[1]{0:T(128)}, f32[1]{0:T(128)}, u32[]{:S(2)}, u32[]{:S(2)}) collective-permute-start(f32[1]{0:T(128)} %get-tuple-element.27), channel_id=1, source_target_pairs={{496,0},{504,8},{0,16},{8,24},{16,32},{24,40},{32,48},{40,56},{48,... | collective-permute-start | bytes 20 | tf_op jit(solution)/shard_map/cond/branch_1_fun/ppermute | solution.py:18
Sparse Core Ops, SparseCore 0:
  11.3 73.8 all-gather.2
  87.4 53.9 all-gather.4
where the time goes:
time: 241 us; the launch traced here: 242 us
  waiting for transfers between devices  173 us (72%)
  starting transfers between devices  19.6 us (8%)
  matrix products  18 us (7%)
  between operations  17.2 us (7%)
  other arithmetic  6.98 us (3%)
  local copies, waits for them, and re-layouts  6.37 us (3%)
    ppermute x2, waiting for transfers between devices, shifted(): return lax.ppermute(block, axis, route)  71 us
    all_gather x2, waiting for transfers between devices, on_device(): lax.all_gather(normed[micro:micro + 1], 'fsdp', axis=1, tiled=True)  65.2 us
    all_to_all x1, waiting for transfers between devices, on_device(): lax.all_to_all(cotangent, 'fsdp', split_axis=2, concat_axis=1, tiled=True)  36.4 us
    dot_general x2, matrix products, add_piece(): jnp.einsum('mrd,mrh->dh', piece, grad_out, preferred_element_type=jnp.flo...  18 us
    all_to_all x1, starting transfers between devices, on_device(): lax.all_to_all(cotangent, 'fsdp', split_axis=2, concat_axis=1, tiled=True)  11.8 us
    ppermute x2, starting transfers between devices, shifted(): return lax.ppermute(block, axis, route)  7.76 us
  transfers between devices with their start and end apart: 5, of which 4 were waited for; matrix products, arithmetic and copies ran while one was open for 6% of the time, Pallas kernels for 0%

commit v1 on v0

v1 whole, which is shorter than its diff:
```python
from functools import partial

import jax
import jax.numpy as jnp
from jax import lax
from jax.experimental import pallas as pl
from jax.experimental.pallas import tpu as pltpu
from jax.sharding import PartitionSpec as P

DW = 2560
LEARN_RATE = 1.5
EPSILON = 1e-05
SCALE = DW ** (-0.5)
LANES = 128
CHUNKS = (512, 768, 768, 512)
VMEM = 48 * 2**20


def pack_cotangent(cot_t, parts):
    cols, tokens = cot_t.shape
    cot_t = cot_t.reshape(parts, cols // parts, tokens)
    half = cols // parts // 2
    rest = cot_t[:, :, LANES:]
    gap = jnp.zeros((parts, half, LANES - 2 * (tokens - LANES)), cot_t.dtype)
    folded = jnp.concatenate([rest[:, :half], rest[:, half:], gap], axis=2)
    return jnp.concatenate([cot_t[:, :, :LANES], folded], axis=1)


def grad_out_kernel(weight_ref, tokens_ref, cot_ref, out_ref):
    cols, count = out_ref.shape[1:]
    half, rest = cols // 2, count - LANES
    pre_act = SCALE * lax.dot_general(
        weight_ref[...], tokens_ref[...], (((1,), (1,)), ((), ())), preferred_element_type=jnp.float32
    )
    sig = jax.nn.sigmoid(pre_act)
    slope = sig * (1.0 + pre_act * (1.0 - sig))
    cot = cot_ref[0]
    head = cot[:cols].astype(jnp.float32)
    tail = cot[cols:].astype(jnp.float32)
    out_ref[0, :, :LANES] = (head * slope[:, :LANES]).astype(jnp.bfloat16)
    out_ref[0, :half, LANES:] = (tail[:, :rest] * slope[:half, LANES:]).astype(jnp.bfloat16)
    out_ref[0, half:, LANES:] = (tail[:, rest : 2 * rest] * slope[half:, LANES:]).astype(jnp.bfloat16)


def grad_out(weight_t, tokens, packed):
    parts, rows = packed.shape[:2]
    cols = weight_t.shape[0]
    count = tokens.shape[0] // parts
    return pl.pallas_call(
        grad_out_kernel,
        grid=(parts,),
        in_specs=[
            pl.BlockSpec((cols, DW), lambda i: (0, 0)),
            pl.BlockSpec((count, DW), lambda i: (i, 0)),
            pl.BlockSpec((1, rows, LANES), lambda i: (i, 0, 0)),
        ],
        out_specs=pl.BlockSpec((1, cols, count), lambda i: (i, 0, 0)),
        out_shape=jax.ShapeDtypeStruct((parts, cols, count), jnp.bfloat16),
        compiler_params=pltpu.CompilerParams(vmem_limit_bytes=VMEM),
        cost_estimate=pl.CostEstimate(
            flops=2 * cols * DW * count * parts, bytes_accessed=2 * DW * count * parts, transcendentals=0
        ),
    )(weight_t, tokens, packed)


def local_kernel(grad_out_ref, tokens_ref, numer_ref, out_ref):
    parts, _, count = grad_out_ref.shape
    total = jnp.zeros(out_ref.shape, jnp.float32)
    for part in range(parts):
        total += jnp.dot(
            grad_out_ref[part], tokens_ref[part * count : (part + 1) * count], preferred_element_type=jnp.float32
        )
    update = (LEARN_RATE * (SCALE * total)).astype(jnp.bfloat16)
    out_ref[...] = (numer_ref[...].astype(jnp.float32) - update.astype(jnp.float32)).astype(jnp.bfloat16)


def local_chunk(grad_out_t, tokens, numer_t, first, width, tile=256):
    parts, cols, count = grad_out_t.shape
    rows = tokens.shape[0]
    offset = first // tile
    return pl.pallas_call(
        local_kernel,
        grid=(width // tile,),
        in_specs=[
            pl.BlockSpec((parts, cols, count), lambda i: (0, 0, 0)),
            pl.BlockSpec((rows, tile), lambda i: (0, i + offset)),
            pl.BlockSpec((cols, tile), lambda i: (0, i + offset)),
        ],
        out_specs=pl.BlockSpec((cols, tile), lambda i: (0, i)),
        out_shape=jax.ShapeDtypeStruct((cols, width), jnp.bfloat16),
        compiler_params=pltpu.CompilerParams(vmem_limit_bytes=VMEM),
        cost_estimate=pl.CostEstimate(
            flops=2 * cols * rows * width, bytes_accessed=2 * rows * width, transcendentals=0
        ),
    )(grad_out_t, tokens, numer_t)


def route(distance):
    devices = range(lax.axis_size("rep"))
    return [((i - distance) % len(devices), i) for i in devices]


def mix_with(hop_size, grad_out_t, tokens, numer_t, weight):
    pieces, first = [], 0
    for width in CHUNKS:
        local = local_chunk(grad_out_t, tokens, numer_t, first, width)
        partner = lax.ppermute(local, "rep", route(hop_size))
        pieces.append((0.5 * local.astype(jnp.float32) + 0.5 * partner.astype(jnp.float32)).astype(jnp.bfloat16))
        first += width
    new_weight = 0.5 * (weight + lax.ppermute(weight, "rep", route(hop_size)))
    return jnp.concatenate(pieces, axis=1), new_weight


def on_device(numerator, push_weight, norm_gain, activations, cotangent, step_index):
    parts = lax.axis_size("fsdp")
    wide = activations.astype(jnp.float32)
    mean_square = jnp.mean(wide * wide, axis=-1, keepdims=True)
    normed = (wide * lax.rsqrt(mean_square + EPSILON) * norm_gain).astype(jnp.bfloat16)
    tokens = lax.all_gather(normed.reshape(-1, DW), "fsdp", axis=0, tiled=True)
    packed = pack_cotangent(cotangent.reshape(-1, cotangent.shape[2]).T, parts)
    packed = lax.all_to_all(packed, "fsdp", split_axis=0, concat_axis=0, tiled=True)
    numer_t = numerator[0].T
    weight_t = (numer_t.astype(jnp.float32) / push_weight[0]).astype(jnp.bfloat16)
    grad_out_t = grad_out(weight_t, tokens, packed)
    bit_count = lax.axis_size("rep").bit_length() - 1
    branches = [partial(mix_with, 2**bit) for bit in range(bit_count)]
    mixed_t, new_weight = lax.switch(
        step_index % bit_count, branches, grad_out_t, tokens, numer_t, push_weight
    )
    return mixed_t.T[None], new_weight


def solution(mesh):
    placed = (
        P("rep", None, "fsdp"),
        P("rep"),
        P(),
        P(None, ("rep", "fsdp"), None),
        P(None, ("rep", "fsdp"), None),
        P(),
    )
    return jax.shard_map(
        on_device,
        mesh=mesh,
        in_specs=placed,
        out_specs=(P("rep", None, "fsdp"), P("rep")),
        check_vma=False,
    )
```

time: 241 us -> 175 us (0.73)
  waiting for transfers between devices: 173 us -> 104 us
  matrix products: 18 us -> 0 us
  Pallas kernels: 0 us -> 15.7 us
  starting transfers between devices: 19.6 us -> 27.7 us
  local copies, waits for them, and re-layouts: 6.37 us -> 1.46 us
    ppermute x2 -> x5, waiting for transfers between devices: 71 us -> 20.9 us  [the longest x4 20.9 us: mix_with(): partner = lax.ppermute(local, 'rep', route(hop_size))]
    dot_general x2 -> x0, matrix products: 18 us -> none  [add_piece(): jnp.einsum('mrd,mrh->dh', piece, grad_out, preferred_element_type=jnp.flo...]
    pallas_call x0 -> x5, Pallas kernels: none -> 15.7 us  [the longest x1 9.79 us: grad_out(): pl.pallas_call(grad_out_kernel, grid=(parts,), in_specs=[pl.BlockSpec((co...]
    all_to_all x1, waiting for transfers between devices: 36.4 us -> 23.2 us  [on_device(): lax.all_to_all(packed, 'fsdp', split_axis=0, concat_axis=0, tiled=True)]
    ppermute x2 -> x5, starting transfers between devices: 7.76 us -> 15.8 us  [the longest x4 13.9 us: mix_with(): partner = lax.ppermute(local, 'rep', route(hop_size))]
    all_gather x2 -> x1, waiting for transfers between devices: 65.2 us -> 59.9 us  [on_device(): tokens = lax.all_gather(normed.reshape(-1, DW), 'fsdp', axis=0, tiled=True)]
  transfers between devices with their start and end apart: 5 -> 7, of which waited for: 4 -> 5; matrix products, arithmetic and copies ran while one was open for 6% -> 3% of each run, Pallas kernels for 0% -> 3%
where the time goes in v1:
time: 175 us; the launch traced here: 174 us
  waiting for transfers between devices  104 us (59%)
  starting transfers between devices  27.7 us (16%)
  between operations  17.2 us (10%)
  Pallas kernels  15.7 us (9%)
  other arithmetic  7.6 us (4%)
    all_gather x1, waiting for transfers between devices, on_device(): tokens = lax.all_gather(normed.reshape(-1, DW), 'fsdp', axis=0, tiled=True)  59.9 us
    all_to_all x1, waiting for transfers between devices, on_device(): lax.all_to_all(packed, 'fsdp', split_axis=0, concat_axis=0, tiled=True)  23.2 us
    ppermute x4, waiting for transfers between devices, mix_with(): partner = lax.ppermute(local, 'rep', route(hop_size))  20.9 us
    ppermute x4, starting transfers between devices, mix_with(): partner = lax.ppermute(local, 'rep', route(hop_size))  13.9 us
    all_to_all x1, starting transfers between devices, on_device(): lax.all_to_all(packed, 'fsdp', split_axis=0, concat_axis=0, tiled=True)  11.8 us
    pallas_call x1, Pallas kernels, grad_out(): pl.pallas_call(grad_out_kernel, grid=(parts,), in_specs=[pl.BlockSpec((co...  9.79 us
    pallas_call x4, Pallas kernels, local_chunk(): pl.pallas_call(local_kernel, grid=(width // tile,), in_specs=[pl.BlockSpe...  5.9 us
  transfers between devices with their start and end apart: 7, of which 5 were waited for; matrix products, arithmetic and copies ran while one was open for 3% of the time, Pallas kernels for 3%

profile of v1, /device:TPU:1, one launch (start us, length us, event | category | flops | bytes accessed | tf_op | source)
XLA Modules:
  0.0 174.0 jit_solution(3074050848772444858)
XLA Ops:
  7.2 1.5 fusion
  8.7 2.5 %fusion.2 = bf16[2,88,2560]{2,1,0:T(8,128)(2,1)} fusion(bf16[2,88,2560]{2,1,0:T(8,128)(2,1)} %param.15, f32[2560]{0:T(1024)} %param.14, f32[2,88]{1,0:T(2,128)S(1)} %add_rsqrt_fusion), kind=kLoop, calls=%fused_computation.35 | loop fusion | flops 1802240 | bytes 1813184 | tf_op jit(solution)/shard_map/convert_element_type | solution.py:118
  11.3 0.6 copy.8
  12.2 1.3 maximum_maximum_fusion
  13.5 11.8 %all-to-all-start = ((bf16[8,480,128]{2,1,0:T(8,128)(2,1)}), bf16[8,480,128]{2,1,0:T(8,128)(2,1)S(1)}, u32[]{:S(2)}, u32[]{:S(2)}) async-start(bf16[8,480,128]{2,1,0:T(8,128)(2,1)} %maximum_maximum_fusion), calls=%async_computation | async-start | bytes 1966080 | tf_op jit(solution)/shard_map/all_to_all | solution.py:121
  26.6 1.7 divide_convert_fusion.weight_ref
  28.3 23.2 %all-to-all-done.cot_ref = bf16[8,480,128]{2,1,0:T(8,128)(2,1)S(1)} async-done(((bf16[8,480,128]{2,1,0:T(8,128)(2,1)}), bf16[8,480,128]{2,1,0:T(8,128)(2,1)S(1)}, u32[]{:S(2)}, u32[]{:S(2)}) %all-to-all-start) | async-done | bytes 983072 | tf_op jit(solution)/shard_map/all_to_all | solution.py:121
  51.5 59.9 %all-gather.2.cloned.1.call-done.tokens_ref = bf16[1408,2560]{1,0:T(8,128)(2,1)} async-done(((bf16[176,2560]{1,0:T(8,128)(2,1)}), bf16[1408,2560]{1,0:T(8,128)(2,1)}) %all-gather.2.cloned.1.call-update) | async-done | bytes 7208976 | tf_op jit(solution)/shard_map/all_gather | solution.py:119
  111.4 9.8 %shard_map.77 = bf16[8,320,176]{2,1,0:T(8,128)(2,1)S(1)} custom-call(bf16[320,2560]{1,0:T(8,128)(2,1)S(1)} %divide_convert_fusion.weight_ref, bf16[1408,2560]{1,0:T(8,128)(2,1)} %all-gather.2.cloned.1.call-done.tokens_ref, bf16[8,480,128]{2,1,0:T(8,128)(2,1)S(1)} %all-to-all-done.cot_ref), custom_call_target="tpu_custom_call" | custom-call | flops 2306867200 | bytes 7208960 | tf_op jit(solution)/shard_map/pallas_call | solution.py:49
  121.3 43.6 %conditional.1 = (bf16[320,2560]{1,0:T(8,128)(2,1)S(1)}, f32[1]{0:T(128)}, f32[1]{0:T(128)}, f32[1]{0:T(128)}) conditional(s32[]{:T(128)} %clamp.3, (bf16[8,320,176]{2,1,0:T(8,128)(2,1)S(1)}, bf16[1408,2560]{1,0:T(8,128)(2,1)S(1)}, bf16[320,2560]{1,0:T(8,128)(2,1)S(1)}, f32[1]{0:T(128)}) %tuple.56, ...), branch_computations={%region_1.2_spmd, %region_2.3_spmd, %region_3.4_spmd, %region_4.5_... | conditional | flops 2317516800 | bytes 21954808 | solution.py:127
  121.3 1.2 branch_2_fun.4
  122.5 1.9 %collective-permute-start.10 = (bf16[320,512]{1,0:T(8,128)(2,1)S(1)}, bf16[320,512]{1,0:T(8,128)(2,1)S(1)}, u32[]{:S(2)}, u32[]{:S(2)}) collective-permute-start(bf16[320,512]{1,0:T(8,128)(2,1)S(1)} %branch_2_fun.4), channel_id=1, source_target_pairs={{480,0},{488,8},{496,16},{504,24},{0,32},{8,40},{16,48},{24,56},{3... | collective-permute-start | bytes 983048 | tf_op jit(solution)/shard_map/cond/branch_2_fun/ppermute | solution.py:107
  124.4 1.9 %collective-permute-start.14 = (f32[1]{0:T(128)}, f32[1]{0:T(128)}, u32[]{:S(2)}, u32[]{:S(2)}) collective-permute-start(f32[1]{0:T(128)} %get-tuple-element.96), channel_id=1, source_target_pairs={{480,0},{488,8},{496,16},{504,24},{0,32},{8,40},{16,48},{24,56},{3... | collective-permute-start | bytes 20 | tf_op jit(solution)/shard_map/cond/branch_2_fun/ppermute | solution.py:110
  126.3 1.2 branch_2_fun.7
  127.5 5.4 %collective-permute-start.13 = (bf16[320,512]{1,0:T(8,128)(2,1)S(1)}, bf16[320,512]{1,0:T(8,128)(2,1)S(1)}, u32[]{:S(2)}, u32[]{:S(2)}) collective-permute-start(bf16[320,512]{1,0:T(8,128)(2,1)S(1)} %branch_2_fun.7), channel_id=1, source_target_pairs={{480,0},{488,8},{496,16},{504,24},{0,32},{8,40},{16,48},{24,56},{3... | collective-permute-start | bytes 983048 | tf_op jit(solution)/shard_map/cond/branch_2_fun/ppermute | solution.py:107
  133.0 1.8 %branch_2_fun.5 = bf16[320,768]{1,0:T(8,128)(2,1)S(1)} custom-call(bf16[8,320,176]{2,1,0:T(8,128)(2,1)S(1)} %get-tuple-element.60.grad_out_ref, bf16[1408,2560]{1,0:T(8,128)(2,1)S(1)} %get-tuple-element.61.tokens_ref, bf16[320,2560]{1,0:T(8,128)(2,1)S(1)} %get-tuple-element.62.numer_ref), custom_call_target="tpu_custom_call" | custom-call | flops 692060160 | bytes 2162688 | tf_op jit(solution)/shard_map/cond/branch_2_fun/pallas_call | solution.py:81
  134.7 4.3 %collective-permute-start.11 = (bf16[320,768]{1,0:T(8,128)(2,1)S(1)}, bf16[320,768]{1,0:T(8,128)(2,1)S(1)}, u32[]{:S(2)}, u32[]{:S(2)}) collective-permute-start(bf16[320,768]{1,0:T(8,128)(2,1)S(1)} %branch_2_fun.5), channel_id=1, source_target_pairs={{480,0},{488,8},{496,16},{504,24},{0,32},{8,40},{16,48},{24,56},{3... | collective-permute-start | bytes 1474568 | tf_op jit(solution)/shard_map/cond/branch_2_fun/ppermute | solution.py:107
  139.0 1.8 %branch_2_fun.6 = bf16[320,768]{1,0:T(8,128)(2,1)S(1)} custom-call(bf16[8,320,176]{2,1,0:T(8,128)(2,1)S(1)} %get-tuple-element.60.grad_out_ref, bf16[1408,2560]{1,0:T(8,128)(2,1)S(1)} %get-tuple-element.61.tokens_ref, bf16[320,2560]{1,0:T(8,128)(2,1)S(1)} %get-tuple-element.62.numer_ref), custom_call_target="tpu_custom_call" | custom-call | flops 692060160 | bytes 2162688 | tf_op jit(solution)/shard_map/cond/branch_2_fun/pallas_call | solution.py:81
  140.8 2.3 %collective-permute-start.12 = (bf16[320,768]{1,0:T(8,128)(2,1)S(1)}, bf16[320,768]{1,0:T(8,128)(2,1)S(1)}, u32[]{:S(2)}, u32[]{:S(2)}) collective-permute-start(bf16[320,768]{1,0:T(8,128)(2,1)S(1)} %branch_2_fun.6), channel_id=1, source_target_pairs={{480,0},{488,8},{496,16},{504,24},{0,32},{8,40},{16,48},{24,56},{3... | collective-permute-start | bytes 1474568 | tf_op jit(solution)/shard_map/cond/branch_2_fun/ppermute | solution.py:107
  143.4 10.4 %collective-permute-done.11 = bf16[320,768]{1,0:T(8,128)(2,1)S(1)} collective-permute-done((bf16[320,768]{1,0:T(8,128)(2,1)S(1)}, bf16[320,768]{1,0:T(8,128)(2,1)S(1)}, u32[]{:S(2)}, u32[]{:S(2)}) %collective-permute-start.11) | collective-permute-done | bytes 491552 | tf_op jit(solution)/shard_map/cond/branch_2_fun/ppermute | solution.py:107
  153.8 0.1 multiply_convert_fusion.9
  154.0 10.4 %collective-permute-done.12 = bf16[320,768]{1,0:T(8,128)(2,1)S(1)} collective-permute-done((bf16[320,768]{1,0:T(8,128)(2,1)S(1)}, bf16[320,768]{1,0:T(8,128)(2,1)S(1)}, u32[]{:S(2)}, u32[]{:S(2)}) %collective-permute-start.12) | collective-permute-done | bytes 491552 | tf_op jit(solution)/shard_map/cond/branch_2_fun/ppermute | solution.py:107
  164.4 0.1 multiply_convert_fusion.8
  165.5 0.5 copy-done.2
  (20 shorter events, 0.8 us)
Async XLA Ops:
  7.2 4.1 %copy-start.3 = (bf16[2,88,2560]{2,1,0:T(8,128)(2,1)S(1)}, bf16[2,88,2560]{2,1,0:T(8,128)(2,1)}, u32[]{:S(2)}) copy-start(bf16[2,88,2560]{2,1,0:T(8,128)(2,1)} %param.16) | copy-start | bytes 2703364
  7.2 104.3 %all-gather.2.cloned.1.call-start = ((), (), s32[]{:S(2)}) async-start(), calls=%async_computation.1 | async-start | bytes 8110080 | tf_op jit(solution)/shard_map/all_gather | solution.py:119
  13.5 38.1 %all-to-all-start = ((bf16[8,480,128]{2,1,0:T(8,128)(2,1)}), bf16[8,480,128]{2,1,0:T(8,128)(2,1)S(1)}, u32[]{:S(2)}, u32[]{:S(2)}) async-start(bf16[8,480,128]{2,1,0:T(8,128)(2,1)} %maximum_maximum_fusion), calls=%async_computation | async-start | bytes 1966080 | tf_op jit(solution)/shard_map/all_to_all | solution.py:121
  111.4 9.8 %copy-start = (bf16[1408,2560]{1,0:T(8,128)(2,1)S(1)}, bf16[1408,2560]{1,0:T(8,128)(2,1)}, u32[]{:S(2)}) copy-start(bf16[1408,2560]{1,0:T(8,128)(2,1)} %all-gather.2.cloned.1.call-done.tokens_ref) | copy-start | bytes 21626884
  111.4 9.8 %copy-start.1 = (bf16[1,2560,320]{1,2,0:T(8,128)(2,1)S(1)}, bf16[1,2560,320]{1,2,0:T(8,128)(2,1)}, u32[]{:S(2)}) copy-start(bf16[1,2560,320]{1,2,0:T(8,128)(2,1)} %param.12) | copy-start | bytes 4915204
  122.5 20.6 %collective-permute-start.10 = (bf16[320,512]{1,0:T(8,128)(2,1)S(1)}, bf16[320,512]{1,0:T(8,128)(2,1)S(1)}, u32[]{:S(2)}, u32[]{:S(2)}) collective-permute-start(bf16[320,512]{1,0:T(8,128)(2,1)S(1)} %branch_2_fun.4), channel_id=1, source_target_pairs={{480,0},{488,8},{496,16},{504,24},{0,32},{8,40},{16,48},{24,56},{3... | collective-permute-start | bytes 983048 | tf_op jit(solution)/shard_map/cond/branch_2_fun/ppermute | solution.py:107
  124.4 40.2 %collective-permute-start.14 = (f32[1]{0:T(128)}, f32[1]{0:T(128)}, u32[]{:S(2)}, u32[]{:S(2)}) collective-permute-start(f32[1]{0:T(128)} %get-tuple-element.96), channel_id=1, source_target_pairs={{480,0},{488,8},{496,16},{504,24},{0,32},{8,40},{16,48},{24,56},{3... | collective-permute-start | bytes 20 | tf_op jit(solution)/shard_map/cond/branch_2_fun/ppermute | solution.py:110
  127.5 15.8 %collective-permute-start.13 = (bf16[320,512]{1,0:T(8,128)(2,1)S(1)}, bf16[320,512]{1,0:T(8,128)(2,1)S(1)}, u32[]{:S(2)}, u32[]{:S(2)}) collective-permute-start(bf16[320,512]{1,0:T(8,128)(2,1)S(1)} %branch_2_fun.7), channel_id=1, source_target_pairs={{480,0},{488,8},{496,16},{504,24},{0,32},{8,40},{16,48},{24,56},{3... | collective-permute-start | bytes 983048 | tf_op jit(solution)/shard_map/cond/branch_2_fun/ppermute | solution.py:107
  134.7 19.1 %collective-permute-start.11 = (bf16[320,768]{1,0:T(8,128)(2,1)S(1)}, bf16[320,768]{1,0:T(8,128)(2,1)S(1)}, u32[]{:S(2)}, u32[]{:S(2)}) collective-permute-start(bf16[320,768]{1,0:T(8,128)(2,1)S(1)} %branch_2_fun.5), channel_id=1, source_target_pairs={{480,0},{488,8},{496,16},{504,24},{0,32},{8,40},{16,48},{24,56},{3... | collective-permute-start | bytes 1474568 | tf_op jit(solution)/shard_map/cond/branch_2_fun/ppermute | solution.py:107
  140.8 23.6 %collective-permute-start.12 = (bf16[320,768]{1,0:T(8,128)(2,1)S(1)}, bf16[320,768]{1,0:T(8,128)(2,1)S(1)}, u32[]{:S(2)}, u32[]{:S(2)}) collective-permute-start(bf16[320,768]{1,0:T(8,128)(2,1)S(1)} %branch_2_fun.6), channel_id=1, source_target_pairs={{480,0},{488,8},{496,16},{504,24},{0,32},{8,40},{16,48},{24,56},{3... | collective-permute-start | bytes 1474568 | tf_op jit(solution)/shard_map/cond/branch_2_fun/ppermute | solution.py:107
  164.9 1.2 copy-start.2
Sparse Core Ops, SparseCore 0:
  11.4 100.0 all-gather.1

commit v2 on v1

v2 whole, which is shorter than its diff:
```python
from functools import partial

import jax
import jax.numpy as jnp
from jax import lax
from jax.experimental import pallas as pl
from jax.experimental.pallas import tpu as pltpu
from jax.sharding import PartitionSpec as P

DW = 2560
LEARN_RATE = 1.5
EPSILON = 1e-05
SCALE = DW ** (-0.5)
LANES = 128
CHUNKS = (512, 768, 768, 512)
VMEM = 48 * 2**20


def pack_cotangent(cot_t, parts):
    cols, tokens = cot_t.shape
    cot_t = cot_t.reshape(parts, cols // parts, tokens)
    half = cols // parts // 2
    rest = cot_t[:, :, LANES:]
    gap = jnp.zeros((parts, half, LANES - 2 * (tokens - LANES)), cot_t.dtype)
    folded = jnp.concatenate([rest[:, :half], rest[:, half:], gap], axis=2)
    return jnp.concatenate([cot_t[:, :, :LANES], folded], axis=1)


def norm_kernel(tokens_ref, gain_ref, out_ref):
    wide = tokens_ref[...].astype(jnp.float32)
    mean_square = jnp.mean(wide * wide, axis=-1, keepdims=True)
    out_ref[...] = (wide * lax.rsqrt(mean_square + EPSILON) * gain_ref[...]).astype(jnp.bfloat16)


def norm(tokens, gain):
    return pl.pallas_call(
        norm_kernel,
        out_shape=jax.ShapeDtypeStruct(tokens.shape, jnp.bfloat16),
        compiler_params=pltpu.CompilerParams(vmem_limit_bytes=VMEM),
        cost_estimate=pl.CostEstimate(flops=8 * tokens.size, bytes_accessed=4 * tokens.size, transcendentals=0),
    )(tokens, gain[None])


def once_there(array, *others):
    whole = pl.BlockSpec(memory_space=pl.ANY)
    return pl.pallas_call(
        lambda *refs: None,
        grid=(1,),
        in_specs=[whole] + [pl.BlockSpec((1, 16, LANES), lambda i: (0, 0, 0))] * len(others),
        out_specs=whole,
        out_shape=jax.ShapeDtypeStruct(array.shape, array.dtype),
        input_output_aliases={0: 0},
    )(array, *others)


def to_chip(values, step):
    count = lax.axis_size("fsdp")
    route = [(i, (i // 2 + (-step if i % 2 else step)) % (count // 2) * 2 + i % 2) for i in range(count)]
    return lax.ppermute(values, "fsdp", route)


def to_core(values):
    return lax.ppermute(values, "fsdp", [(i, i ^ 1) for i in range(lax.axis_size("fsdp"))])


def grad_out_kernel(ids_ref, weight_ref, cot_ref, *refs):
    out_ref = refs[-1]
    _, cols, count = out_ref.shape
    half, rest = cols // 2, count - LANES
    for i in range(out_ref.shape[0]):
        pre_act = SCALE * lax.dot_general(
            weight_ref[...], refs[i][...], (((1,), (1,)), ((), ())), preferred_element_type=jnp.float32
        )
        sig = jax.nn.sigmoid(pre_act)
        slope = sig * (1.0 + pre_act * (1.0 - sig))
        cot = cot_ref[ids_ref[i]]
        head = cot[:cols].astype(jnp.float32)
        tail = cot[cols:].astype(jnp.float32)
        out_ref[i, :, :LANES] = (head * slope[:, :LANES]).astype(jnp.bfloat16)
        out_ref[i, :half, LANES:] = (tail[:, :rest] * slope[:half, LANES:]).astype(jnp.bfloat16)
        out_ref[i, half:, LANES:] = (tail[:, rest : 2 * rest] * slope[half:, LANES:]).astype(jnp.bfloat16)


def grad_out(weight_t, packed, sources, blocks):
    cols, tokens = weight_t.shape[0], blocks[0].shape[0]
    vmem = pl.BlockSpec(memory_space=pltpu.VMEM)
    return pl.pallas_call(
        grad_out_kernel,
        in_specs=[pl.BlockSpec(memory_space=pltpu.SMEM)] + [vmem] * (2 + len(blocks)),
        out_specs=vmem,
        out_shape=jax.ShapeDtypeStruct((len(blocks), cols, tokens), jnp.bfloat16),
        compiler_params=pltpu.CompilerParams(vmem_limit_bytes=VMEM),
        cost_estimate=pl.CostEstimate(
            flops=2 * cols * DW * tokens * len(blocks), bytes_accessed=2 * DW * tokens * len(blocks), transcendentals=0
        ),
    )(jnp.stack(sources), weight_t, packed, *blocks)


def local_kernel(groups, *refs):
    numer_ref, out_ref = refs[-2:]
    tokens_refs = refs[groups:-2]
    total, block = jnp.zeros(out_ref.shape, jnp.float32), 0
    for grad_out_ref in refs[:groups]:
        for i in range(grad_out_ref.shape[0]):
            total += jnp.dot(grad_out_ref[i], tokens_refs[block][...], preferred_element_type=jnp.float32)
            block += 1
    update = (LEARN_RATE * (SCALE * total)).astype(jnp.bfloat16)
    out_ref[...] = (numer_ref[...].astype(jnp.float32) - update.astype(jnp.float32)).astype(jnp.bfloat16)


def local_chunk(grads, blocks, numer_t, first, width, tile=256):
    cols = numer_t.shape[0]
    tokens = blocks[0].shape[0]
    offset = first // tile
    return pl.pallas_call(
        partial(local_kernel, len(grads)),
        grid=(width // tile,),
        in_specs=[pl.BlockSpec(g.shape, lambda i: (0, 0, 0)) for g in grads]
        + [pl.BlockSpec((tokens, tile), lambda i: (0, i + offset))] * len(blocks)
        + [pl.BlockSpec((cols, tile), lambda i: (0, i + offset))],
        out_specs=pl.BlockSpec((cols, tile), lambda i: (0, i)),
        out_shape=jax.ShapeDtypeStruct((cols, width), jnp.bfloat16),
        compiler_params=pltpu.CompilerParams(vmem_limit_bytes=VMEM),
        cost_estimate=pl.CostEstimate(
            flops=2 * cols * tokens * len(blocks) * width,
            bytes_accessed=2 * tokens * len(blocks) * width,
            transcendentals=0,
        ),
    )(*grads, *blocks, numer_t)


def route(distance):
    devices = range(lax.axis_size("rep"))
    return [((i - distance) % len(devices), i) for i in devices]


def mix_with(hop_size, grads, blocks, numer_t, weight):
    pieces, first = [], 0
    for width in CHUNKS:
        local = local_chunk(grads, blocks, numer_t, first, width)
        partner = lax.ppermute(local, "rep", route(hop_size))
        pieces.append((0.5 * local.astype(jnp.float32) + 0.5 * partner.astype(jnp.float32)).astype(jnp.bfloat16))
        first += width
    new_weight = 0.5 * (weight + lax.ppermute(weight, "rep", route(hop_size)))
    return jnp.concatenate(pieces, axis=1), new_weight


def on_device(numerator, push_weight, norm_gain, activations, cotangent, step_index):
    count = lax.axis_size("fsdp")
    me = lax.axis_index("fsdp")
    core = me % 2
    ahead, back, far = ((me + step * (1 - 2 * core) + count) % count for step in (2, -2, 4))
    packed = pack_cotangent(cotangent.reshape(-1, cotangent.shape[2]).T, count)
    packed = lax.all_to_all(packed, "fsdp", split_axis=0, concat_axis=0, tiled=True)
    own = norm(activations.reshape(-1, DW), norm_gain)
    first, second = to_chip(own, 1), to_chip(own, -1)
    first = once_there(first, packed)
    third = to_chip(first, 1)
    numer_t = numerator[0].T
    weight_t = (numer_t.astype(jnp.float32) / push_weight[0]).astype(jnp.bfloat16)
    held = [((me, me ^ 1), own), ((back, ahead ^ 1), first), ((ahead, back ^ 1), second)]
    blocks, grads = [], []
    for sources, block in held:
        pair = (block, to_core(block))
        blocks += pair
        grads.append(grad_out(weight_t, packed, sources, pair))
    third = once_there(third, *grads)
    for source, block in ((far, third), (far ^ 1, to_core(third))):
        blocks.append(block)
        grads.append(grad_out(weight_t, packed, (source,), (block,)))
    bit_count = lax.axis_size("rep").bit_length() - 1
    branches = [partial(mix_with, 2**bit) for bit in range(bit_count)]
    mixed_t, new_weight = lax.switch(
        step_index % bit_count, branches, grads, blocks, numer_t, push_weight
    )
    return mixed_t.T[None], new_weight


def solution(mesh):
    placed = (
        P("rep", None, "fsdp"),
        P("rep"),
        P(),
        P(None, ("rep", "fsdp"), None),
        P(None, ("rep", "fsdp"), None),
        P(),
    )
    return jax.shard_map(
        on_device,
        mesh=mesh,
        in_specs=placed,
        out_specs=(P("rep", None, "fsdp"), P("rep")),
        check_vma=False,
    )
```

time: 175 us -> 171 us (0.977)
  waiting for transfers between devices: 104 us -> 51 us
  starting transfers between devices: 27.7 us -> 80.2 us
  between operations: 17.2 us -> 3.97 us
  Pallas kernels: 15.7 us -> 27.2 us
  other arithmetic: 7.6 us -> 3.9 us
  local copies, waits for them, and re-layouts: 1.46 us -> 3.45 us
    all_gather x1 -> x0, waiting for transfers between devices: 59.9 us -> none  [on_device(): tokens = lax.all_gather(normed.reshape(-1, DW), 'fsdp', axis=0, tiled=True)]
    ppermute x0 -> x7, starting transfers between devices: none -> 53 us  [the longest x4 41.9 us: to_core(): lax.ppermute(values, 'fsdp', [(i, i ^ 1) for i in range(lax.axis_size('fs...]
    ppermute x0 -> x7, waiting for transfers between devices: none -> 31.1 us  [the longest x3 31 us: to_chip(): return lax.ppermute(values, 'fsdp', route)]
    all_to_all x1, waiting for transfers between devices: 23.2 us -> 0.01 us  [on_device(): lax.all_to_all(packed, 'fsdp', split_axis=0, concat_axis=0, tiled=True)]
    pallas_call x5 -> x12, Pallas kernels: 15.7 us -> 27.2 us  [the longest x5 14.3 us: grad_out(): pl.pallas_call(grad_out_kernel, in_specs=[pl.BlockSpec(memory_space=pltpu...]
    convert_element_type x1 -> x0, other arithmetic: 2.49 us -> none  [on_device(): (wide * lax.rsqrt(mean_square + EPSILON) * norm_gain).astype(jnp.bfloat16)]
  transfers between devices with their start and end apart: 7 -> 13, of which waited for: 5 -> 4; matrix products, arithmetic and copies ran while one was open for 3% -> 2% of each run, Pallas kernels for 3% -> 13%
where the time goes in v2:
time: 171 us; the launch traced here: 170 us
  starting transfers between devices  80.2 us (47%)
  waiting for transfers between devices  51 us (30%)
  Pallas kernels  27.2 us (16%)
  between operations  3.97 us (2%)
  other arithmetic  3.9 us (2%)
  local copies, waits for them, and re-layouts  3.45 us (2%)
    ppermute x4, starting transfers between devices, to_core(): lax.ppermute(values, 'fsdp', [(i, i ^ 1) for i in range(lax.axis_size('fs...  41.9 us
    ppermute x3, waiting for transfers between devices, to_chip(): return lax.ppermute(values, 'fsdp', route)  31 us
    ppermute x4, waiting for transfers between devices, mix_with(): partner = lax.ppermute(local, 'rep', route(hop_size))  20 us
    pallas_call x5, Pallas kernels, grad_out(): pl.pallas_call(grad_out_kernel, in_specs=[pl.BlockSpec(memory_space=pltpu...  14.3 us
    ppermute x4, starting transfers between devices, mix_with(): partner = lax.ppermute(local, 'rep', route(hop_size))  12.2 us
    all_to_all x1, starting transfers between devices, on_device(): lax.all_to_all(packed, 'fsdp', split_axis=0, concat_axis=0, tiled=True)  11.8 us
    ppermute x3, starting transfers between devices, to_chip(): return lax.ppermute(values, 'fsdp', route)  11.1 us
    pallas_call x4, Pallas kernels, local_chunk(): pl.pallas_call(partial(local_kernel, len(grads)), grid=(width // tile,),...  11.1 us
  transfers between devices with their start and end apart: 13, of which 4 were waited for; matrix products, arithmetic and copies ran while one was open for 2% of the time, Pallas kernels for 13%

profile of v2, /device:TPU:1, one launch (start us, length us, event | category | flops | bytes accessed | tf_op | source)
XLA Modules:
  0.0 170.1 jit_solution(10617701039974690197)
XLA Ops:
  3.8 11.8 %all-to-all-start = ((bf16[8,480,128]{2,1,0:T(8,128)(2,1)}), bf16[8,480,128]{2,1,0:T(8,128)(2,1)S(1)}, u32[]{:S(2)}, u32[]{:S(2)}) async-start(bf16[8,480,128]{2,1,0:T(8,128)(2,1)} %maximum_maximum_fusion), calls=%async_computation | async-start | bytes 1966080 | tf_op jit(solution)/shard_map/all_to_all | solution.py:154
  16.1 4.2 %collective-permute-start.33 = (bf16[176,2560]{1,0:T(8,128)(2,1)S(1)}, bf16[176,2560]{1,0:T(8,128)(2,1)}, u32[]{:S(2)}, u32[]{:S(2)}) collective-permute-start(bf16[176,2560]{1,0:T(8,128)(2,1)S(1)} %shard_map.77.refs_0_), channel_id=1, source_target_pairs={{0,6},{1,3},{2,0},{3,5},{4,2},{5,7},{6,4},{7,1},{8,14},{9,11},{10,... | collective-permute-start | bytes 2703368 | tf_op jit(solution)/shard_map/ppermute | solution.py:59
  20.3 3.2 %collective-permute-start.31 = (bf16[176,2560]{1,0:T(8,128)(2,1)S(1)}, bf16[176,2560]{1,0:T(8,128)(2,1)}, u32[]{:S(2)}, u32[]{:S(2)}) collective-permute-start(bf16[176,2560]{1,0:T(8,128)(2,1)S(1)} %shard_map.77.refs_0_), channel_id=1, source_target_pairs={{0,2},{1,7},{2,4},{3,1},{4,6},{5,3},{6,0},{7,5},{8,10},{9,15},{10,... | collective-permute-start | bytes 2703368 | tf_op jit(solution)/shard_map/ppermute | solution.py:59
  23.5 2.5 %collective-permute-start.30 = (bf16[176,2560]{1,0:T(8,128)(2,1)S(1)}, bf16[176,2560]{1,0:T(8,128)(2,1)}, u32[]{:S(2)}, u32[]{:S(2)}) collective-permute-start(bf16[176,2560]{1,0:T(8,128)(2,1)S(1)} %shard_map.77.refs_0_), channel_id=1, source_target_pairs={{0,1},{1,0},{2,3},{3,2},{4,5},{5,4},{6,7},{7,6},{8,9},{9,8},{10,11... | collective-permute-start | bytes 2703368 | tf_op jit(solution)/shard_map/ppermute | solution.py:63
  26.2 29.6 %collective-permute-done.33.refs_0_ = bf16[176,2560]{1,0:T(8,128)(2,1)} collective-permute-done((bf16[176,2560]{1,0:T(8,128)(2,1)S(1)}, bf16[176,2560]{1,0:T(8,128)(2,1)}, u32[]{:S(2)}, u32[]{:S(2)}) %collective-permute-start.33) | collective-permute-done | bytes 901152 | tf_op jit(solution)/shard_map/ppermute | solution.py:59
  55.9 25.1 %collective-permute-start.34 = (bf16[176,2560]{1,0:T(8,128)(2,1)}, bf16[176,2560]{1,0:T(8,128)(2,1)}, u32[]{:S(2)}, u32[]{:S(2)}) collective-permute-start(bf16[176,2560]{1,0:T(8,128)(2,1)} %collective-permute-done.33.refs_0_), channel_id=1, source_target_pairs={{0,1},{1,0},{2,3},{3,2},{4,5},{5,4},{6,7},{7,6},{8,9},{9,8},{10,11... | collective-permute-start | bytes 2703368 | tf_op jit(solution)/shard_map/ppermute | solution.py:63
  85.3 3.7 %collective-permute-start.35 = (bf16[176,2560]{1,0:T(8,128)(2,1)}, bf16[176,2560]{1,0:T(8,128)(2,1)}, u32[]{:S(2)}, u32[]{:S(2)}) collective-permute-start(bf16[176,2560]{1,0:T(8,128)(2,1)} %shard_map.79.refs_0_), channel_id=1, source_target_pairs={{0,2},{1,7},{2,4},{3,1},{4,6},{5,3},{6,0},{7,5},{8,10},{9,15},{10,... | collective-permute-start | bytes 2703368 | tf_op jit(solution)/shard_map/ppermute | solution.py:59
  90.8 3.2 %shard_map.78.refs_1_ = bf16[2,320,176]{2,1,0:T(8,128)(2,1)} custom-call(s32[2]{0:T(128)S(1)} %pad_add_fusion.ids_ref, bf16[320,2560]{1,0:T(8,128)(2,1)S(1)} %divide_convert_fusion.weight_ref, bf16[8,480,128]{2,1,0:T(8,128)(2,1)S(1)} %copy-done.1, bf16[176,2560]{1,0:T(8,128)(2,1)S(1)} %shard_map.77.refs_0_, bf16[176,2560]{1,0:T(8,128)(2,1)} %collective-permute-done.30.refs_1_), custom_call_target="tpu_custom_call" | custom-call | flops 576716800 | bytes 1802240 | tf_op jit(solution)/shard_map/pallas_call | solution.py:87
  94.1 3.5 %shard_map.81.refs_3_ = bf16[2,320,176]{2,1,0:T(8,128)(2,1)} custom-call(s32[2]{0:T(128)S(1)} %pad_add_fusion.2.ids_ref, bf16[320,2560]{1,0:T(8,128)(2,1)S(1)} %divide_convert_fusion.weight_ref, bf16[8,480,128]{2,1,0:T(8,128)(2,1)S(1)} %copy-done.1, bf16[176,2560]{1,0:T(8,128)(2,1)} %collective-permute-done.33.refs_0_, ...), custom_call_target="tpu_custom_call" | custom-call | flops 576716800 | bytes 1802240 | tf_op jit(solution)/shard_map/pallas_call | solution.py:87
  97.6 3.5 %shard_map.80.refs_2_ = bf16[2,320,176]{2,1,0:T(8,128)(2,1)} custom-call(s32[2]{0:T(128)S(1)} %pad_add_fusion.1.ids_ref, bf16[320,2560]{1,0:T(8,128)(2,1)S(1)} %divide_convert_fusion.weight_ref, bf16[8,480,128]{2,1,0:T(8,128)(2,1)S(1)} %copy-done.1, bf16[176,2560]{1,0:T(8,128)(2,1)} %shard_map.79.refs_0_, bf16[176,2560]{1,0:T(8,128)(2,1)S(1)} %collective-permute-done.32.refs_1_), custom_call_target="tpu_custom_call" | custom-call | flops 576716800 | bytes 1802240 | tf_op jit(solution)/shard_map/pallas_call | solution.py:87
  103.2 12.4 %collective-permute-start.36 = (bf16[176,2560]{1,0:T(8,128)(2,1)}, bf16[176,2560]{1,0:T(8,128)(2,1)}, u32[]{:S(2)}, u32[]{:S(2)}) collective-permute-start(bf16[176,2560]{1,0:T(8,128)(2,1)} %shard_map.82.refs_0_), channel_id=1, source_target_pairs={{0,1},{1,0},{2,3},{3,2},{4,5},{5,4},{6,7},{7,6},{8,9},{9,8},{10,11... | collective-permute-start | bytes 2703368 | tf_op jit(solution)/shard_map/ppermute | solution.py:63
  118.3 2.1 %shard_map.84 = bf16[1,320,176]{2,1,0:T(8,128)(2,1)S(1)} custom-call(s32[1]{0:T(128)} %bitcast.15.ids_ref, bf16[320,2560]{1,0:T(8,128)(2,1)S(1)} %divide_convert_fusion.weight_ref, bf16[8,480,128]{2,1,0:T(8,128)(2,1)S(1)} %copy-done.1, bf16[176,2560]{1,0:T(8,128)(2,1)} %collective-permute-done.36.refs_0_), custom_call_target="tpu_custom_call" | custom-call | flops 288358400 | bytes 901120 | tf_op jit(solution)/shard_map/pallas_call | solution.py:87
  120.5 47.3 %conditional.1 = (bf16[320,2560]{1,0:T(8,128)(2,1)S(1)}, f32[1]{0:T(128)}, f32[1]{0:T(128)}, f32[1]{0:T(128)}) conditional(s32[]{:T(128)} %clamp.3, (bf16[2,320,176]{2,1,0:T(8,128)(2,1)S(1)}, bf16[2,320,176]{2,1,0:T(8,128)(2,1)S(1)}, bf16[2,320,176]{2,1,0:T(8,128)(2,1)S(1)}, bf16[1,320,176]{2,1,0:T(8,128)(2,1)S(1)}, ...), branch_computations={%region_0.1_spmd, %region_1.2_spmd, %region_2.3_spmd, %region_3.4_... | conditional | flops 2317516800 | bytes 21954808 | solution.py:173
  120.5 2.2 %branch_0_fun.4 = bf16[320,512]{1,0:T(8,128)(2,1)S(1)} custom-call(bf16[2,320,176]{2,1,0:T(8,128)(2,1)S(1)} %get-tuple-element.184.refs_0_, bf16[2,320,176]{2,1,0:T(8,128)(2,1)S(1)} %get-tuple-element.185.refs_1_, bf16[2,320,176]{2,1,0:T(8,128)(2,1)S(1)} %get-tuple-element.186.refs_2_, bf16[1,320,176]{2,1,0:T(8,128)(2,1)S(1)} %get-tuple-element.187.refs_3_, ...), custom_call_target="tpu_custom_call" | custom-call | flops 461373440 | bytes 1441792 | tf_op jit(solution)/shard_map/cond/branch_0_fun/pallas_call | solution.py:115
  122.7 3.1 %collective-permute-start = (bf16[320,512]{1,0:T(8,128)(2,1)S(1)}, bf16[320,512]{1,0:T(8,128)(2,1)S(1)}, u32[]{:S(2)}, u32[]{:S(2)}) collective-permute-start(bf16[320,512]{1,0:T(8,128)(2,1)S(1)} %branch_0_fun.4), channel_id=1, source_target_pairs={{504,0},{0,8},{8,16},{16,24},{24,32},{32,40},{40,48},{48,56},{56,6... | collective-permute-start | bytes 983048 | tf_op jit(solution)/shard_map/cond/branch_0_fun/ppermute | solution.py:141
  125.8 3.1 %collective-permute-start.4 = (f32[1]{0:T(128)}, f32[1]{0:T(128)}, u32[]{:S(2)}, u32[]{:S(2)}) collective-permute-start(f32[1]{0:T(128)} %get-tuple-element.286), channel_id=1, source_target_pairs={{504,0},{0,8},{8,16},{16,24},{24,32},{32,40},{40,48},{48,56},{56,6... | collective-permute-start | bytes 20 | tf_op jit(solution)/shard_map/cond/branch_0_fun/ppermute | solution.py:144
  128.9 2.2 %branch_0_fun.7 = bf16[320,512]{1,0:T(8,128)(2,1)S(1)} custom-call(bf16[2,320,176]{2,1,0:T(8,128)(2,1)S(1)} %get-tuple-element.184.refs_0_, bf16[2,320,176]{2,1,0:T(8,128)(2,1)S(1)} %get-tuple-element.185.refs_1_, bf16[2,320,176]{2,1,0:T(8,128)(2,1)S(1)} %get-tuple-element.186.refs_2_, bf16[1,320,176]{2,1,0:T(8,128)(2,1)S(1)} %get-tuple-element.187.refs_3_, ...), custom_call_target="tpu_custom_call" | custom-call | flops 461373440 | bytes 1441792 | tf_op jit(solution)/shard_map/cond/branch_0_fun/pallas_call | solution.py:115
  131.2 2.8 %collective-permute-start.3 = (bf16[320,512]{1,0:T(8,128)(2,1)S(1)}, bf16[320,512]{1,0:T(8,128)(2,1)S(1)}, u32[]{:S(2)}, u32[]{:S(2)}) collective-permute-start(bf16[320,512]{1,0:T(8,128)(2,1)S(1)} %branch_0_fun.7), channel_id=1, source_target_pairs={{504,0},{0,8},{8,16},{16,24},{24,32},{32,40},{40,48},{48,56},{56,6... | collective-permute-start | bytes 983048 | tf_op jit(solution)/shard_map/cond/branch_0_fun/ppermute | solution.py:141
  134.0 3.3 %branch_0_fun.5 = bf16[320,768]{1,0:T(8,128)(2,1)S(1)} custom-call(bf16[2,320,176]{2,1,0:T(8,128)(2,1)S(1)} %get-tuple-element.184.refs_0_, bf16[2,320,176]{2,1,0:T(8,128)(2,1)S(1)} %get-tuple-element.185.refs_1_, bf16[2,320,176]{2,1,0:T(8,128)(2,1)S(1)} %get-tuple-element.186.refs_2_, bf16[1,320,176]{2,1,0:T(8,128)(2,1)S(1)} %get-tuple-element.187.refs_3_, ...), custom_call_target="tpu_custom_call" | custom-call | flops 692060160 | bytes 2162688 | tf_op jit(solution)/shard_map/cond/branch_0_fun/pallas_call | solution.py:115
  137.3 3.1 %collective-permute-start.1 = (bf16[320,768]{1,0:T(8,128)(2,1)S(1)}, bf16[320,768]{1,0:T(8,128)(2,1)S(1)}, u32[]{:S(2)}, u32[]{:S(2)}) collective-permute-start(bf16[320,768]{1,0:T(8,128)(2,1)S(1)} %branch_0_fun.5), channel_id=1, source_target_pairs={{504,0},{0,8},{8,16},{16,24},{24,32},{32,40},{40,48},{48,56},{56,6... | collective-permute-start | bytes 1474568 | tf_op jit(solution)/shard_map/cond/branch_0_fun/ppermute | solution.py:141
  140.5 3.3 %branch_0_fun.6 = bf16[320,768]{1,0:T(8,128)(2,1)S(1)} custom-call(bf16[2,320,176]{2,1,0:T(8,128)(2,1)S(1)} %get-tuple-element.184.refs_0_, bf16[2,320,176]{2,1,0:T(8,128)(2,1)S(1)} %get-tuple-element.185.refs_1_, bf16[2,320,176]{2,1,0:T(8,128)(2,1)S(1)} %get-tuple-element.186.refs_2_, bf16[1,320,176]{2,1,0:T(8,128)(2,1)S(1)} %get-tuple-element.187.refs_3_, ...), custom_call_target="tpu_custom_call" | custom-call | flops 692060160 | bytes 2162688 | tf_op jit(solution)/shard_map/cond/branch_0_fun/pallas_call | solution.py:115
  143.8 3.1 %collective-permute-start.2 = (bf16[320,768]{1,0:T(8,128)(2,1)S(1)}, bf16[320,768]{1,0:T(8,128)(2,1)S(1)}, u32[]{:S(2)}, u32[]{:S(2)}) collective-permute-start(bf16[320,768]{1,0:T(8,128)(2,1)S(1)} %branch_0_fun.6), channel_id=1, source_target_pairs={{504,0},{0,8},{8,16},{16,24},{24,32},{32,40},{40,48},{48,56},{56,6... | collective-permute-start | bytes 1474568 | tf_op jit(solution)/shard_map/cond/branch_0_fun/ppermute | solution.py:141
  147.2 9.6 %collective-permute-done.1 = bf16[320,768]{1,0:T(8,128)(2,1)S(1)} collective-permute-done((bf16[320,768]{1,0:T(8,128)(2,1)S(1)}, bf16[320,768]{1,0:T(8,128)(2,1)S(1)}, u32[]{:S(2)}, u32[]{:S(2)}) %collective-permute-start.1) | collective-permute-done | bytes 491552 | tf_op jit(solution)/shard_map/cond/branch_0_fun/ppermute | solution.py:141
  156.9 10.4 %collective-permute-done.2 = bf16[320,768]{1,0:T(8,128)(2,1)S(1)} collective-permute-done((bf16[320,768]{1,0:T(8,128)(2,1)S(1)}, bf16[320,768]{1,0:T(8,128)(2,1)S(1)}, u32[]{:S(2)}, u32[]{:S(2)}) %collective-permute-start.2) | collective-permute-done | bytes 491552 | tf_op jit(solution)/shard_map/cond/branch_0_fun/ppermute | solution.py:141
  (53 shorter events, 14.5 us)
Async XLA Ops:
  2.5 13.1 %copy-start.10 = (f32[2560]{0:T(1024)S(1)}, f32[2560]{0:T(1024)}, u32[]{:S(2)}) copy-start(f32[2560]{0:T(1024)} %param.14) | copy-start | bytes 30724
  2.5 13.1 %copy-start.2 = (bf16[2,88,2560]{2,1,0:T(8,128)(2,1)S(1)}, bf16[2,88,2560]{2,1,0:T(8,128)(2,1)}, u32[]{:S(2)}) copy-start(bf16[2,88,2560]{2,1,0:T(8,128)(2,1)} %param.15) | copy-start | bytes 2703364
  3.8 77.2 %all-to-all-start = ((bf16[8,480,128]{2,1,0:T(8,128)(2,1)}), bf16[8,480,128]{2,1,0:T(8,128)(2,1)S(1)}, u32[]{:S(2)}, u32[]{:S(2)}) async-start(bf16[8,480,128]{2,1,0:T(8,128)(2,1)} %maximum_maximum_fusion), calls=%async_computation | async-start | bytes 1966080 | tf_op jit(solution)/shard_map/all_to_all | solution.py:154
  16.1 39.7 %collective-permute-start.33 = (bf16[176,2560]{1,0:T(8,128)(2,1)S(1)}, bf16[176,2560]{1,0:T(8,128)(2,1)}, u32[]{:S(2)}, u32[]{:S(2)}) collective-permute-start(bf16[176,2560]{1,0:T(8,128)(2,1)S(1)} %shard_map.77.refs_0_), channel_id=1, source_target_pairs={{0,6},{1,3},{2,0},{3,5},{4,2},{5,7},{6,4},{7,1},{8,14},{9,11},{10,... | collective-permute-start | bytes 2703368 | tf_op jit(solution)/shard_map/ppermute | solution.py:59
  20.3 60.7 %collective-permute-start.31 = (bf16[176,2560]{1,0:T(8,128)(2,1)S(1)}, bf16[176,2560]{1,0:T(8,128)(2,1)}, u32[]{:S(2)}, u32[]{:S(2)}) collective-permute-start(bf16[176,2560]{1,0:T(8,128)(2,1)S(1)} %shard_map.77.refs_0_), channel_id=1, source_target_pairs={{0,2},{1,7},{2,4},{3,1},{4,6},{5,3},{6,0},{7,5},{8,10},{9,15},{10,... | collective-permute-start | bytes 2703368 | tf_op jit(solution)/shard_map/ppermute | solution.py:59
  23.5 67.3 %collective-permute-start.30 = (bf16[176,2560]{1,0:T(8,128)(2,1)S(1)}, bf16[176,2560]{1,0:T(8,128)(2,1)}, u32[]{:S(2)}, u32[]{:S(2)}) collective-permute-start(bf16[176,2560]{1,0:T(8,128)(2,1)S(1)} %shard_map.77.refs_0_), channel_id=1, source_target_pairs={{0,1},{1,0},{2,3},{3,2},{4,5},{5,4},{6,7},{7,6},{8,9},{9,8},{10,11... | collective-permute-start | bytes 2703368 | tf_op jit(solution)/shard_map/ppermute | solution.py:63
  55.9 38.2 %collective-permute-start.34 = (bf16[176,2560]{1,0:T(8,128)(2,1)}, bf16[176,2560]{1,0:T(8,128)(2,1)}, u32[]{:S(2)}, u32[]{:S(2)}) collective-permute-start(bf16[176,2560]{1,0:T(8,128)(2,1)} %collective-permute-done.33.refs_0_), channel_id=1, source_target_pairs={{0,1},{1,0},{2,3},{3,2},{4,5},{5,4},{6,7},{7,6},{8,9},{9,8},{10,11... | collective-permute-start | bytes 2703368 | tf_op jit(solution)/shard_map/ppermute | solution.py:63
  81.0 0.9 copy-start
  82.7 14.9 %collective-permute-start.32 = (bf16[176,2560]{1,0:T(8,128)(2,1)}, bf16[176,2560]{1,0:T(8,128)(2,1)S(1)}, u32[]{:S(2)}, u32[]{:S(2)}) collective-permute-start(bf16[176,2560]{1,0:T(8,128)(2,1)} %shard_map.79.refs_0_), channel_id=1, source_target_pairs={{0,1},{1,0},{2,3},{3,2},{4,5},{5,4},{6,7},{7,6},{8,9},{9,8},{10,11... | collective-permute-start | bytes 2703368 | tf_op jit(solution)/shard_map/ppermute | solution.py:63
  85.3 17.2 %collective-permute-start.35 = (bf16[176,2560]{1,0:T(8,128)(2,1)}, bf16[176,2560]{1,0:T(8,128)(2,1)}, u32[]{:S(2)}, u32[]{:S(2)}) collective-permute-start(bf16[176,2560]{1,0:T(8,128)(2,1)} %shard_map.79.refs_0_), channel_id=1, source_target_pairs={{0,2},{1,7},{2,4},{3,1},{4,6},{5,3},{6,0},{7,5},{8,10},{9,15},{10,... | collective-permute-start | bytes 2703368 | tf_op jit(solution)/shard_map/ppermute | solution.py:59
  89.0 1.8 %copy-start.1 = (bf16[8,480,128]{2,1,0:T(8,128)(2,1)S(1)}, bf16[8,480,128]{2,1,0:T(8,128)(2,1)}, u32[]{:S(2)}) copy-start(bf16[8,480,128]{2,1,0:T(8,128)(2,1)} %copy-done) | copy-start | bytes 2949124
  97.6 3.5 %copy-start.4 = (bf16[176,2560]{1,0:T(8,128)(2,1)}, bf16[176,2560]{1,0:T(8,128)(2,1)S(1)}, u32[]{:S(2)}) copy-start(bf16[176,2560]{1,0:T(8,128)(2,1)S(1)} %collective-permute-done.32.refs_1_) | copy-start | bytes 2703364
  103.2 15.1 %collective-permute-start.36 = (bf16[176,2560]{1,0:T(8,128)(2,1)}, bf16[176,2560]{1,0:T(8,128)(2,1)}, u32[]{:S(2)}, u32[]{:S(2)}) collective-permute-start(bf16[176,2560]{1,0:T(8,128)(2,1)} %shard_map.82.refs_0_), channel_id=1, source_target_pairs={{0,1},{1,0},{2,3},{3,2},{4,5},{5,4},{6,7},{7,6},{8,9},{9,8},{10,11... | collective-permute-start | bytes 2703368 | tf_op jit(solution)/shard_map/ppermute | solution.py:63
  118.2 2.2 %copy-start.3 = (bf16[1,2560,320]{1,2,0:T(8,128)(2,1)S(1)}, bf16[1,2560,320]{1,2,0:T(8,128)(2,1)}, u32[]{:S(2)}) copy-start(bf16[1,2560,320]{1,2,0:T(8,128)(2,1)} %param.12) | copy-start | bytes 4915204
  118.3 2.1 %copy-start.5 = (bf16[176,2560]{1,0:T(8,128)(2,1)S(1)}, bf16[176,2560]{1,0:T(8,128)(2,1)}, u32[]{:S(2)}) copy-start(bf16[176,2560]{1,0:T(8,128)(2,1)} %copy-done.4) | copy-start | bytes 2703364
  118.3 2.1 %copy-start.6 = (bf16[2,320,176]{2,1,0:T(8,128)(2,1)S(1)}, bf16[2,320,176]{2,1,0:T(8,128)(2,1)}, u32[]{:S(2)}) copy-start(bf16[2,320,176]{2,1,0:T(8,128)(2,1)} %shard_map.78.refs_1_) | copy-start | bytes 675844
  118.3 2.1 %copy-start.7 = (bf16[2,320,176]{2,1,0:T(8,128)(2,1)S(1)}, bf16[2,320,176]{2,1,0:T(8,128)(2,1)}, u32[]{:S(2)}) copy-start(bf16[2,320,176]{2,1,0:T(8,128)(2,1)} %shard_map.81.refs_3_) | copy-start | bytes 675844
  118.3 2.2 %copy-start.8 = (bf16[2,320,176]{2,1,0:T(8,128)(2,1)S(1)}, bf16[2,320,176]{2,1,0:T(8,128)(2,1)}, u32[]{:S(2)}) copy-start(bf16[2,320,176]{2,1,0:T(8,128)(2,1)} %shard_map.80.refs_2_) | copy-start | bytes 675844
  122.7 24.3 %collective-permute-start = (bf16[320,512]{1,0:T(8,128)(2,1)S(1)}, bf16[320,512]{1,0:T(8,128)(2,1)S(1)}, u32[]{:S(2)}, u32[]{:S(2)}) collective-permute-start(bf16[320,512]{1,0:T(8,128)(2,1)S(1)} %branch_0_fun.4), channel_id=1, source_target_pairs={{504,0},{0,8},{8,16},{16,24},{24,32},{32,40},{40,48},{48,56},{56,6... | collective-permute-start | bytes 983048 | tf_op jit(solution)/shard_map/cond/branch_0_fun/ppermute | solution.py:141
  125.8 41.7 %collective-permute-start.4 = (f32[1]{0:T(128)}, f32[1]{0:T(128)}, u32[]{:S(2)}, u32[]{:S(2)}) collective-permute-start(f32[1]{0:T(128)} %get-tuple-element.286), channel_id=1, source_target_pairs={{504,0},{0,8},{8,16},{16,24},{24,32},{32,40},{40,48},{48,56},{56,6... | collective-permute-start | bytes 20 | tf_op jit(solution)/shard_map/cond/branch_0_fun/ppermute | solution.py:144
  131.2 15.9 %collective-permute-start.3 = (bf16[320,512]{1,0:T(8,128)(2,1)S(1)}, bf16[320,512]{1,0:T(8,128)(2,1)S(1)}, u32[]{:S(2)}, u32[]{:S(2)}) collective-permute-start(bf16[320,512]{1,0:T(8,128)(2,1)S(1)} %branch_0_fun.7), channel_id=1, source_target_pairs={{504,0},{0,8},{8,16},{16,24},{24,32},{32,40},{40,48},{48,56},{56,6... | collective-permute-start | bytes 983048 | tf_op jit(solution)/shard_map/cond/branch_0_fun/ppermute | solution.py:141
  137.3 19.4 %collective-permute-start.1 = (bf16[320,768]{1,0:T(8,128)(2,1)S(1)}, bf16[320,768]{1,0:T(8,128)(2,1)S(1)}, u32[]{:S(2)}, u32[]{:S(2)}) collective-permute-start(bf16[320,768]{1,0:T(8,128)(2,1)S(1)} %branch_0_fun.5), channel_id=1, source_target_pairs={{504,0},{0,8},{8,16},{16,24},{24,32},{32,40},{40,48},{48,56},{56,6... | collective-permute-start | bytes 1474568 | tf_op jit(solution)/shard_map/cond/branch_0_fun/ppermute | solution.py:141
  143.8 23.5 %collective-permute-start.2 = (bf16[320,768]{1,0:T(8,128)(2,1)S(1)}, bf16[320,768]{1,0:T(8,128)(2,1)S(1)}, u32[]{:S(2)}, u32[]{:S(2)}) collective-permute-start(bf16[320,768]{1,0:T(8,128)(2,1)S(1)} %branch_0_fun.6), channel_id=1, source_target_pairs={{504,0},{0,8},{8,16},{16,24},{24,32},{32,40},{40,48},{48,56},{56,6... | collective-permute-start | bytes 1474568 | tf_op jit(solution)/shard_map/cond/branch_0_fun/ppermute | solution.py:141
  167.8 1.2 copy-start.9

commit v3 on v2

v3 whole, which is shorter than its diff:
```python
from functools import partial

import jax
import jax.numpy as jnp
from jax import lax
from jax.experimental import pallas as pl
from jax.experimental.pallas import tpu as pltpu
from jax.sharding import PartitionSpec as P

DW = 2560
LEARN_RATE = 1.5
EPSILON = 1e-05
SCALE = DW ** (-0.5)
LANES = 128
CHUNKS = (512, 768, 768, 512)
VMEM = 12 * 2**20


def pack_cotangent(cot_t, parts):
    cols, tokens = cot_t.shape
    cot_t = cot_t.reshape(parts, cols // parts, tokens)
    half = cols // parts // 2
    rest = cot_t[:, :, LANES:]
    gap = jnp.zeros((parts, half, LANES - 2 * (tokens - LANES)), cot_t.dtype)
    folded = jnp.concatenate([rest[:, :half], rest[:, half:], gap], axis=2)
    return jnp.concatenate([cot_t[:, :, :LANES], folded], axis=1)


def norm_kernel(tokens_ref, gain_ref, out_ref):
    wide = tokens_ref[...].astype(jnp.float32)
    mean_square = jnp.mean(wide * wide, axis=-1, keepdims=True)
    out_ref[...] = (wide * lax.rsqrt(mean_square + EPSILON) * gain_ref[...]).astype(jnp.bfloat16)


def norm(tokens, gain):
    return pl.pallas_call(
        norm_kernel,
        out_shape=jax.ShapeDtypeStruct(tokens.shape, jnp.bfloat16),
        compiler_params=pltpu.CompilerParams(vmem_limit_bytes=VMEM),
        cost_estimate=pl.CostEstimate(flops=8 * tokens.size, bytes_accessed=4 * tokens.size, transcendentals=0),
    )(tokens, gain[None])


def copy_kernel(array_ref, token_ref, out_ref):
    out_ref[...] = array_ref[...]


def copy_after(array, token):
    return pl.pallas_call(
        copy_kernel,
        grid=(1,),
        in_specs=[pl.BlockSpec(array.shape, lambda i: (0, 0)), pl.BlockSpec((1, 16, LANES), lambda i: (0, 0, 0))],
        out_specs=pl.BlockSpec(array.shape, lambda i: (0, 0)),
        out_shape=jax.ShapeDtypeStruct(array.shape, array.dtype),
        compiler_params=pltpu.CompilerParams(vmem_limit_bytes=VMEM),
    )(array, token)


def once_there(array, *tokens):
    whole = pl.BlockSpec(memory_space=pl.ANY)
    return pl.pallas_call(
        lambda *refs: None,
        in_specs=[whole] + [pl.BlockSpec(memory_space=pltpu.VMEM)] * len(tokens),
        out_specs=whole,
        out_shape=jax.ShapeDtypeStruct(array.shape, array.dtype),
        input_output_aliases={0: 0},
        compiler_params=pltpu.CompilerParams(vmem_limit_bytes=VMEM),
    )(array, *tokens)


def to_chip(values, step):
    count = lax.axis_size("fsdp")
    route = [(i, (i // 2 + (-step if i % 2 else step)) % (count // 2) * 2 + i % 2) for i in range(count)]
    return lax.ppermute(values, "fsdp", route)


def to_core(values):
    return lax.ppermute(values, "fsdp", [(i, i ^ 1) for i in range(lax.axis_size("fsdp"))])


def grad_out_kernel(ids_ref, weight_ref, cot_ref, *refs):
    count = len(refs) - 4
    blocks, (out_ref, token_ref, held, sems) = refs[:count], refs[count:]
    _, cols, tokens = out_ref.shape
    half, rest = cols // 2, tokens - LANES
    copies = [pltpu.make_async_copy(block, held.at[i], sems.at[i]) for i, block in enumerate(blocks)]
    for copy in copies:
        copy.start()
    token_ref[...] = jnp.zeros(token_ref.shape, token_ref.dtype)
    for i, copy in enumerate(copies):
        copy.wait()
        pre_act = SCALE * lax.dot_general(
            weight_ref[...], held[i], (((1,), (1,)), ((), ())), preferred_element_type=jnp.float32
        )
        sig = jax.nn.sigmoid(pre_act)
        slope = sig * (1.0 + pre_act * (1.0 - sig))
        cot = cot_ref[ids_ref[i]]
        head = cot[:cols].astype(jnp.float32)
        tail = cot[cols:].astype(jnp.float32)
        out_ref[i, :, :LANES] = (head * slope[:, :LANES]).astype(jnp.bfloat16)
        out_ref[i, :half, LANES:] = (tail[:, :rest] * slope[:half, LANES:]).astype(jnp.bfloat16)
        out_ref[i, half:, LANES:] = (tail[:, rest : 2 * rest] * slope[half:, LANES:]).astype(jnp.bfloat16)


def grad_out(weight_t, packed, sources, blocks):
    cols, tokens = weight_t.shape[0], blocks[0].shape[0]
    vmem, whole = pl.BlockSpec(memory_space=pltpu.VMEM), pl.BlockSpec(memory_space=pl.ANY)
    return pl.pallas_call(
        grad_out_kernel,
        in_specs=[pl.BlockSpec(memory_space=pltpu.SMEM), vmem, vmem] + [whole] * len(blocks),
        out_specs=(vmem, vmem),
        out_shape=(
            jax.ShapeDtypeStruct((len(blocks), cols, tokens), jnp.bfloat16),
            jax.ShapeDtypeStruct((8, LANES), jnp.float32),
        ),
        scratch_shapes=[
            pltpu.VMEM((len(blocks), tokens, DW), jnp.bfloat16),
            pltpu.SemaphoreType.DMA((len(blocks),)),
        ],
        compiler_params=pltpu.CompilerParams(vmem_limit_bytes=VMEM),
        cost_estimate=pl.CostEstimate(flops=0, bytes_accessed=0, transcendentals=0),
    )(jnp.stack(sources), weight_t, packed, *blocks)


def local_kernel(groups, blocks, first, *refs):
    grads, blocks, (numer_ref, weight_ref) = refs[:groups], refs[groups : groups + blocks], refs[groups + blocks :][:2]
    out_ref, weight_out_ref, held, numer, sems = refs[-5:]
    width, tile = out_ref.shape[1], 256
    columns = pl.ds(first, width)
    copies = [pltpu.make_async_copy(block.at[:, columns], held.at[i], sems.at[i]) for i, block in enumerate(blocks)]
    copies.append(pltpu.make_async_copy(numer_ref.at[:, columns], numer, sems.at[len(blocks)]))
    for copy in copies:
        copy.start()
    weight_out_ref[0] = weight_ref[0]
    for copy in copies:
        copy.wait()
    terms = [grad_ref[i] for grad_ref in grads for i in range(grad_ref.shape[0])]
    for at in range(0, width, tile):
        part = slice(at, at + tile)
        total = jnp.zeros((out_ref.shape[0], tile), jnp.float32)
        for i, term in enumerate(terms):
            total += jnp.dot(term, held[i, :, part], preferred_element_type=jnp.float32)
        update = (LEARN_RATE * (SCALE * total)).astype(jnp.bfloat16)
        out_ref[:, part] = (numer[:, part].astype(jnp.float32) - update.astype(jnp.float32)).astype(jnp.bfloat16)


def local_chunk(grads, blocks, numer_t, weight, first, width):
    cols = numer_t.shape[0]
    tokens = blocks[0].shape[0]
    vmem, smem = pl.BlockSpec(memory_space=pltpu.VMEM), pl.BlockSpec(memory_space=pltpu.SMEM)
    whole = pl.BlockSpec(memory_space=pl.ANY)
    return pl.pallas_call(
        partial(local_kernel, len(grads), len(blocks), first),
        in_specs=[vmem] * len(grads) + [whole] * (len(blocks) + 1) + [smem],
        out_specs=(vmem, smem),
        out_shape=(jax.ShapeDtypeStruct((cols, width), jnp.bfloat16), jax.ShapeDtypeStruct((1,), jnp.float32)),
        scratch_shapes=[
            pltpu.VMEM((len(blocks), tokens, width), jnp.bfloat16),
            pltpu.VMEM((cols, width), jnp.bfloat16),
            pltpu.SemaphoreType.DMA((len(blocks) + 1,)),
        ],
        compiler_params=pltpu.CompilerParams(vmem_limit_bytes=VMEM),
        cost_estimate=pl.CostEstimate(flops=0, bytes_accessed=0, transcendentals=0),
    )(*grads, *blocks, numer_t, weight)


def route(distance):
    devices = range(lax.axis_size("rep"))
    return [((i - distance) % len(devices), i) for i in devices]


def mix_with(hop_size, grads, blocks, numer_t, weight):
    pieces, weights, first = [], [], 0
    for width in CHUNKS:
        local, handed_on = local_chunk(grads, blocks, numer_t, weight, first, width)
        weights.append(handed_on)
        partner = lax.ppermute(local, "rep", route(hop_size))
        pieces.append((0.5 * local.astype(jnp.float32) + 0.5 * partner.astype(jnp.float32)).astype(jnp.bfloat16))
        first += width
    new_weight = 0.5 * (weight + lax.ppermute(weights[1], "rep", route(hop_size)))
    return jnp.concatenate(pieces, axis=1), new_weight


def on_device(numerator, push_weight, norm_gain, activations, cotangent, step_index):
    count = lax.axis_size("fsdp")
    me = lax.axis_index("fsdp")
    core = me % 2
    ahead, back, far = ((me + step * (1 - 2 * core) + count) % count for step in (2, -2, 4))
    packed = pack_cotangent(cotangent.reshape(-1, cotangent.shape[2]).T, count)
    packed = lax.all_to_all(packed, "fsdp", split_axis=0, concat_axis=0, tiled=True)
    own = norm(activations.reshape(-1, DW), norm_gain)
    first = to_chip(own, 1)
    second = to_chip(copy_after(own, packed), -1)
    third = to_chip(first, 1)
    numer_t = numerator[0].T
    weight_t = (numer_t.astype(jnp.float32) / push_weight[0]).astype(jnp.bfloat16)
    held = [((me, me ^ 1), own), ((back, ahead ^ 1), first), ((ahead, back ^ 1), second)]
    blocks, grads, tokens = [], [], []
    for sources, block in held:
        pair = (block, to_core(block))
        blocks += pair
        grad, token = grad_out(weight_t, packed, sources, pair)
        grads.append(grad)
        tokens.append(token)
    third = once_there(third, *tokens)
    for source, block in ((far, third), (far ^ 1, to_core(third))):
        blocks.append(block)
        grads.append(grad_out(weight_t, packed, (source,), (block,))[0])
    bit_count = lax.axis_size("rep").bit_length() - 1
    branches = [partial(mix_with, 2**bit) for bit in range(bit_count)]
    mixed_t, new_weight = lax.switch(
        step_index % bit_count, branches, grads, blocks, numer_t, push_weight
    )
    return mixed_t.T[None], new_weight


def solution(mesh):
    placed = (
        P("rep", None, "fsdp"),
        P("rep"),
        P(),
        P(None, ("rep", "fsdp"), None),
        P(None, ("rep", "fsdp"), None),
        P(),
    )
    return jax.shard_map(
        on_device,
        mesh=mesh,
        in_specs=placed,
        out_specs=(P("rep", None, "fsdp"), P("rep")),
        check_vma=False,
    )
```

time: 171 us -> 199 us (1.16)
  waiting for transfers between devices: 51 us -> 93.8 us
  starting transfers between devices: 80.2 us -> 61.7 us
  Pallas kernels: 27.2 us -> 30.8 us
    ppermute x4, starting transfers between devices: 41.9 us -> 9.51 us  [to_core(): lax.ppermute(values, 'fsdp', [(i, i ^ 1) for i in range(lax.axis_size('fs...]
    ppermute x4, waiting for transfers between devices: 20 us -> 46 us  [mix_with(): partner = lax.ppermute(local, 'rep', route(hop_size))]
    all_to_all x1, waiting for transfers between devices: 0.01 us -> 14.6 us  [on_device(): lax.all_to_all(packed, 'fsdp', split_axis=0, concat_axis=0, tiled=True)]
    ppermute x4, starting transfers between devices: 12.2 us -> 25.4 us  [mix_with(): partner = lax.ppermute(local, 'rep', route(hop_size))]
    pallas_call x5, Pallas kernels: 14.3 us -> 17.5 us  [grad_out(): pl.pallas_call(grad_out_kernel, in_specs=[pl.BlockSpec(memory_space=pltpu...]
    ppermute x3, waiting for transfers between devices: 31 us -> 33 us  [to_chip(): return lax.ppermute(values, 'fsdp', route)]
  transfers between devices with their start and end apart: 13 -> 13, of which waited for: 4 -> 7; matrix products, arithmetic and copies ran while one was open for 2% -> 1% of each run, Pallas kernels for 13% -> 13%
where the time goes in v3:
time: 199 us; the launch traced here: 197 us
  waiting for transfers between devices  93.8 us (47%)
  starting transfers between devices  61.7 us (31%)
  Pallas kernels  30.8 us (15%)
  between operations  4.03 us (2%)
  other arithmetic  3.82 us (2%)
  local copies, waits for them, and re-layouts  2.4 us (1%)
    ppermute x4, waiting for transfers between devices, mix_with(): partner = lax.ppermute(local, 'rep', route(hop_size))  46 us
    ppermute x3, waiting for transfers between devices, to_chip(): return lax.ppermute(values, 'fsdp', route)  33 us
    ppermute x4, starting transfers between devices, mix_with(): partner = lax.ppermute(local, 'rep', route(hop_size))  25.4 us
    pallas_call x5, Pallas kernels, grad_out(): pl.pallas_call(grad_out_kernel, in_specs=[pl.BlockSpec(memory_space=pltpu...  17.5 us
    all_to_all x1, waiting for transfers between devices, on_device(): lax.all_to_all(packed, 'fsdp', split_axis=0, concat_axis=0, tiled=True)  14.6 us
    pallas_call x4, Pallas kernels, local_chunk(): pl.pallas_call(partial(local_kernel, len(grads), len(blocks), first), in_...  12.8 us
    ppermute x3, starting transfers between devices, to_chip(): return lax.ppermute(values, 'fsdp', route)  12.5 us
    all_to_all x1, starting transfers between devices, on_device(): lax.all_to_all(packed, 'fsdp', split_axis=0, concat_axis=0, tiled=True)  11.8 us
  transfers between devices with their start and end apart: 13, of which 7 were waited for; matrix products, arithmetic and copies ran while one was open for 1% of the time, Pallas kernels for 13%

profile of v3, /device:TPU:1, one launch (start us, length us, event | category | flops | bytes accessed | tf_op | source)
XLA Modules:
  0.0 196.9 jit_solution(5404668354849597264)
XLA Ops:
  3.8 11.8 %all-to-all-start = ((bf16[8,480,128]{2,1,0:T(8,128)(2,1)}), bf16[8,480,128]{2,1,0:T(8,128)(2,1)S(1)}, u32[]{:S(2)}, u32[]{:S(2)}) async-start(bf16[8,480,128]{2,1,0:T(8,128)(2,1)} %maximum_maximum_fusion), calls=%async_computation | async-start | bytes 1966080 | tf_op jit(solution)/shard_map/all_to_all | solution.py:190
  16.1 5.4 %collective-permute-start.31 = (bf16[176,2560]{1,0:T(8,128)(2,1)S(1)}, bf16[176,2560]{1,0:T(8,128)(2,1)}, u32[]{:S(2)}, u32[]{:S(2)}) collective-permute-start(bf16[176,2560]{1,0:T(8,128)(2,1)S(1)} %shard_map.77.refs_0_.array_ref), channel_id=1, source_target_pairs={{0,2},{1,7},{2,4},{3,1},{4,6},{5,3},{6,0},{7,5},{8,10},{9,15},{10,... | collective-permute-start | bytes 2703368 | tf_op jit(solution)/shard_map/ppermute | solution.py:74
  21.5 14.6 %all-to-all-done.cot_ref.token_ref = bf16[8,480,128]{2,1,0:T(8,128)(2,1)S(1)} async-done(((bf16[8,480,128]{2,1,0:T(8,128)(2,1)}), bf16[8,480,128]{2,1,0:T(8,128)(2,1)S(1)}, u32[]{:S(2)}, u32[]{:S(2)}) %all-to-all-start) | async-done | bytes 983072 | tf_op jit(solution)/shard_map/all_to_all | solution.py:190
  36.2 3.6 %collective-permute-start.33 = (bf16[176,2560]{1,0:T(8,128)(2,1)S(1)}, bf16[176,2560]{1,0:T(8,128)(2,1)}, u32[]{:S(2)}, u32[]{:S(2)}) collective-permute-start(bf16[176,2560]{1,0:T(8,128)(2,1)S(1)} %shard_map.80), channel_id=1, source_target_pairs={{0,6},{1,3},{2,0},{3,5},{4,2},{5,7},{6,4},{7,1},{8,14},{9,11},{10,... | collective-permute-start | bytes 2703368 | tf_op jit(solution)/shard_map/ppermute | solution.py:74
  39.8 3.3 %collective-permute-start.30 = (bf16[176,2560]{1,0:T(8,128)(2,1)S(1)}, bf16[176,2560]{1,0:T(8,128)(2,1)}, u32[]{:S(2)}, u32[]{:S(2)}) collective-permute-start(bf16[176,2560]{1,0:T(8,128)(2,1)S(1)} %shard_map.77.refs_0_.array_ref), channel_id=1, source_target_pairs={{0,1},{1,0},{2,3},{3,2},{4,5},{5,4},{6,7},{7,6},{8,9},{9,8},{10,11... | collective-permute-start | bytes 2703368 | tf_op jit(solution)/shard_map/ppermute | solution.py:78
  43.2 21.4 %collective-permute-done.31.refs_0_ = bf16[176,2560]{1,0:T(8,128)(2,1)} collective-permute-done((bf16[176,2560]{1,0:T(8,128)(2,1)S(1)}, bf16[176,2560]{1,0:T(8,128)(2,1)}, u32[]{:S(2)}, u32[]{:S(2)}) %collective-permute-start.31) | collective-permute-done | bytes 901152 | tf_op jit(solution)/shard_map/ppermute | solution.py:74
  64.6 3.5 %collective-permute-start.35 = (bf16[176,2560]{1,0:T(8,128)(2,1)}, bf16[176,2560]{1,0:T(8,128)(2,1)}, u32[]{:S(2)}, u32[]{:S(2)}) collective-permute-start(bf16[176,2560]{1,0:T(8,128)(2,1)} %collective-permute-done.31.refs_0_), channel_id=1, source_target_pairs={{0,2},{1,7},{2,4},{3,1},{4,6},{5,3},{6,0},{7,5},{8,10},{9,15},{10,... | collective-permute-start | bytes 2703368 | tf_op jit(solution)/shard_map/ppermute | solution.py:74
  75.0 3.8 %shard_map.78 = (bf16[2,320,176]{2,1,0:T(8,128)(2,1)}, f32[8,128]{1,0:T(8,128)S(1)}) custom-call(s32[2]{0:T(128)S(1)} %pad_add_fusion.ids_ref, bf16[320,2560]{1,0:T(8,128)(2,1)S(1)} %divide_convert_fusion.weight_ref, bf16[8,480,128]{2,1,0:T(8,128)(2,1)S(1)} %all-to-all-done.cot_ref.token_ref, bf16[176,2560]{1,0:T(8,128)(2,1)S(1)} %shard_map.77.refs_0_.array_ref, ...), custom_call_target="tpu_custom_call" | custom-call | tf_op jit(solution)/shard_map/pallas_call | solution.py:108
  78.9 4.8 %shard_map.79 = (bf16[2,320,176]{2,1,0:T(8,128)(2,1)}, f32[8,128]{1,0:T(8,128)S(1)}) custom-call(s32[2]{0:T(128)S(1)} %pad_add_fusion.1.ids_ref, bf16[320,2560]{1,0:T(8,128)(2,1)S(1)} %divide_convert_fusion.weight_ref, bf16[8,480,128]{2,1,0:T(8,128)(2,1)S(1)} %all-to-all-done.cot_ref.token_ref, bf16[176,2560]{1,0:T(8,128)(2,1)} %collective-permute-done.31.refs_0_, ...), custom_call_target="tpu_custom_call" | custom-call | tf_op jit(solution)/shard_map/pallas_call | solution.py:108
  83.7 4.8 %shard_map.81 = (bf16[2,320,176]{2,1,0:T(8,128)(2,1)}, f32[8,128]{1,0:T(8,128)S(1)}) custom-call(s32[2]{0:T(128)S(1)} %pad_add_fusion.2.ids_ref, bf16[320,2560]{1,0:T(8,128)(2,1)S(1)} %divide_convert_fusion.weight_ref, bf16[8,480,128]{2,1,0:T(8,128)(2,1)S(1)} %all-to-all-done.cot_ref.token_ref, bf16[176,2560]{1,0:T(8,128)(2,1)} %collective-permute-done.33.refs_0_, ...), custom_call_target="tpu_custom_call" | custom-call | tf_op jit(solution)/shard_map/pallas_call | solution.py:108
  88.5 11.6 %collective-permute-done.35.refs_0_ = bf16[176,2560]{1,0:T(8,128)(2,1)} collective-permute-done((bf16[176,2560]{1,0:T(8,128)(2,1)}, bf16[176,2560]{1,0:T(8,128)(2,1)}, u32[]{:S(2)}, u32[]{:S(2)}) %collective-permute-start.35) | collective-permute-done | bytes 901152 | tf_op jit(solution)/shard_map/ppermute | solution.py:74
  107.0 87.6 %conditional.1 = (bf16[320,2560]{1,0:T(8,128)(2,1)S(1)}, f32[1]{0:T(128)}, f32[1]{0:T(128)}, f32[1]{0:T(128)}) conditional(s32[]{:T(128)} %clamp.3, (bf16[2,320,176]{2,1,0:T(8,128)(2,1)S(1)}, bf16[2,320,176]{2,1,0:T(8,128)(2,1)S(1)}, bf16[2,320,176]{2,1,0:T(8,128)(2,1)S(1)}, bf16[1,320,176]{2,1,0:T(8,128)(2,1)S(1)}, ...), branch_computations={%region_0.1_spmd, %region_1.2_spmd, %region_2.3_spmd, %region_3.4_... | conditional | flops 10649600 | bytes 14745848 | solution.py:211
  107.3 3.0 %branch_3_fun.4 = (bf16[320,512]{1,0:T(8,128)(2,1)S(1)}, f32[1]{0:T(128)}) custom-call(bf16[2,320,176]{2,1,0:T(8,128)(2,1)S(1)} %get-tuple-element.244.refs_0_, bf16[2,320,176]{2,1,0:T(8,128)(2,1)S(1)} %get-tuple-element.245.refs_1_, bf16[2,320,176]{2,1,0:T(8,128)(2,1)S(1)} %get-tuple-element.246.refs_2_, ...), custom_call_target="tpu_custom_call" | custom-call | tf_op jit(solution)/shard_map/cond/branch_3_fun/pallas_call | solution.py:152
  110.2 4.2 %collective-permute-start.15 = (bf16[320,512]{1,0:T(8,128)(2,1)S(1)}, bf16[320,512]{1,0:T(8,128)(2,1)S(1)}, u32[]{:S(2)}, u32[]{:S(2)}) collective-permute-start(bf16[320,512]{1,0:T(8,128)(2,1)S(1)} %get-tuple-element.259), channel_id=1, source_target_pairs={{448,0},{456,8},{464,16},{472,24},{480,32},{488,40},{496,48},{504,... | collective-permute-start | bytes 983048 | tf_op jit(solution)/shard_map/cond/branch_3_fun/ppermute | solution.py:177
  114.5 3.0 %branch_3_fun.7 = (bf16[320,512]{1,0:T(8,128)(2,1)S(1)}, f32[1]{0:T(128)}) custom-call(bf16[2,320,176]{2,1,0:T(8,128)(2,1)S(1)} %get-tuple-element.244.refs_0_, bf16[2,320,176]{2,1,0:T(8,128)(2,1)S(1)} %get-tuple-element.245.refs_1_, bf16[2,320,176]{2,1,0:T(8,128)(2,1)S(1)} %get-tuple-element.246.refs_2_, ...), custom_call_target="tpu_custom_call" | custom-call | tf_op jit(solution)/shard_map/cond/branch_3_fun/pallas_call | solution.py:152
  117.4 5.4 %collective-permute-start.18 = (bf16[320,512]{1,0:T(8,128)(2,1)S(1)}, bf16[320,512]{1,0:T(8,128)(2,1)S(1)}, u32[]{:S(2)}, u32[]{:S(2)}) collective-permute-start(bf16[320,512]{1,0:T(8,128)(2,1)S(1)} %get-tuple-element.262), channel_id=1, source_target_pairs={{448,0},{456,8},{464,16},{472,24},{480,32},{488,40},{496,48},{504,... | collective-permute-start | bytes 983048 | tf_op jit(solution)/shard_map/cond/branch_3_fun/ppermute | solution.py:177
  122.9 3.4 %branch_3_fun.5 = (bf16[320,768]{1,0:T(8,128)(2,1)S(1)}, f32[1]{0:T(128)}) custom-call(bf16[2,320,176]{2,1,0:T(8,128)(2,1)S(1)} %get-tuple-element.244.refs_0_, bf16[2,320,176]{2,1,0:T(8,128)(2,1)S(1)} %get-tuple-element.245.refs_1_, bf16[2,320,176]{2,1,0:T(8,128)(2,1)S(1)} %get-tuple-element.246.refs_2_, ...), custom_call_target="tpu_custom_call" | custom-call | tf_op jit(solution)/shard_map/cond/branch_3_fun/pallas_call | solution.py:152
  126.3 2.4 %collective-permute-start.19 = (f32[1]{0:T(128)}, f32[1]{0:T(128)}, u32[]{:S(2)}, u32[]{:S(2)}) collective-permute-start(f32[1]{0:T(128)} %get-tuple-element.263), channel_id=1, source_target_pairs={{448,0},{456,8},{464,16},{472,24},{480,32},{488,40},{496,48},{504,... | collective-permute-start | bytes 20 | tf_op jit(solution)/shard_map/cond/branch_3_fun/ppermute | solution.py:180
  128.7 11.6 %collective-permute-start.16 = (bf16[320,768]{1,0:T(8,128)(2,1)S(1)}, bf16[320,768]{1,0:T(8,128)(2,1)S(1)}, u32[]{:S(2)}, u32[]{:S(2)}) collective-permute-start(bf16[320,768]{1,0:T(8,128)(2,1)S(1)} %get-tuple-element.260), channel_id=1, source_target_pairs={{448,0},{456,8},{464,16},{472,24},{480,32},{488,40},{496,48},{504,... | collective-permute-start | bytes 1474568 | tf_op jit(solution)/shard_map/cond/branch_3_fun/ppermute | solution.py:177
  140.3 3.4 %branch_3_fun.6 = (bf16[320,768]{1,0:T(8,128)(2,1)S(1)}, f32[1]{0:T(128)}) custom-call(bf16[2,320,176]{2,1,0:T(8,128)(2,1)S(1)} %get-tuple-element.244.refs_0_, bf16[2,320,176]{2,1,0:T(8,128)(2,1)S(1)} %get-tuple-element.245.refs_1_, bf16[2,320,176]{2,1,0:T(8,128)(2,1)S(1)} %get-tuple-element.246.refs_2_, ...), custom_call_target="tpu_custom_call" | custom-call | tf_op jit(solution)/shard_map/cond/branch_3_fun/pallas_call | solution.py:152
  143.7 4.2 %collective-permute-start.17 = (bf16[320,768]{1,0:T(8,128)(2,1)S(1)}, bf16[320,768]{1,0:T(8,128)(2,1)S(1)}, u32[]{:S(2)}, u32[]{:S(2)}) collective-permute-start(bf16[320,768]{1,0:T(8,128)(2,1)S(1)} %get-tuple-element.261), channel_id=1, source_target_pairs={{448,0},{456,8},{464,16},{472,24},{480,32},{488,40},{496,48},{504,... | collective-permute-start | bytes 1474568 | tf_op jit(solution)/shard_map/cond/branch_3_fun/ppermute | solution.py:177
  148.1 2.8 %collective-permute-done.18 = bf16[320,512]{1,0:T(8,128)(2,1)S(1)} collective-permute-done((bf16[320,512]{1,0:T(8,128)(2,1)S(1)}, bf16[320,512]{1,0:T(8,128)(2,1)S(1)}, u32[]{:S(2)}, u32[]{:S(2)}) %collective-permute-start.18) | collective-permute-done | bytes 327712 | tf_op jit(solution)/shard_map/cond/branch_3_fun/ppermute | solution.py:177
  151.0 20.6 %collective-permute-done.16 = bf16[320,768]{1,0:T(8,128)(2,1)S(1)} collective-permute-done((bf16[320,768]{1,0:T(8,128)(2,1)S(1)}, bf16[320,768]{1,0:T(8,128)(2,1)S(1)}, u32[]{:S(2)}, u32[]{:S(2)}) %collective-permute-start.16) | collective-permute-done | bytes 491552 | tf_op jit(solution)/shard_map/cond/branch_3_fun/ppermute | solution.py:177
  171.8 22.6 %collective-permute-done.17 = bf16[320,768]{1,0:T(8,128)(2,1)S(1)} collective-permute-done((bf16[320,768]{1,0:T(8,128)(2,1)S(1)}, bf16[320,768]{1,0:T(8,128)(2,1)S(1)}, u32[]{:S(2)}, u32[]{:S(2)}) %collective-permute-start.17) | collective-permute-done | bytes 491552 | tf_op jit(solution)/shard_map/cond/branch_3_fun/ppermute | solution.py:177
  (45 shorter events, 17.2 us)
Async XLA Ops:
  2.5 13.1 %copy-start.6 = (f32[2560]{0:T(1024)S(1)}, f32[2560]{0:T(1024)}, u32[]{:S(2)}) copy-start(f32[2560]{0:T(1024)} %param.14) | copy-start | bytes 30724
  2.5 13.1 %copy-start = (bf16[2,88,2560]{2,1,0:T(8,128)(2,1)S(1)}, bf16[2,88,2560]{2,1,0:T(8,128)(2,1)}, u32[]{:S(2)}) copy-start(bf16[2,88,2560]{2,1,0:T(8,128)(2,1)} %param.15) | copy-start | bytes 2703364
  3.8 32.3 %all-to-all-start = ((bf16[8,480,128]{2,1,0:T(8,128)(2,1)}), bf16[8,480,128]{2,1,0:T(8,128)(2,1)S(1)}, u32[]{:S(2)}, u32[]{:S(2)}) async-start(bf16[8,480,128]{2,1,0:T(8,128)(2,1)} %maximum_maximum_fusion), calls=%async_computation | async-start | bytes 1966080 | tf_op jit(solution)/shard_map/all_to_all | solution.py:190
  16.1 48.5 %collective-permute-start.31 = (bf16[176,2560]{1,0:T(8,128)(2,1)S(1)}, bf16[176,2560]{1,0:T(8,128)(2,1)}, u32[]{:S(2)}, u32[]{:S(2)}) collective-permute-start(bf16[176,2560]{1,0:T(8,128)(2,1)S(1)} %shard_map.77.refs_0_.array_ref), channel_id=1, source_target_pairs={{0,2},{1,7},{2,4},{3,1},{4,6},{5,3},{6,0},{7,5},{8,10},{9,15},{10,... | collective-permute-start | bytes 2703368 | tf_op jit(solution)/shard_map/ppermute | solution.py:74
  36.2 33.9 %collective-permute-start.33 = (bf16[176,2560]{1,0:T(8,128)(2,1)S(1)}, bf16[176,2560]{1,0:T(8,128)(2,1)}, u32[]{:S(2)}, u32[]{:S(2)}) collective-permute-start(bf16[176,2560]{1,0:T(8,128)(2,1)S(1)} %shard_map.80), channel_id=1, source_target_pairs={{0,6},{1,3},{2,0},{3,5},{4,2},{5,7},{6,4},{7,1},{8,14},{9,11},{10,... | collective-permute-start | bytes 2703368 | tf_op jit(solution)/shard_map/ppermute | solution.py:74
  39.8 35.2 %collective-permute-start.30 = (bf16[176,2560]{1,0:T(8,128)(2,1)S(1)}, bf16[176,2560]{1,0:T(8,128)(2,1)}, u32[]{:S(2)}, u32[]{:S(2)}) collective-permute-start(bf16[176,2560]{1,0:T(8,128)(2,1)S(1)} %shard_map.77.refs_0_.array_ref), channel_id=1, source_target_pairs={{0,1},{1,0},{2,3},{3,2},{4,5},{5,4},{6,7},{7,6},{8,9},{9,8},{10,11... | collective-permute-start | bytes 2703368 | tf_op jit(solution)/shard_map/ppermute | solution.py:78
  64.6 35.5 %collective-permute-start.35 = (bf16[176,2560]{1,0:T(8,128)(2,1)}, bf16[176,2560]{1,0:T(8,128)(2,1)}, u32[]{:S(2)}, u32[]{:S(2)}) collective-permute-start(bf16[176,2560]{1,0:T(8,128)(2,1)} %collective-permute-done.31.refs_0_), channel_id=1, source_target_pairs={{0,2},{1,7},{2,4},{3,1},{4,6},{5,3},{6,0},{7,5},{8,10},{9,15},{10,... | collective-permute-start | bytes 2703368 | tf_op jit(solution)/shard_map/ppermute | solution.py:74
  68.2 10.7 %collective-permute-start.32 = (bf16[176,2560]{1,0:T(8,128)(2,1)}, bf16[176,2560]{1,0:T(8,128)(2,1)}, u32[]{:S(2)}, u32[]{:S(2)}) collective-permute-start(bf16[176,2560]{1,0:T(8,128)(2,1)} %collective-permute-done.31.refs_0_), channel_id=1, source_target_pairs={{0,1},{1,0},{2,3},{3,2},{4,5},{5,4},{6,7},{7,6},{8,9},{9,8},{10,11... | collective-permute-start | bytes 2703368 | tf_op jit(solution)/shard_map/ppermute | solution.py:78
  70.1 13.6 %collective-permute-start.34 = (bf16[176,2560]{1,0:T(8,128)(2,1)}, bf16[176,2560]{1,0:T(8,128)(2,1)}, u32[]{:S(2)}, u32[]{:S(2)}) collective-permute-start(bf16[176,2560]{1,0:T(8,128)(2,1)} %collective-permute-done.33.refs_0_), channel_id=1, source_target_pairs={{0,1},{1,0},{2,3},{3,2},{4,5},{5,4},{6,7},{7,6},{8,9},{9,8},{10,11... | collective-permute-start | bytes 2703368 | tf_op jit(solution)/shard_map/ppermute | solution.py:78
  100.1 4.7 %collective-permute-start.36 = (bf16[176,2560]{1,0:T(8,128)(2,1)}, bf16[176,2560]{1,0:T(8,128)(2,1)}, u32[]{:S(2)}, u32[]{:S(2)}) collective-permute-start(bf16[176,2560]{1,0:T(8,128)(2,1)} %shard_map.82.refs_0_), channel_id=1, source_target_pairs={{0,1},{1,0},{2,3},{3,2},{4,5},{5,4},{6,7},{7,6},{8,9},{9,8},{10,11... | collective-permute-start | bytes 2703368 | tf_op jit(solution)/shard_map/ppermute | solution.py:78
  104.8 2.1 %copy-start.1 = (bf16[1,2560,320]{1,2,0:T(8,128)(2,1)S(1)}, bf16[1,2560,320]{1,2,0:T(8,128)(2,1)}, u32[]{:S(2)}) copy-start(bf16[1,2560,320]{1,2,0:T(8,128)(2,1)} %param.12) | copy-start | bytes 4915204
  104.8 2.1 %copy-start.2 = (bf16[2,320,176]{2,1,0:T(8,128)(2,1)S(1)}, bf16[2,320,176]{2,1,0:T(8,128)(2,1)}, u32[]{:S(2)}) copy-start(bf16[2,320,176]{2,1,0:T(8,128)(2,1)} %get-tuple-element.317) | copy-start | bytes 675844
  104.8 2.1 %copy-start.3 = (bf16[2,320,176]{2,1,0:T(8,128)(2,1)S(1)}, bf16[2,320,176]{2,1,0:T(8,128)(2,1)}, u32[]{:S(2)}) copy-start(bf16[2,320,176]{2,1,0:T(8,128)(2,1)} %get-tuple-element.318) | copy-start | bytes 675844
  104.8 2.2 %copy-start.4 = (bf16[2,320,176]{2,1,0:T(8,128)(2,1)S(1)}, bf16[2,320,176]{2,1,0:T(8,128)(2,1)}, u32[]{:S(2)}) copy-start(bf16[2,320,176]{2,1,0:T(8,128)(2,1)} %get-tuple-element.319) | copy-start | bytes 675844
  110.2 37.7 %collective-permute-start.15 = (bf16[320,512]{1,0:T(8,128)(2,1)S(1)}, bf16[320,512]{1,0:T(8,128)(2,1)S(1)}, u32[]{:S(2)}, u32[]{:S(2)}) collective-permute-start(bf16[320,512]{1,0:T(8,128)(2,1)S(1)} %get-tuple-element.259), channel_id=1, source_target_pairs={{448,0},{456,8},{464,16},{472,24},{480,32},{488,40},{496,48},{504,... | collective-permute-start | bytes 983048 | tf_op jit(solution)/shard_map/cond/branch_3_fun/ppermute | solution.py:177
  117.4 33.5 %collective-permute-start.18 = (bf16[320,512]{1,0:T(8,128)(2,1)S(1)}, bf16[320,512]{1,0:T(8,128)(2,1)S(1)}, u32[]{:S(2)}, u32[]{:S(2)}) collective-permute-start(bf16[320,512]{1,0:T(8,128)(2,1)S(1)} %get-tuple-element.262), channel_id=1, source_target_pairs={{448,0},{456,8},{464,16},{472,24},{480,32},{488,40},{496,48},{504,... | collective-permute-start | bytes 983048 | tf_op jit(solution)/shard_map/cond/branch_3_fun/ppermute | solution.py:177
  126.3 68.3 %collective-permute-start.19 = (f32[1]{0:T(128)}, f32[1]{0:T(128)}, u32[]{:S(2)}, u32[]{:S(2)}) collective-permute-start(f32[1]{0:T(128)} %get-tuple-element.263), channel_id=1, source_target_pairs={{448,0},{456,8},{464,16},{472,24},{480,32},{488,40},{496,48},{504,... | collective-permute-start | bytes 20 | tf_op jit(solution)/shard_map/cond/branch_3_fun/ppermute | solution.py:180
  128.7 42.9 %collective-permute-start.16 = (bf16[320,768]{1,0:T(8,128)(2,1)S(1)}, bf16[320,768]{1,0:T(8,128)(2,1)S(1)}, u32[]{:S(2)}, u32[]{:S(2)}) collective-permute-start(bf16[320,768]{1,0:T(8,128)(2,1)S(1)} %get-tuple-element.260), channel_id=1, source_target_pairs={{448,0},{456,8},{464,16},{472,24},{480,32},{488,40},{496,48},{504,... | collective-permute-start | bytes 1474568 | tf_op jit(solution)/shard_map/cond/branch_3_fun/ppermute | solution.py:177
  143.7 50.6 %collective-permute-start.17 = (bf16[320,768]{1,0:T(8,128)(2,1)S(1)}, bf16[320,768]{1,0:T(8,128)(2,1)S(1)}, u32[]{:S(2)}, u32[]{:S(2)}) collective-permute-start(bf16[320,768]{1,0:T(8,128)(2,1)S(1)} %get-tuple-element.261), channel_id=1, source_target_pairs={{448,0},{456,8},{464,16},{472,24},{480,32},{488,40},{496,48},{504,... | collective-permute-start | bytes 1474568 | tf_op jit(solution)/shard_map/cond/branch_3_fun/ppermute | solution.py:177
  194.6 1.2 copy-start.5

commit v4 on v3

--- a/solution.py
+++ b/solution.py
@@ -14,6 +14,8 @@
 LANES = 128
 CHUNKS = (512, 768, 768, 512)
 VMEM = 12 * 2**20
+EARLY_VMEM = 24 * 2**20
+HIDDEN = pl.CostEstimate(flops=1, bytes_accessed=1, transcendentals=0)
 
 
 def pack_cotangent(cot_t, parts):
@@ -41,31 +43,54 @@
     )(tokens, gain[None])
 
 
-def copy_kernel(array_ref, token_ref, out_ref):
-    out_ref[...] = array_ref[...]
-
-
-def copy_after(array, token):
+def corner(array):
+    return pl.BlockSpec((1,) * (array.ndim - 2) + (16, LANES), lambda i: (0,) * array.ndim)
+
+
+def copy_kernel(array_ref, *refs):
+    refs[-1][...] = array_ref[...]
+
+
+def copy_after(array, token, *scalars):
+    whole = pl.BlockSpec(array.shape, lambda i: (0,) * array.ndim)
     return pl.pallas_call(
         copy_kernel,
         grid=(1,),
-        in_specs=[pl.BlockSpec(array.shape, lambda i: (0, 0)), pl.BlockSpec((1, 16, LANES), lambda i: (0, 0, 0))],
-        out_specs=pl.BlockSpec(array.shape, lambda i: (0, 0)),
+        in_specs=[whole, corner(token)] + [pl.BlockSpec(memory_space=pltpu.SMEM)] * len(scalars),
+        out_specs=whole,
         out_shape=jax.ShapeDtypeStruct(array.shape, array.dtype),
         compiler_params=pltpu.CompilerParams(vmem_limit_bytes=VMEM),
-    )(array, token)
-
-
-def once_there(array, *tokens):
+        cost_estimate=HIDDEN,
+    )(array, token, *scalars)
+
+
+def once_there(array, token):
     whole = pl.BlockSpec(memory_space=pl.ANY)
     return pl.pallas_call(
         lambda *refs: None,
-        in_specs=[whole] + [pl.BlockSpec(memory_space=pltpu.VMEM)] * len(tokens),
+        in_specs=[whole, pl.BlockSpec(memory_space=pltpu.VMEM)],
         out_specs=whole,
         out_shape=jax.ShapeDtypeStruct(array.shape, array.dtype),
         input_output_aliases={0: 0},
         compiler_params=pltpu.CompilerParams(vmem_limit_bytes=VMEM),
-    )(array, *tokens)
+        cost_estimate=HIDDEN,
+    )(array, token)
+
+
+def scalar_kernel(value_ref, token_ref, out_ref):
+    out_ref[0] = value_ref[0]
+
+
+def scalar_after(value, token):
+    smem = pl.BlockSpec(memory_space=pltpu.SMEM)
+    return pl.pallas_call(
+        scalar_kernel,
+        grid=(1,),
+        in_specs=[smem, corner(token)],
+        out_specs=smem,
+        out_shape=jax.ShapeDtypeStruct(value.shape, value.dtype),
+        cost_estimate=HIDDEN,
+    )(value, token)
 
 
 def to_chip(values, step):
@@ -118,50 +143,88 @@
             pltpu.SemaphoreType.DMA((len(blocks),)),
         ],
         compiler_params=pltpu.CompilerParams(vmem_limit_bytes=VMEM),
-        cost_estimate=pl.CostEstimate(flops=0, bytes_accessed=0, transcendentals=0),
+        cost_estimate=HIDDEN,
     )(jnp.stack(sources), weight_t, packed, *blocks)
 
 
-def local_kernel(groups, blocks, first, *refs):
-    grads, blocks, (numer_ref, weight_ref) = refs[:groups], refs[groups : groups + blocks], refs[groups + blocks :][:2]
-    out_ref, weight_out_ref, held, numer, sems = refs[-5:]
-    width, tile = out_ref.shape[1], 256
-    columns = pl.ds(first, width)
-    copies = [pltpu.make_async_copy(block.at[:, columns], held.at[i], sems.at[i]) for i, block in enumerate(blocks)]
-    copies.append(pltpu.make_async_copy(numer_ref.at[:, columns], numer, sems.at[len(blocks)]))
-    for copy in copies:
-        copy.start()
-    weight_out_ref[0] = weight_ref[0]
-    for copy in copies:
-        copy.wait()
+def add_products(totals_ref, width, grads, held, copies):
+    tile, block = 256, 0
     terms = [grad_ref[i] for grad_ref in grads for i in range(grad_ref.shape[0])]
     for at in range(0, width, tile):
         part = slice(at, at + tile)
-        total = jnp.zeros((out_ref.shape[0], tile), jnp.float32)
+        total = jnp.zeros((totals_ref.shape[0], tile), jnp.float32)
         for i, term in enumerate(terms):
+            if at == 0:
+                copies[i].wait()
             total += jnp.dot(term, held[i, :, part], preferred_element_type=jnp.float32)
-        update = (LEARN_RATE * (SCALE * total)).astype(jnp.bfloat16)
-        out_ref[:, part] = (numer[:, part].astype(jnp.float32) - update.astype(jnp.float32)).astype(jnp.bfloat16)
-
-
-def local_chunk(grads, blocks, numer_t, weight, first, width):
-    cols = numer_t.shape[0]
-    tokens = blocks[0].shape[0]
+        totals_ref[:, part] = total
+
+
+def early_kernel(groups, blocks, *refs):
+    grads, blocks, (numer_ref, weight_ref, partner_ref) = refs[:groups], refs[groups : groups + blocks], refs[groups + blocks :][:3]
+    out_ref, token_ref, weight_out_ref, held, sems = refs[-5:]
+    copies = [pltpu.make_async_copy(block, held.at[i], sems.at[i]) for i, block in enumerate(blocks)]
+    for copy in copies:
+        copy.start()
+    weight_out_ref[0] = 0.5 * (weight_ref[0] + partner_ref[0])
+    token_ref[...] = jnp.zeros(token_ref.shape, token_ref.dtype)
+    add_products(out_ref, out_ref.shape[1], grads, held, copies)
+    out_ref[...] = numer_ref[...].astype(jnp.float32) - LEARN_RATE * (SCALE * out_ref[...])
+
+
+def early_blocks(grads, blocks, numer_t, weight, partner_weight):
     vmem, smem = pl.BlockSpec(memory_space=pltpu.VMEM), pl.BlockSpec(memory_space=pltpu.SMEM)
     whole = pl.BlockSpec(memory_space=pl.ANY)
     return pl.pallas_call(
-        partial(local_kernel, len(grads), len(blocks), first),
-        in_specs=[vmem] * len(grads) + [whole] * (len(blocks) + 1) + [smem],
-        out_specs=(vmem, smem),
-        out_shape=(jax.ShapeDtypeStruct((cols, width), jnp.bfloat16), jax.ShapeDtypeStruct((1,), jnp.float32)),
+        partial(early_kernel, len(grads), len(blocks)),
+        in_specs=[vmem] * len(grads) + [whole] * len(blocks) + [vmem, smem, smem],
+        out_specs=(vmem, vmem, smem),
+        out_shape=(
+            jax.ShapeDtypeStruct(numer_t.shape, jnp.float32),
+            jax.ShapeDtypeStruct((8, LANES), jnp.float32),
+            jax.ShapeDtypeStruct((1,), jnp.float32),
+        ),
+        scratch_shapes=[
+            pltpu.VMEM((len(blocks),) + blocks[0].shape, jnp.bfloat16),
+            pltpu.SemaphoreType.DMA((len(blocks),)),
+        ],
+        compiler_params=pltpu.CompilerParams(vmem_limit_bytes=EARLY_VMEM),
+        cost_estimate=HIDDEN,
+    )(*grads, *blocks, numer_t, weight, partner_weight)
+
+
+def late_kernel(groups, blocks, first, *refs):
+    grads, blocks, early_ref = refs[:groups], refs[groups : groups + blocks], refs[groups + blocks]
+    out_ref, held, early, total, sems = refs[-5:]
+    width = out_ref.shape[1]
+    columns = pl.ds(first, width)
+    copies = [pltpu.make_async_copy(block.at[:, columns], held.at[i], sems.at[i]) for i, block in enumerate(blocks)]
+    copies.append(pltpu.make_async_copy(early_ref.at[:, columns], early, sems.at[len(blocks)]))
+    for copy in copies:
+        copy.start()
+    add_products(total, width, grads, held, copies)
+    copies[-1].wait()
+    out_ref[...] = (early[...] - LEARN_RATE * (SCALE * total[...])).astype(jnp.bfloat16)
+
+
+def late_chunk(grads, blocks, early, first, width):
+    cols = early.shape[0]
+    tokens = blocks[0].shape[0]
+    vmem, whole = pl.BlockSpec(memory_space=pltpu.VMEM), pl.BlockSpec(memory_space=pl.ANY)
+    return pl.pallas_call(
+        partial(late_kernel, len(grads), len(blocks), first),
+        in_specs=[vmem] * len(grads) + [whole] * (len(blocks) + 1),
+        out_specs=vmem,
+        out_shape=jax.ShapeDtypeStruct((cols, width), jnp.bfloat16),
         scratch_shapes=[
             pltpu.VMEM((len(blocks), tokens, width), jnp.bfloat16),
-            pltpu.VMEM((cols, width), jnp.bfloat16),
+            pltpu.VMEM((cols, width), jnp.float32),
+            pltpu.VMEM((cols, width), jnp.float32),
             pltpu.SemaphoreType.DMA((len(blocks) + 1,)),
         ],
         compiler_params=pltpu.CompilerParams(vmem_limit_bytes=VMEM),
-        cost_estimate=pl.CostEstimate(flops=0, bytes_accessed=0, transcendentals=0),
-    )(*grads, *blocks, numer_t, weight)
+        cost_estimate=HIDDEN,
+    )(*grads, *blocks, early)
 
 
 def route(distance):
@@ -169,16 +232,23 @@
     return [((i - distance) % len(devices), i) for i in devices]
 
 
-def mix_with(hop_size, grads, blocks, numer_t, weight):
-    pieces, weights, first = [], [], 0
+def mix_with(hop_size, grads, blocks, early):
+    pieces, first = [], 0
     for width in CHUNKS:
-        local, handed_on = local_chunk(grads, blocks, numer_t, weight, first, width)
-        weights.append(handed_on)
+        local = late_chunk(grads, blocks, early, first, width)
         partner = lax.ppermute(local, "rep", route(hop_size))
         pieces.append((0.5 * local.astype(jnp.float32) + 0.5 * partner.astype(jnp.float32)).astype(jnp.bfloat16))
         first += width
-    new_weight = 0.5 * (weight + lax.ppermute(weights[1], "rep", route(hop_size)))
-    return jnp.concatenate(pieces, axis=1), new_weight
+    return jnp.concatenate(pieces, axis=1)
+
+
+def weight_from(hop_size, weight):
+    return lax.ppermute(weight, "rep", route(hop_size))
+
+
+def per_hop(step_index, act, *operands):
+    bit_count = lax.axis_size("rep").bit_length() - 1
+    return lax.switch(step_index % bit_count, [partial(act, 2**bit) for bit in range(bit_count)], *operands)
 
 
 def on_device(numerator, push_weight, norm_gain, activations, cotangent, step_index):
@@ -186,31 +256,27 @@
     me = lax.axis_index("fsdp")
     core = me % 2
     ahead, back, far = ((me + step * (1 - 2 * core) + count) % count for step in (2, -2, 4))
-    packed = pack_cotangent(cotangent.reshape(-1, cotangent.shape[2]).T, count)
-    packed = lax.all_to_all(packed, "fsdp", split_axis=0, concat_axis=0, tiled=True)
+    numer_t = numerator[0].T
+    weight_t = (numer_t.astype(jnp.float32) / push_weight[0]).astype(jnp.bfloat16)
     own = norm(activations.reshape(-1, DW), norm_gain)
     first = to_chip(own, 1)
+    third = to_chip(first, 1)
+    packed = pack_cotangent(cotangent.reshape(-1, cotangent.shape[2]).T, count)
+    partner_weight = per_hop(step_index, weight_from, scalar_after(push_weight, own))
+    packed = copy_after(packed, own, partner_weight)
+    packed = lax.all_to_all(packed, "fsdp", split_axis=0, concat_axis=0, tiled=True)
     second = to_chip(copy_after(own, packed), -1)
-    third = to_chip(first, 1)
-    numer_t = numerator[0].T
-    weight_t = (numer_t.astype(jnp.float32) / push_weight[0]).astype(jnp.bfloat16)
-    held = [((me, me ^ 1), own), ((back, ahead ^ 1), first), ((ahead, back ^ 1), second)]
-    blocks, grads, tokens = [], [], []
-    for sources, block in held:
+    blocks, grads = [], []
+    for sources, block in (((me, me ^ 1), own), ((back, ahead ^ 1), first), ((far, far ^ 1), third)):
         pair = (block, to_core(block))
         blocks += pair
         grad, token = grad_out(weight_t, packed, sources, pair)
         grads.append(grad)
-        tokens.append(token)
-    third = once_there(third, *tokens)
-    for source, block in ((far, third), (far ^ 1, to_core(third))):
-        blocks.append(block)
-        grads.append(grad_out(weight_t, packed, (source,), (block,))[0])
-    bit_count = lax.axis_size("rep").bit_length() - 1
-    branches = [partial(mix_with, 2**bit) for bit in range(bit_count)]
-    mixed_t, new_weight = lax.switch(
-        step_index % bit_count, branches, grads, blocks, numer_t, push_weight
-    )
+    early, token, new_weight = early_blocks(grads, blocks, numer_t, push_weight, partner_weight)
+    second = once_there(second, token)
+    blocks = [second, to_core(second)]
+    grads = [grad_out(weight_t, packed, (s,), (b,))[0] for s, b in zip((ahead, back ^ 1), blocks)]
+    mixed_t = per_hop(step_index, mix_with, grads, blocks, early)
     return mixed_t.T[None], new_weight
 
 

time: 199 us -> 177 us (0.89)
  the two profiles are of different devices: /device:TPU:1 before, /device:TPU:64 now
where the time goes in v4:
time: 177 us; the launch traced here: 176 us
  waiting for transfers between devices  81.4 us (46%)
  starting transfers between devices  48.7 us (28%)
  Pallas kernels  35.7 us (20%)
  local copies, waits for them, and re-layouts  4.61 us (3%)
  other arithmetic  2.87 us (2%)
  between operations  2.25 us (1%)
    all_to_all x1, waiting for transfers between devices, on_device(): lax.all_to_all(packed, 'fsdp', split_axis=0, concat_axis=0, tiled=True)  31.4 us
    ppermute x4, waiting for transfers between devices, mix_with(): partner = lax.ppermute(local, 'rep', route(hop_size))  28 us
    ppermute x3, waiting for transfers between devices, to_chip(): return lax.ppermute(values, 'fsdp', route)  16.6 us
    ppermute x3, starting transfers between devices, to_chip(): return lax.ppermute(values, 'fsdp', route)  15.7 us
    pallas_call x5, Pallas kernels, grad_out(): pl.pallas_call(grad_out_kernel, in_specs=[pl.BlockSpec(memory_space=pltpu...  15.5 us
    ppermute x4, starting transfers between devices, mix_with(): partner = lax.ppermute(local, 'rep', route(hop_size))  11.3 us
    ppermute x4, starting transfers between devices, to_core(): lax.ppermute(values, 'fsdp', [(i, i ^ 1) for i in range(lax.axis_size('fs...  9.22 us
    all_to_all x1, starting transfers between devices, on_device(): lax.all_to_all(packed, 'fsdp', split_axis=0, concat_axis=0, tiled=True)  7.59 us
  transfers between devices with their start and end apart: 13, of which 9 were waited for; matrix products, arithmetic and copies ran while one was open for 2% of the time, Pallas kernels for 18%

profile of v4, /device:TPU:64, one launch (start us, length us, event | category | flops | bytes accessed | tf_op | source)
XLA Modules:
  0.0 175.9 jit_solution(16090753146742206362)
XLA Ops:
  3.9 6.1 %collective-permute-start.32 = (bf16[176,2560]{1,0:T(8,128)(2,1)}, bf16[176,2560]{1,0:T(8,128)(2,1)S(1)}, u32[]{:S(2)}, u32[]{:S(2)}) collective-permute-start(bf16[176,2560]{1,0:T(8,128)(2,1)} %shard_map.77.token_ref.refs_0_.array_ref.refs_3_), channel_id=1, source_target_pairs={{0,2},{1,7},{2,4},{3,1},{4,6},{5,3},{6,0},{7,5},{8,10},{9,15},{10,... | collective-permute-start | bytes 2703368 | tf_op jit(solution)/shard_map/ppermute | solution.py:99
  13.8 10.1 %conditional.2 = (f32[1]{0:T(128)}) conditional(s32[]{:T(128)} %clamp.4, f32[1]{0:T(128)} %shard_map.78, f32[1]{0:T(128)} %shard_map.78, f32[1]{0:T(128)} %shard_map.78, f32[1]{0:T(128)} %shard_map.78, f32[1]{0:T(128)} %shard_map.78, f32[1]{0:T(128)} %shard_map.78), branch_computations={%region_0.1_spmd, %region_1.2_spmd, %region_2.3_spmd, %region_3.4_... | conditional | bytes 64 | solution.py:251
  13.9 4.9 %collective-permute-start.1 = (f32[1]{0:T(128)}, f32[1]{0:T(128)}, u32[]{:S(2)}, u32[]{:S(2)}) collective-permute-start(f32[1]{0:T(128)} %param.1), channel_id=1, source_target_pairs={{496,0},{504,8},{0,16},{8,24},{16,32},{24,40},{32,48},{40,56},{48,... | collective-permute-start | bytes 20 | tf_op jit(solution)/shard_map/cond/branch_1_fun/ppermute | solution.py:246
  18.8 5.1 %collective-permute-done.1 = f32[1]{0:T(128)} collective-permute-done((f32[1]{0:T(128)}, f32[1]{0:T(128)}, u32[]{:S(2)}, u32[]{:S(2)}) %collective-permute-start.1) | collective-permute-done | bytes 36 | tf_op jit(solution)/shard_map/cond/branch_1_fun/ppermute | solution.py:246
  23.9 2.3 %shard_map.79 = bf16[8,480,128]{2,1,0:T(8,128)(2,1)} custom-call(bf16[8,480,128]{2,1,0:T(8,128)(2,1)S(1)} %maximum_maximum_fusion.array_ref, bf16[176,2560]{1,0:T(8,128)(2,1)} %shard_map.77.token_ref.refs_0_.array_ref.refs_3_, f32[1]{0:T(128)} %get-tuple-element.130.refs_1_.refs_11_), custom_call_target="tpu_custom_call" | custom-call | flops 1 | bytes 1 | tf_op jit(solution)/shard_map/pallas_call | solution.py:56
  26.2 7.6 %all-to-all-start = ((bf16[8,480,128]{2,1,0:T(8,128)(2,1)}), bf16[8,480,128]{2,1,0:T(8,128)(2,1)S(1)}, u32[]{:S(2)}, u32[]{:S(2)}) async-start(bf16[8,480,128]{2,1,0:T(8,128)(2,1)} %shard_map.79), calls=%async_computation | async-start | bytes 1966080 | tf_op jit(solution)/shard_map/all_to_all | solution.py:267
  35.0 3.6 %collective-permute-start.34 = (bf16[176,2560]{1,0:T(8,128)(2,1)S(1)}, bf16[176,2560]{1,0:T(8,128)(2,1)}, u32[]{:S(2)}, u32[]{:S(2)}) collective-permute-start(bf16[176,2560]{1,0:T(8,128)(2,1)S(1)} %collective-permute-done.32.refs_0_.refs_5_), channel_id=1, source_target_pairs={{0,2},{1,7},{2,4},{3,1},{4,6},{5,3},{6,0},{7,5},{8,10},{9,15},{10,... | collective-permute-start | bytes 2703368 | tf_op jit(solution)/shard_map/ppermute | solution.py:99
  38.6 3.0 %collective-permute-start.31 = (bf16[176,2560]{1,0:T(8,128)(2,1)}, bf16[176,2560]{1,0:T(8,128)(2,1)}, u32[]{:S(2)}, u32[]{:S(2)}) collective-permute-start(bf16[176,2560]{1,0:T(8,128)(2,1)} %shard_map.77.token_ref.refs_0_.array_ref.refs_3_), channel_id=1, source_target_pairs={{0,1},{1,0},{2,3},{3,2},{4,5},{5,4},{6,7},{7,6},{8,9},{9,8},{10,11... | collective-permute-start | bytes 2703368 | tf_op jit(solution)/shard_map/ppermute | solution.py:103
  43.7 31.4 %all-to-all-done.refs_0_.cot_ref = bf16[8,480,128]{2,1,0:T(8,128)(2,1)S(1)} async-done(((bf16[8,480,128]{2,1,0:T(8,128)(2,1)}), bf16[8,480,128]{2,1,0:T(8,128)(2,1)S(1)}, u32[]{:S(2)}, u32[]{:S(2)}) %all-to-all-start) | async-done | bytes 983072 | tf_op jit(solution)/shard_map/all_to_all | solution.py:267
  75.1 2.1 %shard_map.80 = bf16[176,2560]{1,0:T(8,128)(2,1)} custom-call(bf16[176,2560]{1,0:T(8,128)(2,1)} %shard_map.77.token_ref.refs_0_.array_ref.refs_3_, bf16[8,480,128]{2,1,0:T(8,128)(2,1)S(1)} %all-to-all-done.refs_0_.cot_ref), custom_call_target="tpu_custom_call" | custom-call | flops 1 | bytes 1 | tf_op jit(solution)/shard_map/pallas_call | solution.py:56
  77.2 6.0 %collective-permute-start.30 = (bf16[176,2560]{1,0:T(8,128)(2,1)}, bf16[176,2560]{1,0:T(8,128)(2,1)}, u32[]{:S(2)}, u32[]{:S(2)}) collective-permute-start(bf16[176,2560]{1,0:T(8,128)(2,1)} %shard_map.80), channel_id=1, source_target_pairs={{0,6},{1,3},{2,0},{3,5},{4,2},{5,7},{6,4},{7,1},{8,14},{9,11},{10,... | collective-permute-start | bytes 2703368 | tf_op jit(solution)/shard_map/ppermute | solution.py:99
  83.2 15.4 %collective-permute-done.34.refs_0_.refs_7_ = bf16[176,2560]{1,0:T(8,128)(2,1)} collective-permute-done((bf16[176,2560]{1,0:T(8,128)(2,1)S(1)}, bf16[176,2560]{1,0:T(8,128)(2,1)}, u32[]{:S(2)}, u32[]{:S(2)}) %collective-permute-start.34) | collective-permute-done | bytes 901152 | tf_op jit(solution)/shard_map/ppermute | solution.py:99
  102.4 4.5 %shard_map.81 = (bf16[2,320,176]{2,1,0:T(8,128)(2,1)S(1)}, f32[8,128]{1,0:T(8,128)}) custom-call(s32[2]{0:T(128)S(1)} %pad_add_fusion.ids_ref, bf16[320,2560]{1,0:T(8,128)(2,1)S(1)} %divide_convert_fusion.weight_ref, bf16[8,480,128]{2,1,0:T(8,128)(2,1)S(1)} %all-to-all-done.refs_0_.cot_ref, bf16[176,2560]{1,0:T(8,128)(2,1)} %shard_map.77.token_ref.refs_0_.array_ref.refs_3_, ...), custom_call_target="tpu_custom_call" | custom-call | flops 1 | bytes 1 | tf_op jit(solution)/shard_map/pallas_call | solution.py:133
  106.9 3.6 %shard_map.82 = (bf16[2,320,176]{2,1,0:T(8,128)(2,1)S(1)}, f32[8,128]{1,0:T(8,128)}) custom-call(s32[2]{0:T(128)S(1)} %pad_add_fusion.1.ids_ref, bf16[320,2560]{1,0:T(8,128)(2,1)S(1)} %divide_convert_fusion.weight_ref, bf16[8,480,128]{2,1,0:T(8,128)(2,1)S(1)} %all-to-all-done.refs_0_.cot_ref, bf16[176,2560]{1,0:T(8,128)(2,1)S(1)} %collective-permute-done.32.refs_0_.refs_5_, ...), custom_call_target="tpu_custom_call" | custom-call | flops 1 | bytes 1 | tf_op jit(solution)/shard_map/pallas_call | solution.py:133
  110.5 4.5 %shard_map.83 = (bf16[2,320,176]{2,1,0:T(8,128)(2,1)S(1)}, f32[8,128]{1,0:T(8,128)}) custom-call(s32[2]{0:T(128)S(1)} %pad_add_fusion.2.ids_ref, bf16[320,2560]{1,0:T(8,128)(2,1)S(1)} %divide_convert_fusion.weight_ref, bf16[8,480,128]{2,1,0:T(8,128)(2,1)S(1)} %all-to-all-done.refs_0_.cot_ref, bf16[176,2560]{1,0:T(8,128)(2,1)} %collective-permute-done.34.refs_0_.refs_7_, ...), custom_call_target="tpu_custom_call" | custom-call | flops 1 | bytes 1 | tf_op jit(solution)/shard_map/pallas_call | solution.py:133
  115.0 7.3 %shard_map.84 = (f32[320,2560]{1,0:T(8,128)}, f32[8,128]{1,0:T(8,128)S(1)}, f32[1]{0:T(128)}) custom-call(bf16[2,320,176]{2,1,0:T(8,128)(2,1)S(1)} %get-tuple-element.120.refs_0_, bf16[2,320,176]{2,1,0:T(8,128)(2,1)S(1)} %get-tuple-element.121.refs_1_, bf16[2,320,176]{2,1,0:T(8,128)(2,1)S(1)} %get-tuple-element.122.refs_2_, ...), custom_call_target="tpu_custom_call" | custom-call | flops 1 | bytes 1 | tf_op jit(solution)/shard_map/pallas_call | solution.py:178
  122.4 2.4 %collective-permute-start.36 = (bf16[176,2560]{1,0:T(8,128)(2,1)}, bf16[176,2560]{1,0:T(8,128)(2,1)S(1)}, u32[]{:S(2)}, u32[]{:S(2)}) collective-permute-start(bf16[176,2560]{1,0:T(8,128)(2,1)} %shard_map.85.refs_0_), channel_id=1, source_target_pairs={{0,1},{1,0},{2,3},{3,2},{4,5},{5,4},{6,7},{7,6},{8,9},{9,8},{10,11... | collective-permute-start | bytes 2703368 | tf_op jit(solution)/shard_map/ppermute | solution.py:103
  124.8 2.0 %shard_map.86 = (bf16[1,320,176]{2,1,0:T(8,128)(2,1)S(1)}, f32[8,128]{1,0:T(8,128)}) custom-call(s32[1]{0:T(128)} %bitcast.ids_ref, bf16[320,2560]{1,0:T(8,128)(2,1)S(1)} %divide_convert_fusion.weight_ref, bf16[8,480,128]{2,1,0:T(8,128)(2,1)S(1)} %all-to-all-done.refs_0_.cot_ref, bf16[176,2560]{1,0:T(8,128)(2,1)} %shard_map.85.refs_0_), custom_call_target="tpu_custom_call" | custom-call | flops 1 | bytes 1 | tf_op jit(solution)/shard_map/pallas_call | solution.py:133
  128.7 46.0 %conditional.3 = (bf16[320,2560]{1,0:T(8,128)(2,1)S(1)}) conditional(s32[]{:T(128)} %clamp.4, (bf16[1,320,176]{2,1,0:T(8,128)(2,1)S(1)}, bf16[1,320,176]{2,1,0:T(8,128)(2,1)S(1)}, bf16[176,2560]{1,0:T(8,128)(2,1)}, bf16[176,2560]{1,0:T(8,128)(2,1)S(1)}, f32[320,2560]{1,0:T(8,128)S(1)}) %tuple.59, ...), branch_computations={%region_6.7_spmd, %region_7.8_spmd, %region_8.9_spmd, %region_9.10... | conditional | flops 10649604 | bytes 14745772 | solution.py:251
  130.1 1.9 %collective-permute-start.10 = (bf16[320,512]{1,0:T(8,128)(2,1)S(1)}, bf16[320,512]{1,0:T(8,128)(2,1)S(1)}, u32[]{:S(2)}, u32[]{:S(2)}) collective-permute-start(bf16[320,512]{1,0:T(8,128)(2,1)S(1)} %branch_1_fun.4), channel_id=1, source_target_pairs={{496,0},{504,8},{0,16},{8,24},{16,32},{24,40},{32,48},{40,56},{48,... | collective-permute-start | bytes 983048 | tf_op jit(solution)/shard_map/cond/branch_1_fun/ppermute | solution.py:239
  140.3 5.5 %collective-permute-start.11 = (bf16[320,768]{1,0:T(8,128)(2,1)S(1)}, bf16[320,768]{1,0:T(8,128)(2,1)S(1)}, u32[]{:S(2)}, u32[]{:S(2)}) collective-permute-start(bf16[320,768]{1,0:T(8,128)(2,1)S(1)} %branch_1_fun.5), channel_id=1, source_target_pairs={{496,0},{504,8},{0,16},{8,24},{16,32},{24,40},{32,48},{40,56},{48,... | collective-permute-start | bytes 1474568 | tf_op jit(solution)/shard_map/cond/branch_1_fun/ppermute | solution.py:239
  147.2 6.9 %collective-permute-done.13 = bf16[320,512]{1,0:T(8,128)(2,1)S(1)} collective-permute-done((bf16[320,512]{1,0:T(8,128)(2,1)S(1)}, bf16[320,512]{1,0:T(8,128)(2,1)S(1)}, u32[]{:S(2)}, u32[]{:S(2)}) %collective-permute-start.13) | collective-permute-done | bytes 327712 | tf_op jit(solution)/shard_map/cond/branch_1_fun/ppermute | solution.py:239
  154.2 10.4 %collective-permute-done.12 = bf16[320,768]{1,0:T(8,128)(2,1)S(1)} collective-permute-done((bf16[320,768]{1,0:T(8,128)(2,1)S(1)}, bf16[320,768]{1,0:T(8,128)(2,1)S(1)}, u32[]{:S(2)}, u32[]{:S(2)}) %collective-permute-start.12) | collective-permute-done | bytes 491552 | tf_op jit(solution)/shard_map/cond/branch_1_fun/ppermute | solution.py:239
  164.8 9.4 %collective-permute-done.11 = bf16[320,768]{1,0:T(8,128)(2,1)S(1)} collective-permute-done((bf16[320,768]{1,0:T(8,128)(2,1)S(1)}, bf16[320,768]{1,0:T(8,128)(2,1)S(1)}, u32[]{:S(2)}, u32[]{:S(2)}) %collective-permute-start.11) | collective-permute-done | bytes 491552 | tf_op jit(solution)/shard_map/cond/branch_1_fun/ppermute | solution.py:239
  (45 shorter events, 27.3 us)
Async XLA Ops:
  1.3 1.2 copy-start.1
  2.5 7.5 %copy-start.4 = (bf16[2,88,2560]{2,1,0:T(8,128)(2,1)S(1)}, bf16[2,88,2560]{2,1,0:T(8,128)(2,1)}, u32[]{:S(2)}) copy-start(bf16[2,88,2560]{2,1,0:T(8,128)(2,1)} %param.22) | copy-start | bytes 2703364
  3.9 31.1 %collective-permute-start.32 = (bf16[176,2560]{1,0:T(8,128)(2,1)}, bf16[176,2560]{1,0:T(8,128)(2,1)S(1)}, u32[]{:S(2)}, u32[]{:S(2)}) collective-permute-start(bf16[176,2560]{1,0:T(8,128)(2,1)} %shard_map.77.token_ref.refs_0_.array_ref.refs_3_), channel_id=1, source_target_pairs={{0,2},{1,7},{2,4},{3,1},{4,6},{5,3},{6,0},{7,5},{8,10},{9,15},{10,... | collective-permute-start | bytes 2703368 | tf_op jit(solution)/shard_map/ppermute | solution.py:99
  13.9 10.0 %collective-permute-start.1 = (f32[1]{0:T(128)}, f32[1]{0:T(128)}, u32[]{:S(2)}, u32[]{:S(2)}) collective-permute-start(f32[1]{0:T(128)} %param.1), channel_id=1, source_target_pairs={{496,0},{504,8},{0,16},{8,24},{16,32},{24,40},{32,48},{40,56},{48,... | collective-permute-start | bytes 20 | tf_op jit(solution)/shard_map/cond/branch_1_fun/ppermute | solution.py:246
  26.2 48.9 %all-to-all-start = ((bf16[8,480,128]{2,1,0:T(8,128)(2,1)}), bf16[8,480,128]{2,1,0:T(8,128)(2,1)S(1)}, u32[]{:S(2)}, u32[]{:S(2)}) async-start(bf16[8,480,128]{2,1,0:T(8,128)(2,1)} %shard_map.79), calls=%async_computation | async-start | bytes 1966080 | tf_op jit(solution)/shard_map/all_to_all | solution.py:267
  35.0 63.6 %collective-permute-start.34 = (bf16[176,2560]{1,0:T(8,128)(2,1)S(1)}, bf16[176,2560]{1,0:T(8,128)(2,1)}, u32[]{:S(2)}, u32[]{:S(2)}) collective-permute-start(bf16[176,2560]{1,0:T(8,128)(2,1)S(1)} %collective-permute-done.32.refs_0_.refs_5_), channel_id=1, source_target_pairs={{0,2},{1,7},{2,4},{3,1},{4,6},{5,3},{6,0},{7,5},{8,10},{9,15},{10,... | collective-permute-start | bytes 2703368 | tf_op jit(solution)/shard_map/ppermute | solution.py:99
  38.6 63.8 %collective-permute-start.31 = (bf16[176,2560]{1,0:T(8,128)(2,1)}, bf16[176,2560]{1,0:T(8,128)(2,1)}, u32[]{:S(2)}, u32[]{:S(2)}) collective-permute-start(bf16[176,2560]{1,0:T(8,128)(2,1)} %shard_map.77.token_ref.refs_0_.array_ref.refs_3_), channel_id=1, source_target_pairs={{0,1},{1,0},{2,3},{3,2},{4,5},{5,4},{6,7},{7,6},{8,9},{9,8},{10,11... | collective-permute-start | bytes 2703368 | tf_op jit(solution)/shard_map/ppermute | solution.py:103
  41.8 65.2 %collective-permute-start.33 = (bf16[176,2560]{1,0:T(8,128)(2,1)S(1)}, bf16[176,2560]{1,0:T(8,128)(2,1)}, u32[]{:S(2)}, u32[]{:S(2)}) collective-permute-start(bf16[176,2560]{1,0:T(8,128)(2,1)S(1)} %collective-permute-done.32.refs_0_.refs_5_), channel_id=1, source_target_pairs={{0,1},{1,0},{2,3},{3,2},{4,5},{5,4},{6,7},{7,6},{8,9},{9,8},{10,11... | collective-permute-start | bytes 2703368 | tf_op jit(solution)/shard_map/ppermute | solution.py:103
  77.2 45.2 %collective-permute-start.30 = (bf16[176,2560]{1,0:T(8,128)(2,1)}, bf16[176,2560]{1,0:T(8,128)(2,1)}, u32[]{:S(2)}, u32[]{:S(2)}) collective-permute-start(bf16[176,2560]{1,0:T(8,128)(2,1)} %shard_map.80), channel_id=1, source_target_pairs={{0,6},{1,3},{2,0},{3,5},{4,2},{5,7},{6,4},{7,1},{8,14},{9,11},{10,... | collective-permute-start | bytes 2703368 | tf_op jit(solution)/shard_map/ppermute | solution.py:99
  98.6 11.9 %collective-permute-start.35 = (bf16[176,2560]{1,0:T(8,128)(2,1)}, bf16[176,2560]{1,0:T(8,128)(2,1)}, u32[]{:S(2)}, u32[]{:S(2)}) collective-permute-start(bf16[176,2560]{1,0:T(8,128)(2,1)} %collective-permute-done.34.refs_0_.refs_7_), channel_id=1, source_target_pairs={{0,1},{1,0},{2,3},{3,2},{4,5},{5,4},{6,7},{7,6},{8,9},{9,8},{10,11... | collective-permute-start | bytes 2703368 | tf_op jit(solution)/shard_map/ppermute | solution.py:103
  110.5 4.5 %copy-start = (bf16[1,2560,320]{1,2,0:T(8,128)(2,1)S(1)}, bf16[1,2560,320]{1,2,0:T(8,128)(2,1)}, u32[]{:S(2)}) copy-start(bf16[1,2560,320]{1,2,0:T(8,128)(2,1)} %param.18) | copy-start | bytes 4915204
  122.4 4.7 %collective-permute-start.36 = (bf16[176,2560]{1,0:T(8,128)(2,1)}, bf16[176,2560]{1,0:T(8,128)(2,1)S(1)}, u32[]{:S(2)}, u32[]{:S(2)}) collective-permute-start(bf16[176,2560]{1,0:T(8,128)(2,1)} %shard_map.85.refs_0_), channel_id=1, source_target_pairs={{0,1},{1,0},{2,3},{3,2},{4,5},{5,4},{6,7},{7,6},{8,9},{9,8},{10,11... | collective-permute-start | bytes 2703368 | tf_op jit(solution)/shard_map/ppermute | solution.py:103
  126.8 1.9 %copy-start.2 = (f32[320,2560]{1,0:T(8,128)S(1)}, f32[320,2560]{1,0:T(8,128)}, u32[]{:S(2)}) copy-start(f32[320,2560]{1,0:T(8,128)} %get-tuple-element.126) | copy-start | bytes 9830404
  130.1 17.0 %collective-permute-start.10 = (bf16[320,512]{1,0:T(8,128)(2,1)S(1)}, bf16[320,512]{1,0:T(8,128)(2,1)S(1)}, u32[]{:S(2)}, u32[]{:S(2)}) collective-permute-start(bf16[320,512]{1,0:T(8,128)(2,1)S(1)} %branch_1_fun.4), channel_id=1, source_target_pairs={{496,0},{504,8},{0,16},{8,24},{16,32},{24,40},{32,48},{40,56},{48,... | collective-permute-start | bytes 983048 | tf_op jit(solution)/shard_map/cond/branch_1_fun/ppermute | solution.py:239
  133.4 20.7 %collective-permute-start.13 = (bf16[320,512]{1,0:T(8,128)(2,1)S(1)}, bf16[320,512]{1,0:T(8,128)(2,1)S(1)}, u32[]{:S(2)}, u32[]{:S(2)}) collective-permute-start(bf16[320,512]{1,0:T(8,128)(2,1)S(1)} %branch_1_fun.7), channel_id=1, source_target_pairs={{496,0},{504,8},{0,16},{8,24},{16,32},{24,40},{32,48},{40,56},{48,... | collective-permute-start | bytes 983048 | tf_op jit(solution)/shard_map/cond/branch_1_fun/ppermute | solution.py:239
  136.8 27.8 %collective-permute-start.12 = (bf16[320,768]{1,0:T(8,128)(2,1)S(1)}, bf16[320,768]{1,0:T(8,128)(2,1)S(1)}, u32[]{:S(2)}, u32[]{:S(2)}) collective-permute-start(bf16[320,768]{1,0:T(8,128)(2,1)S(1)} %branch_1_fun.6), channel_id=1, source_target_pairs={{496,0},{504,8},{0,16},{8,24},{16,32},{24,40},{32,48},{40,56},{48,... | collective-permute-start | bytes 1474568 | tf_op jit(solution)/shard_map/cond/branch_1_fun/ppermute | solution.py:239
  140.3 33.9 %collective-permute-start.11 = (bf16[320,768]{1,0:T(8,128)(2,1)S(1)}, bf16[320,768]{1,0:T(8,128)(2,1)S(1)}, u32[]{:S(2)}, u32[]{:S(2)}) collective-permute-start(bf16[320,768]{1,0:T(8,128)(2,1)S(1)} %branch_1_fun.5), channel_id=1, source_target_pairs={{496,0},{504,8},{0,16},{8,24},{16,32},{24,40},{32,48},{40,56},{48,... | collective-permute-start | bytes 1474568 | tf_op jit(solution)/shard_map/cond/branch_1_fun/ppermute | solution.py:239
  174.7 1.2 copy-start.3

commit v5 on v2

v5 whole, which is shorter than its diff:
```python
from functools import partial

import jax
import jax.numpy as jnp
from jax import lax
from jax.experimental import pallas as pl
from jax.experimental.pallas import tpu as pltpu
from jax.sharding import PartitionSpec as P

DW = 2560
LEARN_RATE = 1.5
EPSILON = 1e-05
SCALE = DW ** (-0.5)
LANES = 128
CHUNKS = (512, 768, 768, 512)
VMEM = 12 * 2**20
TILE = 256
HIDDEN = pl.CostEstimate(flops=1, bytes_accessed=1, transcendentals=0)


def pack_cotangent(cot_t, parts):
    cols, tokens = cot_t.shape
    cot_t = cot_t.reshape(parts, cols // parts, tokens)
    half = cols // parts // 2
    rest = cot_t[:, :, LANES:]
    gap = jnp.zeros((parts, half, LANES - 2 * (tokens - LANES)), cot_t.dtype)
    folded = jnp.concatenate([rest[:, :half], rest[:, half:], gap], axis=2)
    return jnp.concatenate([cot_t[:, :, :LANES], folded], axis=1)


def norm_kernel(tokens_ref, gain_ref, out_ref):
    wide = tokens_ref[...].astype(jnp.float32)
    mean_square = jnp.mean(wide * wide, axis=-1, keepdims=True)
    out_ref[...] = (wide * lax.rsqrt(mean_square + EPSILON) * gain_ref[...]).astype(jnp.bfloat16)


def norm(tokens, gain):
    return pl.pallas_call(
        norm_kernel,
        out_shape=jax.ShapeDtypeStruct(tokens.shape, jnp.bfloat16),
        compiler_params=pltpu.CompilerParams(vmem_limit_bytes=VMEM),
        cost_estimate=pl.CostEstimate(flops=8 * tokens.size, bytes_accessed=4 * tokens.size, transcendentals=0),
    )(tokens, gain[None])


def corner(array):
    return pl.BlockSpec((1,) * (array.ndim - 2) + (16, LANES), lambda i: (0,) * array.ndim)


def copy_kernel(array_ref, token_ref, out_ref):
    out_ref[...] = array_ref[...]


def copy_after(array, token):
    whole = pl.BlockSpec(array.shape, lambda i: (0,) * array.ndim)
    return pl.pallas_call(
        copy_kernel,
        grid=(1,),
        in_specs=[whole, corner(token)],
        out_specs=whole,
        out_shape=jax.ShapeDtypeStruct(array.shape, array.dtype),
        compiler_params=pltpu.CompilerParams(vmem_limit_bytes=VMEM),
        cost_estimate=HIDDEN,
    )(array, token)


def once_there(array, *tokens):
    whole = pl.BlockSpec(memory_space=pl.ANY)
    return pl.pallas_call(
        lambda *refs: None,
        in_specs=[whole] + [pl.BlockSpec(memory_space=pltpu.VMEM)] * len(tokens),
        out_specs=whole,
        out_shape=jax.ShapeDtypeStruct(array.shape, array.dtype),
        input_output_aliases={0: 0},
        compiler_params=pltpu.CompilerParams(vmem_limit_bytes=VMEM),
        cost_estimate=HIDDEN,
    )(array, *tokens)


def to_chip(values, step):
    count = lax.axis_size("fsdp")
    route = [(i, (i // 2 + (-step if i % 2 else step)) % (count // 2) * 2 + i % 2) for i in range(count)]
    return lax.ppermute(values, "fsdp", route)


def to_core(values):
    return lax.ppermute(values, "fsdp", [(i, i ^ 1) for i in range(lax.axis_size("fsdp"))])


def grad_out_kernel(ids_ref, weight_ref, cot_ref, *refs):
    blocks, out_ref = refs[:-1], refs[-1]
    _, cols, tokens = out_ref.shape
    half, rest = cols // 2, tokens - LANES
    for i, block in enumerate(blocks):
        pre_act = SCALE * lax.dot_general(
            weight_ref[...], block[...], (((1,), (1,)), ((), ())), preferred_element_type=jnp.float32
        )
        sig = jax.nn.sigmoid(pre_act)
        slope = sig * (1.0 + pre_act * (1.0 - sig))
        cot = cot_ref[ids_ref[i]]
        head = cot[:cols].astype(jnp.float32)
        tail = cot[cols:].astype(jnp.float32)
        out_ref[i, :, :LANES] = (head * slope[:, :LANES]).astype(jnp.bfloat16)
        out_ref[i, :half, LANES:] = (tail[:, :rest] * slope[:half, LANES:]).astype(jnp.bfloat16)
        out_ref[i, half:, LANES:] = (tail[:, rest : 2 * rest] * slope[half:, LANES:]).astype(jnp.bfloat16)


def grad_out(weight_t, packed, sources, blocks):
    cols, tokens = weight_t.shape[0], blocks[0].shape[0]
    vmem = pl.BlockSpec(memory_space=pltpu.VMEM)
    return pl.pallas_call(
        grad_out_kernel,
        in_specs=[pl.BlockSpec(memory_space=pltpu.SMEM)] + [vmem] * (2 + len(blocks)),
        out_specs=vmem,
        out_shape=jax.ShapeDtypeStruct((len(blocks), cols, tokens), jnp.bfloat16),
        compiler_params=pltpu.CompilerParams(vmem_limit_bytes=VMEM),
        cost_estimate=HIDDEN,
    )(jnp.stack(sources), weight_t, packed, *blocks)


def products(grads, blocks, columns):
    terms = [grad_ref[i] for grad_ref in grads for i in range(grad_ref.shape[0])]
    return sum(
        jnp.dot(term, block[:, columns], preferred_element_type=jnp.float32) for term, block in zip(terms, blocks)
    )


def early_kernel(groups, *refs):
    grads, blocks, (numer_ref, out_ref, token_ref) = refs[:groups], refs[groups:-3], refs[-3:]
    token_ref[...] = jnp.zeros(token_ref.shape, token_ref.dtype)
    for at in range(0, out_ref.shape[1], TILE):
        part = slice(at, at + TILE)
        update = LEARN_RATE * (SCALE * products(grads, blocks, part))
        out_ref[:, part] = numer_ref[:, part].astype(jnp.float32) - update


def early_blocks(grads, blocks, numer_t):
    vmem = pl.BlockSpec(memory_space=pltpu.VMEM)
    return pl.pallas_call(
        partial(early_kernel, len(grads)),
        in_specs=[vmem] * (len(grads) + len(blocks) + 1),
        out_specs=(vmem, vmem),
        out_shape=(
            jax.ShapeDtypeStruct(numer_t.shape, jnp.float32),
            jax.ShapeDtypeStruct((8, LANES), jnp.float32),
        ),
        compiler_params=pltpu.CompilerParams(vmem_limit_bytes=VMEM),
        cost_estimate=HIDDEN,
    )(*grads, *blocks, numer_t)


def late_kernel(groups, first, *refs):
    grads, blocks = refs[:groups], refs[groups:-4]
    early_ref, weight_ref, out_ref, weight_out_ref = refs[-4:]
    weight_out_ref[0] = weight_ref[0]
    for at in range(0, out_ref.shape[1], TILE):
        part = slice(first + at, first + at + TILE)
        update = LEARN_RATE * (SCALE * products(grads, blocks, part))
        out_ref[:, at : at + TILE] = (early_ref[:, part] - update).astype(jnp.bfloat16)


def late_chunk(grads, blocks, early, weight, first, width):
    vmem, smem = pl.BlockSpec(memory_space=pltpu.VMEM), pl.BlockSpec(memory_space=pltpu.SMEM)
    return pl.pallas_call(
        partial(late_kernel, len(grads), first),
        in_specs=[vmem] * (len(grads) + len(blocks) + 1) + [smem],
        out_specs=(vmem, smem),
        out_shape=(
            jax.ShapeDtypeStruct((early.shape[0], width), jnp.bfloat16),
            jax.ShapeDtypeStruct(weight.shape, weight.dtype),
        ),
        compiler_params=pltpu.CompilerParams(vmem_limit_bytes=VMEM),
        cost_estimate=HIDDEN,
    )(*grads, *blocks, early, weight)


def route(distance):
    devices = range(lax.axis_size("rep"))
    return [((i - distance) % len(devices), i) for i in devices]


def mix_with(hop_size, grads, blocks, early, weight):
    pieces, weights, first = [], [], 0
    for width in CHUNKS:
        local, handed_on = late_chunk(grads, blocks, early, weight, first, width)
        weights.append(handed_on)
        partner = lax.ppermute(local, "rep", route(hop_size))
        pieces.append((0.5 * local.astype(jnp.float32) + 0.5 * partner.astype(jnp.float32)).astype(jnp.bfloat16))
        first += width
    new_weight = 0.5 * (weight + lax.ppermute(weights[1], "rep", route(hop_size)))
    return jnp.concatenate(pieces, axis=1), new_weight


def per_hop(step_index, act, *operands):
    bit_count = lax.axis_size("rep").bit_length() - 1
    return lax.switch(step_index % bit_count, [partial(act, 2**bit) for bit in range(bit_count)], *operands)


def on_device(numerator, push_weight, norm_gain, activations, cotangent, step_index):
    count = lax.axis_size("fsdp")
    me = lax.axis_index("fsdp")
    core = me % 2
    ahead, back, far = ((me + step * (1 - 2 * core) + count) % count for step in (2, -2, 4))
    numer_t = numerator[0].T
    weight_t = (numer_t.astype(jnp.float32) / push_weight[0]).astype(jnp.bfloat16)
    own = norm(activations.reshape(-1, DW), norm_gain)
    first = to_chip(own, 1)
    third = to_chip(first, 1)
    packed = pack_cotangent(cotangent.reshape(-1, cotangent.shape[2]).T, count)
    packed = lax.all_to_all(packed, "fsdp", split_axis=0, concat_axis=0, tiled=True)
    second = to_chip(copy_after(own, packed), -1)
    blocks, grads = [], []
    for sources, block in (((me, me ^ 1), own), ((back, ahead ^ 1), first), ((ahead, back ^ 1), second)):
        pair = (block, to_core(block))
        blocks += pair
        grads.append(grad_out(weight_t, packed, sources, pair))
    early, token = early_blocks(grads, blocks, numer_t)
    third = once_there(third, token)
    blocks = [third, to_core(third)]
    grads = [grad_out(weight_t, packed, (s,), (b,)) for s, b in zip((far, far ^ 1), blocks)]
    mixed_t, new_weight = per_hop(step_index, mix_with, grads, blocks, early, push_weight)
    return mixed_t.T[None], new_weight


def solution(mesh):
    placed = (
        P("rep", None, "fsdp"),
        P("rep"),
        P(),
        P(None, ("rep", "fsdp"), None),
        P(None, ("rep", "fsdp"), None),
        P(),
    )
    return jax.shard_map(
        on_device,
        mesh=mesh,
        in_specs=placed,
        out_specs=(P("rep", None, "fsdp"), P("rep")),
        check_vma=False,
    )
```

time: 171 us -> 161 us (0.942)
  starting transfers between devices: 80.2 us -> 51.5 us
  waiting for transfers between devices: 51 us -> 68 us
  Pallas kernels: 27.2 us -> 29.9 us
    ppermute x4, starting transfers between devices: 41.9 us -> 11.8 us  [to_core(): lax.ppermute(values, 'fsdp', [(i, i ^ 1) for i in range(lax.axis_size('fs...]
    all_to_all x1, waiting for transfers between devices: 0.01 us -> 14.6 us  [on_device(): lax.all_to_all(packed, 'fsdp', split_axis=0, concat_axis=0, tiled=True)]
    ppermute x4, waiting for transfers between devices: 20 us -> 31.9 us  [mix_with(): partner = lax.ppermute(local, 'rep', route(hop_size))]
    ppermute x3, waiting for transfers between devices: 31 us -> 21.4 us  [to_chip(): return lax.ppermute(values, 'fsdp', route)]
    pallas_call x6 -> x7, Pallas kernels: 12.4 us -> 17.2 us  [the longest x4 10.5 us: late_chunk(): pl.pallas_call(partial(late_kernel, len(grads), first), in_specs=[vmem] *...]
    pallas_call x5, Pallas kernels: 14.3 us -> 12.1 us  [grad_out(): pl.pallas_call(grad_out_kernel, in_specs=[pl.BlockSpec(memory_space=pltpu...]
  transfers between devices with their start and end apart: 13 -> 13, of which waited for: 4 -> 6; matrix products, arithmetic and copies ran while one was open for 2% -> 2% of each run, Pallas kernels for 13% -> 16%
where the time goes in v5:
time: 161 us; the launch traced here: 160 us
  waiting for transfers between devices  68 us (42%)
  starting transfers between devices  51.5 us (32%)
  Pallas kernels  29.9 us (19%)
  between operations  3.99 us (2%)
  other arithmetic  3.81 us (2%)
  local copies, waits for them, and re-layouts  2.49 us (2%)
    ppermute x4, waiting for transfers between devices, mix_with(): partner = lax.ppermute(local, 'rep', route(hop_size))  31.9 us
    ppermute x3, waiting for transfers between devices, to_chip(): return lax.ppermute(values, 'fsdp', route)  21.4 us
    all_to_all x1, waiting for transfers between devices, on_device(): lax.all_to_all(packed, 'fsdp', split_axis=0, concat_axis=0, tiled=True)  14.6 us
    ppermute x3, starting transfers between devices, to_chip(): return lax.ppermute(values, 'fsdp', route)  12.6 us
    ppermute x4, starting transfers between devices, mix_with(): partner = lax.ppermute(local, 'rep', route(hop_size))  12.2 us
    pallas_call x5, Pallas kernels, grad_out(): pl.pallas_call(grad_out_kernel, in_specs=[pl.BlockSpec(memory_space=pltpu...  12.1 us
    ppermute x4, starting transfers between devices, to_core(): lax.ppermute(values, 'fsdp', [(i, i ^ 1) for i in range(lax.axis_size('fs...  11.8 us
    all_to_all x1, starting transfers between devices, on_device(): lax.all_to_all(packed, 'fsdp', split_axis=0, concat_axis=0, tiled=True)  11.8 us
  transfers between devices with their start and end apart: 13, of which 6 were waited for; matrix products, arithmetic and copies ran while one was open for 2% of the time, Pallas kernels for 16%

profile of v5, /device:TPU:1, one launch (start us, length us, event | category | flops | bytes accessed | tf_op | source)
XLA Modules:
  0.0 159.9 jit_solution(2107519832242157152)
XLA Ops:
  3.8 11.8 %all-to-all-start = ((bf16[8,480,128]{2,1,0:T(8,128)(2,1)}), bf16[8,480,128]{2,1,0:T(8,128)(2,1)S(1)}, u32[]{:S(2)}, u32[]{:S(2)}) async-start(bf16[8,480,128]{2,1,0:T(8,128)(2,1)} %maximum_maximum_fusion), calls=%async_computation | async-start | bytes 1966080 | tf_op jit(solution)/shard_map/all_to_all | solution.py:210
  16.1 5.4 %collective-permute-start.30 = (bf16[176,2560]{1,0:T(8,128)(2,1)S(1)}, bf16[176,2560]{1,0:T(8,128)(2,1)}, u32[]{:S(2)}, u32[]{:S(2)}) collective-permute-start(bf16[176,2560]{1,0:T(8,128)(2,1)S(1)} %shard_map.77.refs_0_.array_ref.refs_3_), channel_id=1, source_target_pairs={{0,2},{1,7},{2,4},{3,1},{4,6},{5,3},{6,0},{7,5},{8,10},{9,15},{10,... | collective-permute-start | bytes 2703368 | tf_op jit(solution)/shard_map/ppermute | solution.py:83
  21.6 14.6 %all-to-all-done.cot_ref.token_ref = bf16[8,480,128]{2,1,0:T(8,128)(2,1)S(1)} async-done(((bf16[8,480,128]{2,1,0:T(8,128)(2,1)}), bf16[8,480,128]{2,1,0:T(8,128)(2,1)S(1)}, u32[]{:S(2)}, u32[]{:S(2)}) %all-to-all-start) | async-done | bytes 983072 | tf_op jit(solution)/shard_map/all_to_all | solution.py:210
  36.2 3.6 %collective-permute-start.34 = (bf16[176,2560]{1,0:T(8,128)(2,1)S(1)}, bf16[176,2560]{1,0:T(8,128)(2,1)}, u32[]{:S(2)}, u32[]{:S(2)}) collective-permute-start(bf16[176,2560]{1,0:T(8,128)(2,1)S(1)} %shard_map.80), channel_id=1, source_target_pairs={{0,6},{1,3},{2,0},{3,5},{4,2},{5,7},{6,4},{7,1},{8,14},{9,11},{10,... | collective-permute-start | bytes 2703368 | tf_op jit(solution)/shard_map/ppermute | solution.py:83
  39.8 3.3 %collective-permute-start.32 = (bf16[176,2560]{1,0:T(8,128)(2,1)S(1)}, bf16[176,2560]{1,0:T(8,128)(2,1)}, u32[]{:S(2)}, u32[]{:S(2)}) collective-permute-start(bf16[176,2560]{1,0:T(8,128)(2,1)S(1)} %shard_map.77.refs_0_.array_ref.refs_3_), channel_id=1, source_target_pairs={{0,1},{1,0},{2,3},{3,2},{4,5},{5,4},{6,7},{7,6},{8,9},{9,8},{10,11... | collective-permute-start | bytes 2703368 | tf_op jit(solution)/shard_map/ppermute | solution.py:87
  43.2 21.4 %collective-permute-done.30.refs_0_.refs_5_ = bf16[176,2560]{1,0:T(8,128)(2,1)} collective-permute-done((bf16[176,2560]{1,0:T(8,128)(2,1)S(1)}, bf16[176,2560]{1,0:T(8,128)(2,1)}, u32[]{:S(2)}, u32[]{:S(2)}) %collective-permute-start.30) | collective-permute-done | bytes 901152 | tf_op jit(solution)/shard_map/ppermute | solution.py:83
  66.6 3.5 %collective-permute-start.31 = (bf16[176,2560]{1,0:T(8,128)(2,1)}, bf16[176,2560]{1,0:T(8,128)(2,1)}, u32[]{:S(2)}, u32[]{:S(2)}) collective-permute-start(bf16[176,2560]{1,0:T(8,128)(2,1)} %collective-permute-done.30.refs_0_.refs_5_), channel_id=1, source_target_pairs={{0,2},{1,7},{2,4},{3,1},{4,6},{5,3},{6,0},{7,5},{8,10},{9,15},{10,... | collective-permute-start | bytes 2703368 | tf_op jit(solution)/shard_map/ppermute | solution.py:83
  70.1 4.4 %collective-permute-start.35 = (bf16[176,2560]{1,0:T(8,128)(2,1)}, bf16[176,2560]{1,0:T(8,128)(2,1)}, u32[]{:S(2)}, u32[]{:S(2)}) collective-permute-start(bf16[176,2560]{1,0:T(8,128)(2,1)} %collective-permute-done.34.refs_0_.refs_7_), channel_id=1, source_target_pairs={{0,1},{1,0},{2,3},{3,2},{4,5},{5,4},{6,7},{7,6},{8,9},{9,8},{10,11... | collective-permute-start | bytes 2703368 | tf_op jit(solution)/shard_map/ppermute | solution.py:87
  79.6 2.7 %shard_map.79.refs_1_ = bf16[2,320,176]{2,1,0:T(8,128)(2,1)S(1)} custom-call(s32[2]{0:T(128)S(1)} %pad_add_fusion.1.ids_ref, bf16[320,2560]{1,0:T(8,128)(2,1)S(1)} %divide_convert_fusion.weight_ref, bf16[8,480,128]{2,1,0:T(8,128)(2,1)S(1)} %all-to-all-done.cot_ref.token_ref, bf16[176,2560]{1,0:T(8,128)(2,1)} %collective-permute-done.30.refs_0_.refs_5_, ...), custom_call_target="tpu_custom_call" | custom-call | flops 1 | bytes 1 | tf_op jit(solution)/shard_map/pallas_call | solution.py:111
  82.3 2.9 %shard_map.81.refs_2_ = bf16[2,320,176]{2,1,0:T(8,128)(2,1)S(1)} custom-call(s32[2]{0:T(128)S(1)} %pad_add_fusion.2.ids_ref, bf16[320,2560]{1,0:T(8,128)(2,1)S(1)} %divide_convert_fusion.weight_ref, bf16[8,480,128]{2,1,0:T(8,128)(2,1)S(1)} %all-to-all-done.cot_ref.token_ref, bf16[176,2560]{1,0:T(8,128)(2,1)} %collective-permute-done.34.refs_0_.refs_7_, ...), custom_call_target="tpu_custom_call" | custom-call | flops 1 | bytes 1 | tf_op jit(solution)/shard_map/pallas_call | solution.py:111
  85.2 6.7 %shard_map.82 = (f32[320,2560]{1,0:T(8,128)}, f32[8,128]{1,0:T(8,128)S(1)}) custom-call(bf16[2,320,176]{2,1,0:T(8,128)(2,1)S(1)} %shard_map.78.refs_0_, bf16[2,320,176]{2,1,0:T(8,128)(2,1)S(1)} %shard_map.79.refs_1_, bf16[2,320,176]{2,1,0:T(8,128)(2,1)S(1)} %shard_map.81.refs_2_, bf16[176,2560]{1,0:T(8,128)(2,1)S(1)} %shard_map.77.refs_0_.array_ref.refs_3_, ...), custom_call_target="tpu_custom_call" | custom-call | flops 1 | bytes 1 | tf_op jit(solution)/shard_map/pallas_call | solution.py:139
  98.9 58.6 %conditional.1 = (bf16[320,2560]{1,0:T(8,128)(2,1)S(1)}, f32[1]{0:T(128)}, f32[1]{0:T(128)}, f32[1]{0:T(128)}) conditional(s32[]{:T(128)} %clamp.3, (bf16[1,320,176]{2,1,0:T(8,128)(2,1)S(1)}, bf16[1,320,176]{2,1,0:T(8,128)(2,1)S(1)}, bf16[176,2560]{1,0:T(8,128)(2,1)}, bf16[176,2560]{1,0:T(8,128)(2,1)}, ...), branch_computations={%region_0.1_spmd, %region_1.2_spmd, %region_2.3_spmd, %region_3.4_... | conditional | flops 10649604 | bytes 14745852 | solution.py:196
  98.9 2.6 %branch_0_fun.4 = (bf16[320,512]{1,0:T(8,128)(2,1)S(1)}, f32[1]{0:T(128)}) custom-call(bf16[1,320,176]{2,1,0:T(8,128)(2,1)S(1)} %get-tuple-element.76.refs_0_, bf16[1,320,176]{2,1,0:T(8,128)(2,1)S(1)} %get-tuple-element.77.refs_1_, bf16[176,2560]{1,0:T(8,128)(2,1)} %get-tuple-element.78.refs_2_, bf16[176,2560]{1,0:T(8,128)(2,1)} %get-tuple-element.79.refs_3_, ...), custom_call_target="tpu_custom_call" | custom-call | flops 1 | bytes 1 | tf_op jit(solution)/shard_map/cond/branch_0_fun/pallas_call | solution.py:164
  101.6 3.1 %collective-permute-start = (bf16[320,512]{1,0:T(8,128)(2,1)S(1)}, bf16[320,512]{1,0:T(8,128)(2,1)S(1)}, u32[]{:S(2)}, u32[]{:S(2)}) collective-permute-start(bf16[320,512]{1,0:T(8,128)(2,1)S(1)} %get-tuple-element.82), channel_id=1, source_target_pairs={{504,0},{0,8},{8,16},{16,24},{24,32},{32,40},{40,48},{48,56},{56,6... | collective-permute-start | bytes 983048 | tf_op jit(solution)/shard_map/cond/branch_0_fun/ppermute | solution.py:187
  104.7 2.6 %branch_0_fun.7 = (bf16[320,512]{1,0:T(8,128)(2,1)S(1)}, f32[1]{0:T(128)}) custom-call(bf16[1,320,176]{2,1,0:T(8,128)(2,1)S(1)} %get-tuple-element.76.refs_0_, bf16[1,320,176]{2,1,0:T(8,128)(2,1)S(1)} %get-tuple-element.77.refs_1_, bf16[176,2560]{1,0:T(8,128)(2,1)} %get-tuple-element.78.refs_2_, bf16[176,2560]{1,0:T(8,128)(2,1)} %get-tuple-element.79.refs_3_, ...), custom_call_target="tpu_custom_call" | custom-call | flops 1 | bytes 1 | tf_op jit(solution)/shard_map/cond/branch_0_fun/pallas_call | solution.py:164
  107.3 3.1 %collective-permute-start.3 = (bf16[320,512]{1,0:T(8,128)(2,1)S(1)}, bf16[320,512]{1,0:T(8,128)(2,1)S(1)}, u32[]{:S(2)}, u32[]{:S(2)}) collective-permute-start(bf16[320,512]{1,0:T(8,128)(2,1)S(1)} %get-tuple-element.85), channel_id=1, source_target_pairs={{504,0},{0,8},{8,16},{16,24},{24,32},{32,40},{40,48},{48,56},{56,6... | collective-permute-start | bytes 983048 | tf_op jit(solution)/shard_map/cond/branch_0_fun/ppermute | solution.py:187
  110.5 2.6 %branch_0_fun.6 = (bf16[320,768]{1,0:T(8,128)(2,1)S(1)}, f32[1]{0:T(128)}) custom-call(bf16[1,320,176]{2,1,0:T(8,128)(2,1)S(1)} %get-tuple-element.76.refs_0_, bf16[1,320,176]{2,1,0:T(8,128)(2,1)S(1)} %get-tuple-element.77.refs_1_, bf16[176,2560]{1,0:T(8,128)(2,1)} %get-tuple-element.78.refs_2_, bf16[176,2560]{1,0:T(8,128)(2,1)} %get-tuple-element.79.refs_3_, ...), custom_call_target="tpu_custom_call" | custom-call | flops 1 | bytes 1 | tf_op jit(solution)/shard_map/cond/branch_0_fun/pallas_call | solution.py:164
  113.1 2.8 %collective-permute-start.2 = (bf16[320,768]{1,0:T(8,128)(2,1)S(1)}, bf16[320,768]{1,0:T(8,128)(2,1)S(1)}, u32[]{:S(2)}, u32[]{:S(2)}) collective-permute-start(bf16[320,768]{1,0:T(8,128)(2,1)S(1)} %get-tuple-element.84), channel_id=1, source_target_pairs={{504,0},{0,8},{8,16},{16,24},{24,32},{32,40},{40,48},{48,56},{56,6... | collective-permute-start | bytes 1474568 | tf_op jit(solution)/shard_map/cond/branch_0_fun/ppermute | solution.py:187
  118.5 3.1 %collective-permute-start.1 = (bf16[320,768]{1,0:T(8,128)(2,1)S(1)}, bf16[320,768]{1,0:T(8,128)(2,1)S(1)}, u32[]{:S(2)}, u32[]{:S(2)}) collective-permute-start(bf16[320,768]{1,0:T(8,128)(2,1)S(1)} %get-tuple-element.83), channel_id=1, source_target_pairs={{504,0},{0,8},{8,16},{16,24},{24,32},{32,40},{40,48},{48,56},{56,6... | collective-permute-start | bytes 1474568 | tf_op jit(solution)/shard_map/cond/branch_0_fun/ppermute | solution.py:187
  121.7 3.1 %collective-permute-start.4 = (f32[1]{0:T(128)}, f32[1]{0:T(128)}, u32[]{:S(2)}, u32[]{:S(2)}) collective-permute-start(f32[1]{0:T(128)} %get-tuple-element.86), channel_id=1, source_target_pairs={{504,0},{0,8},{8,16},{16,24},{24,32},{32,40},{40,48},{48,56},{56,6... | collective-permute-start | bytes 20 | tf_op jit(solution)/shard_map/cond/branch_0_fun/ppermute | solution.py:190
  124.8 4.2 %collective-permute-done = bf16[320,512]{1,0:T(8,128)(2,1)S(1)} collective-permute-done((bf16[320,512]{1,0:T(8,128)(2,1)S(1)}, bf16[320,512]{1,0:T(8,128)(2,1)S(1)}, u32[]{:S(2)}, u32[]{:S(2)}) %collective-permute-start) | collective-permute-done | bytes 327712 | tf_op jit(solution)/shard_map/cond/branch_0_fun/ppermute | solution.py:187
  129.1 6.9 %collective-permute-done.3 = bf16[320,512]{1,0:T(8,128)(2,1)S(1)} collective-permute-done((bf16[320,512]{1,0:T(8,128)(2,1)S(1)}, bf16[320,512]{1,0:T(8,128)(2,1)S(1)}, u32[]{:S(2)}, u32[]{:S(2)}) %collective-permute-start.3) | collective-permute-done | bytes 327712 | tf_op jit(solution)/shard_map/cond/branch_0_fun/ppermute | solution.py:187
  136.1 10.4 %collective-permute-done.2 = bf16[320,768]{1,0:T(8,128)(2,1)S(1)} collective-permute-done((bf16[320,768]{1,0:T(8,128)(2,1)S(1)}, bf16[320,768]{1,0:T(8,128)(2,1)S(1)}, u32[]{:S(2)}, u32[]{:S(2)}) %collective-permute-start.2) | collective-permute-done | bytes 491552 | tf_op jit(solution)/shard_map/cond/branch_0_fun/ppermute | solution.py:187
  146.7 10.4 %collective-permute-done.1 = bf16[320,768]{1,0:T(8,128)(2,1)S(1)} collective-permute-done((bf16[320,768]{1,0:T(8,128)(2,1)S(1)}, bf16[320,768]{1,0:T(8,128)(2,1)S(1)}, u32[]{:S(2)}, u32[]{:S(2)}) %collective-permute-start.1) | collective-permute-done | bytes 491552 | tf_op jit(solution)/shard_map/cond/branch_0_fun/ppermute | solution.py:187
  (42 shorter events, 20.1 us)
Async XLA Ops:
  2.5 13.1 %copy-start.4 = (f32[2560]{0:T(1024)S(1)}, f32[2560]{0:T(1024)}, u32[]{:S(2)}) copy-start(f32[2560]{0:T(1024)} %param.14) | copy-start | bytes 30724
  2.5 13.1 %copy-start.1 = (bf16[2,88,2560]{2,1,0:T(8,128)(2,1)S(1)}, bf16[2,88,2560]{2,1,0:T(8,128)(2,1)}, u32[]{:S(2)}) copy-start(bf16[2,88,2560]{2,1,0:T(8,128)(2,1)} %param.15) | copy-start | bytes 2703364
  3.8 32.3 %all-to-all-start = ((bf16[8,480,128]{2,1,0:T(8,128)(2,1)}), bf16[8,480,128]{2,1,0:T(8,128)(2,1)S(1)}, u32[]{:S(2)}, u32[]{:S(2)}) async-start(bf16[8,480,128]{2,1,0:T(8,128)(2,1)} %maximum_maximum_fusion), calls=%async_computation | async-start | bytes 1966080 | tf_op jit(solution)/shard_map/all_to_all | solution.py:210
  16.1 48.5 %collective-permute-start.30 = (bf16[176,2560]{1,0:T(8,128)(2,1)S(1)}, bf16[176,2560]{1,0:T(8,128)(2,1)}, u32[]{:S(2)}, u32[]{:S(2)}) collective-permute-start(bf16[176,2560]{1,0:T(8,128)(2,1)S(1)} %shard_map.77.refs_0_.array_ref.refs_3_), channel_id=1, source_target_pairs={{0,2},{1,7},{2,4},{3,1},{4,6},{5,3},{6,0},{7,5},{8,10},{9,15},{10,... | collective-permute-start | bytes 2703368 | tf_op jit(solution)/shard_map/ppermute | solution.py:83
  36.2 33.9 %collective-permute-start.34 = (bf16[176,2560]{1,0:T(8,128)(2,1)S(1)}, bf16[176,2560]{1,0:T(8,128)(2,1)}, u32[]{:S(2)}, u32[]{:S(2)}) collective-permute-start(bf16[176,2560]{1,0:T(8,128)(2,1)S(1)} %shard_map.80), channel_id=1, source_target_pairs={{0,6},{1,3},{2,0},{3,5},{4,2},{5,7},{6,4},{7,1},{8,14},{9,11},{10,... | collective-permute-start | bytes 2703368 | tf_op jit(solution)/shard_map/ppermute | solution.py:83
  39.8 37.2 %collective-permute-start.32 = (bf16[176,2560]{1,0:T(8,128)(2,1)S(1)}, bf16[176,2560]{1,0:T(8,128)(2,1)}, u32[]{:S(2)}, u32[]{:S(2)}) collective-permute-start(bf16[176,2560]{1,0:T(8,128)(2,1)S(1)} %shard_map.77.refs_0_.array_ref.refs_3_), channel_id=1, source_target_pairs={{0,1},{1,0},{2,3},{3,2},{4,5},{5,4},{6,7},{7,6},{8,9},{9,8},{10,11... | collective-permute-start | bytes 2703368 | tf_op jit(solution)/shard_map/ppermute | solution.py:87
  64.6 14.9 %collective-permute-start.33 = (bf16[176,2560]{1,0:T(8,128)(2,1)}, bf16[176,2560]{1,0:T(8,128)(2,1)}, u32[]{:S(2)}, u32[]{:S(2)}) collective-permute-start(bf16[176,2560]{1,0:T(8,128)(2,1)} %collective-permute-done.30.refs_0_.refs_5_), channel_id=1, source_target_pairs={{0,1},{1,0},{2,3},{3,2},{4,5},{5,4},{6,7},{7,6},{8,9},{9,8},{10,11... | collective-permute-start | bytes 2703368 | tf_op jit(solution)/shard_map/ppermute | solution.py:87
  66.6 25.4 %collective-permute-start.31 = (bf16[176,2560]{1,0:T(8,128)(2,1)}, bf16[176,2560]{1,0:T(8,128)(2,1)}, u32[]{:S(2)}, u32[]{:S(2)}) collective-permute-start(bf16[176,2560]{1,0:T(8,128)(2,1)} %collective-permute-done.30.refs_0_.refs_5_), channel_id=1, source_target_pairs={{0,2},{1,7},{2,4},{3,1},{4,6},{5,3},{6,0},{7,5},{8,10},{9,15},{10,... | collective-permute-start | bytes 2703368 | tf_op jit(solution)/shard_map/ppermute | solution.py:83
  70.1 12.2 %collective-permute-start.35 = (bf16[176,2560]{1,0:T(8,128)(2,1)}, bf16[176,2560]{1,0:T(8,128)(2,1)}, u32[]{:S(2)}, u32[]{:S(2)}) collective-permute-start(bf16[176,2560]{1,0:T(8,128)(2,1)} %collective-permute-done.34.refs_0_.refs_7_), channel_id=1, source_target_pairs={{0,1},{1,0},{2,3},{3,2},{4,5},{5,4},{6,7},{7,6},{8,9},{9,8},{10,11... | collective-permute-start | bytes 2703368 | tf_op jit(solution)/shard_map/ppermute | solution.py:87
  82.3 2.9 %copy-start = (bf16[1,2560,320]{1,2,0:T(8,128)(2,1)S(1)}, bf16[1,2560,320]{1,2,0:T(8,128)(2,1)}, u32[]{:S(2)}) copy-start(bf16[1,2560,320]{1,2,0:T(8,128)(2,1)} %param.12) | copy-start | bytes 4915204
  91.9 4.8 %collective-permute-start.36 = (bf16[176,2560]{1,0:T(8,128)(2,1)}, bf16[176,2560]{1,0:T(8,128)(2,1)}, u32[]{:S(2)}, u32[]{:S(2)}) collective-permute-start(bf16[176,2560]{1,0:T(8,128)(2,1)} %shard_map.83.refs_0_), channel_id=1, source_target_pairs={{0,1},{1,0},{2,3},{3,2},{4,5},{5,4},{6,7},{7,6},{8,9},{9,8},{10,11... | collective-permute-start | bytes 2703368 | tf_op jit(solution)/shard_map/ppermute | solution.py:87
  96.7 2.2 %copy-start.2 = (f32[320,2560]{1,0:T(8,128)S(1)}, f32[320,2560]{1,0:T(8,128)}, u32[]{:S(2)}) copy-start(f32[320,2560]{1,0:T(8,128)} %get-tuple-element.150) | copy-start | bytes 9830404
  101.6 27.4 %collective-permute-start = (bf16[320,512]{1,0:T(8,128)(2,1)S(1)}, bf16[320,512]{1,0:T(8,128)(2,1)S(1)}, u32[]{:S(2)}, u32[]{:S(2)}) collective-permute-start(bf16[320,512]{1,0:T(8,128)(2,1)S(1)} %get-tuple-element.82), channel_id=1, source_target_pairs={{504,0},{0,8},{8,16},{16,24},{24,32},{32,40},{40,48},{48,56},{56,6... | collective-permute-start | bytes 983048 | tf_op jit(solution)/shard_map/cond/branch_0_fun/ppermute | solution.py:187
  107.3 28.7 %collective-permute-start.3 = (bf16[320,512]{1,0:T(8,128)(2,1)S(1)}, bf16[320,512]{1,0:T(8,128)(2,1)S(1)}, u32[]{:S(2)}, u32[]{:S(2)}) collective-permute-start(bf16[320,512]{1,0:T(8,128)(2,1)S(1)} %get-tuple-element.85), channel_id=1, source_target_pairs={{504,0},{0,8},{8,16},{16,24},{24,32},{32,40},{40,48},{48,56},{56,6... | collective-permute-start | bytes 983048 | tf_op jit(solution)/shard_map/cond/branch_0_fun/ppermute | solution.py:187
  113.1 33.5 %collective-permute-start.2 = (bf16[320,768]{1,0:T(8,128)(2,1)S(1)}, bf16[320,768]{1,0:T(8,128)(2,1)S(1)}, u32[]{:S(2)}, u32[]{:S(2)}) collective-permute-start(bf16[320,768]{1,0:T(8,128)(2,1)S(1)} %get-tuple-element.84), channel_id=1, source_target_pairs={{504,0},{0,8},{8,16},{16,24},{24,32},{32,40},{40,48},{48,56},{56,6... | collective-permute-start | bytes 1474568 | tf_op jit(solution)/shard_map/cond/branch_0_fun/ppermute | solution.py:187
  118.5 38.6 %collective-permute-start.1 = (bf16[320,768]{1,0:T(8,128)(2,1)S(1)}, bf16[320,768]{1,0:T(8,128)(2,1)S(1)}, u32[]{:S(2)}, u32[]{:S(2)}) collective-permute-start(bf16[320,768]{1,0:T(8,128)(2,1)S(1)} %get-tuple-element.83), channel_id=1, source_target_pairs={{504,0},{0,8},{8,16},{16,24},{24,32},{32,40},{40,48},{48,56},{56,6... | collective-permute-start | bytes 1474568 | tf_op jit(solution)/shard_map/cond/branch_0_fun/ppermute | solution.py:187
  121.7 35.7 %collective-permute-start.4 = (f32[1]{0:T(128)}, f32[1]{0:T(128)}, u32[]{:S(2)}, u32[]{:S(2)}) collective-permute-start(f32[1]{0:T(128)} %get-tuple-element.86), channel_id=1, source_target_pairs={{504,0},{0,8},{8,16},{16,24},{24,32},{32,40},{40,48},{48,56},{56,6... | collective-permute-start | bytes 20 | tf_op jit(solution)/shard_map/cond/branch_0_fun/ppermute | solution.py:190
  157.6 1.2 copy-start.3

commit v6 on v5

--- a/solution.py
+++ b/solution.py
@@ -15,6 +15,7 @@
 CHUNKS = (512, 768, 768, 512)
 VMEM = 12 * 2**20
 TILE = 256
+COT_ROWS = 48
 HIDDEN = pl.CostEstimate(flops=1, bytes_accessed=1, transcendentals=0)
 
 
@@ -28,40 +29,68 @@
     return jnp.concatenate([cot_t[:, :, :LANES], folded], axis=1)
 
 
-def norm_kernel(tokens_ref, gain_ref, out_ref):
+def prepare_kernel(ids_ref, tokens_ref, gain_ref, packed_ref, *out_refs):
     wide = tokens_ref[...].astype(jnp.float32)
     mean_square = jnp.mean(wide * wide, axis=-1, keepdims=True)
-    out_ref[...] = (wide * lax.rsqrt(mean_square + EPSILON) * gain_ref[...]).astype(jnp.bfloat16)
-
-
-def norm(tokens, gain):
-    return pl.pallas_call(
-        norm_kernel,
-        out_shape=jax.ShapeDtypeStruct(tokens.shape, jnp.bfloat16),
-        compiler_params=pltpu.CompilerParams(vmem_limit_bytes=VMEM),
-        cost_estimate=pl.CostEstimate(flops=8 * tokens.size, bytes_accessed=4 * tokens.size, transcendentals=0),
-    )(tokens, gain[None])
-
-
-def corner(array):
-    return pl.BlockSpec((1,) * (array.ndim - 2) + (16, LANES), lambda i: (0,) * array.ndim)
-
-
-def copy_kernel(array_ref, token_ref, out_ref):
-    out_ref[...] = array_ref[...]
-
-
-def copy_after(array, token):
-    whole = pl.BlockSpec(array.shape, lambda i: (0,) * array.ndim)
-    return pl.pallas_call(
-        copy_kernel,
-        grid=(1,),
-        in_specs=[whole, corner(token)],
-        out_specs=whole,
-        out_shape=jax.ShapeDtypeStruct(array.shape, array.dtype),
-        compiler_params=pltpu.CompilerParams(vmem_limit_bytes=VMEM),
-        cost_estimate=HIDDEN,
-    )(array, token)
+    normed = (wide * lax.rsqrt(mean_square + EPSILON) * gain_ref[...]).astype(jnp.bfloat16)
+    place = 0
+    for out_ref in out_refs:
+        cots = out_ref.shape[0] // COT_ROWS - tokens_ref.shape[0] // COT_ROWS
+        for slot in range(cots):
+            chip = ids_ref[place]
+            place += 1
+            for part in range(packed_ref.shape[1] // COT_ROWS * 2):
+                core, rows = divmod(part, packed_ref.shape[1] // COT_ROWS)
+                out_ref[slot * COT_ROWS : (slot + 1) * COT_ROWS, part * LANES : (part + 1) * LANES] = packed_ref[
+                    2 * chip + core, rows * COT_ROWS : (rows + 1) * COT_ROWS, :
+                ]
+        out_ref[cots * COT_ROWS :, :] = normed
+
+
+def prepare(tokens, gain, packed, chips):
+    vmem = pl.BlockSpec(memory_space=pltpu.VMEM)
+    rows = [tokens.shape[0] + cots * COT_ROWS for cots in (2, 1, 1)]
+    return pl.pallas_call(
+        prepare_kernel,
+        in_specs=[pl.BlockSpec(memory_space=pltpu.SMEM)] + [vmem] * 3,
+        out_specs=[vmem] * 3,
+        out_shape=[jax.ShapeDtypeStruct((r, DW), jnp.bfloat16) for r in rows],
+        compiler_params=pltpu.CompilerParams(vmem_limit_bytes=VMEM),
+        cost_estimate=HIDDEN,
+    )(jnp.stack(chips), tokens, gain[None], packed)
+
+
+def pass_on_kernel(message_ref, on_ref, kept_ref, sems):
+    spare = on_ref.shape[0] - kept_ref.shape[0]
+    tokens = message_ref.at[pl.ds(2 * COT_ROWS, message_ref.shape[0] - 2 * COT_ROWS)]
+    moves = (
+        (message_ref.at[pl.ds(0, COT_ROWS)], on_ref.at[pl.ds(spare, COT_ROWS)]),
+        (tokens, on_ref.at[pl.ds(spare + COT_ROWS, tokens.shape[0])]),
+        (message_ref.at[pl.ds(COT_ROWS, kept_ref.shape[0])], kept_ref),
+    )
+    copies = [pltpu.make_async_copy(*move, sems.at[i]) for i, move in enumerate(moves)]
+    copies.append(pltpu.make_async_copy(message_ref.at[pl.ds(0, spare)], on_ref.at[pl.ds(0, spare)], sems.at[3]))
+    for copy in copies:
+        copy.start()
+    for copy in copies:
+        copy.wait()
+
+
+def pass_on(message, spare=16):
+    rows = message.shape[0] - COT_ROWS
+    whole = pl.BlockSpec(memory_space=pl.ANY)
+    return pl.pallas_call(
+        pass_on_kernel,
+        in_specs=[whole],
+        out_specs=(whole, whole),
+        out_shape=(
+            jax.ShapeDtypeStruct((rows + spare, DW), message.dtype),
+            jax.ShapeDtypeStruct((rows, DW), message.dtype),
+        ),
+        scratch_shapes=[pltpu.SemaphoreType.DMA((4,))],
+        compiler_params=pltpu.CompilerParams(vmem_limit_bytes=VMEM),
+        cost_estimate=HIDDEN,
+    )(message)
 
 
 def once_there(array, *tokens):
@@ -87,17 +116,21 @@
     return lax.ppermute(values, "fsdp", [(i, i ^ 1) for i in range(lax.axis_size("fsdp"))])
 
 
-def grad_out_kernel(ids_ref, weight_ref, cot_ref, *refs):
-    blocks, out_ref = refs[:-1], refs[-1]
+def grad_out_kernel(core_ref, weight_ref, *refs):
+    messages, (out_ref, token_ref) = refs[:-2], refs[-2:]
     _, cols, tokens = out_ref.shape
     half, rest = cols // 2, tokens - LANES
-    for i, block in enumerate(blocks):
+    token_ref[...] = jnp.zeros(token_ref.shape, token_ref.dtype)
+    mine = pl.ds(pl.multiple_of(core_ref[0] * (DW // 2), LANES), DW // 2)
+    for i, message in enumerate(messages):
         pre_act = SCALE * lax.dot_general(
-            weight_ref[...], block[...], (((1,), (1,)), ((), ())), preferred_element_type=jnp.float32
+            weight_ref[...], message[-tokens:, :], (((1,), (1,)), ((), ())), preferred_element_type=jnp.float32
         )
         sig = jax.nn.sigmoid(pre_act)
         slope = sig * (1.0 + pre_act * (1.0 - sig))
-        cot = cot_ref[ids_ref[i]]
+        at = message.shape[0] - tokens - COT_ROWS
+        cot = message[at : at + COT_ROWS, mine]
+        cot = jnp.concatenate([cot[:, at : at + LANES] for at in range(0, DW // 2, LANES)], axis=0)
         head = cot[:cols].astype(jnp.float32)
         tail = cot[cols:].astype(jnp.float32)
         out_ref[i, :, :LANES] = (head * slope[:, :LANES]).astype(jnp.bfloat16)
@@ -105,23 +138,27 @@
         out_ref[i, half:, LANES:] = (tail[:, rest : 2 * rest] * slope[half:, LANES:]).astype(jnp.bfloat16)
 
 
-def grad_out(weight_t, packed, sources, blocks):
-    cols, tokens = weight_t.shape[0], blocks[0].shape[0]
+def grad_out(weight_t, core, tokens, messages):
+    cols = weight_t.shape[0]
     vmem = pl.BlockSpec(memory_space=pltpu.VMEM)
     return pl.pallas_call(
         grad_out_kernel,
-        in_specs=[pl.BlockSpec(memory_space=pltpu.SMEM)] + [vmem] * (2 + len(blocks)),
-        out_specs=vmem,
-        out_shape=jax.ShapeDtypeStruct((len(blocks), cols, tokens), jnp.bfloat16),
-        compiler_params=pltpu.CompilerParams(vmem_limit_bytes=VMEM),
-        cost_estimate=HIDDEN,
-    )(jnp.stack(sources), weight_t, packed, *blocks)
+        in_specs=[pl.BlockSpec(memory_space=pltpu.SMEM)] + [vmem] * (1 + len(messages)),
+        out_specs=(vmem, vmem),
+        out_shape=(
+            jax.ShapeDtypeStruct((len(messages), cols, tokens), jnp.bfloat16),
+            jax.ShapeDtypeStruct((8, LANES), jnp.float32),
+        ),
+        compiler_params=pltpu.CompilerParams(vmem_limit_bytes=VMEM),
+        cost_estimate=HIDDEN,
+    )(core[None], weight_t, *messages)
 
 
 def products(grads, blocks, columns):
     terms = [grad_ref[i] for grad_ref in grads for i in range(grad_ref.shape[0])]
     return sum(
-        jnp.dot(term, block[:, columns], preferred_element_type=jnp.float32) for term, block in zip(terms, blocks)
+        jnp.dot(term, block[-term.shape[1] :, columns], preferred_element_type=jnp.float32)
+        for term, block in zip(terms, blocks)
     )
 
 
@@ -150,25 +187,42 @@
 
 
 def late_kernel(groups, first, *refs):
-    grads, blocks = refs[:groups], refs[groups:-4]
-    early_ref, weight_ref, out_ref, weight_out_ref = refs[-4:]
+    grads, blocks = refs[:groups], refs[groups:-7]
+    early_ref, weight_ref, out_ref, weight_out_ref, held, early, sems = refs[-7:]
+    tokens, width = held.shape[1:]
+    columns = pl.ds(first, width)
+    copies = [
+        pltpu.make_async_copy(block.at[pl.ds(block.shape[0] - tokens, tokens), columns], held.at[i], sems.at[i])
+        for i, block in enumerate(blocks)
+    ]
+    copies.append(pltpu.make_async_copy(early_ref.at[:, columns], early, sems.at[len(blocks)]))
+    for copy in copies:
+        copy.start()
     weight_out_ref[0] = weight_ref[0]
-    for at in range(0, out_ref.shape[1], TILE):
-        part = slice(first + at, first + at + TILE)
-        update = LEARN_RATE * (SCALE * products(grads, blocks, part))
-        out_ref[:, at : at + TILE] = (early_ref[:, part] - update).astype(jnp.bfloat16)
+    for copy in copies:
+        copy.wait()
+    for at in range(0, width, TILE):
+        part = slice(at, at + TILE)
+        update = LEARN_RATE * (SCALE * products(grads, [held.at[i] for i in range(len(blocks))], part))
+        out_ref[:, part] = (early[:, part] - update).astype(jnp.bfloat16)
 
 
 def late_chunk(grads, blocks, early, weight, first, width):
     vmem, smem = pl.BlockSpec(memory_space=pltpu.VMEM), pl.BlockSpec(memory_space=pltpu.SMEM)
+    whole = pl.BlockSpec(memory_space=pl.ANY)
     return pl.pallas_call(
         partial(late_kernel, len(grads), first),
-        in_specs=[vmem] * (len(grads) + len(blocks) + 1) + [smem],
+        in_specs=[vmem] * len(grads) + [whole] * (len(blocks) + 1) + [smem],
         out_specs=(vmem, smem),
         out_shape=(
             jax.ShapeDtypeStruct((early.shape[0], width), jnp.bfloat16),
             jax.ShapeDtypeStruct(weight.shape, weight.dtype),
         ),
+        scratch_shapes=[
+            pltpu.VMEM((len(blocks), grads[0].shape[2], width), jnp.bfloat16),
+            pltpu.VMEM((early.shape[0], width), jnp.float32),
+            pltpu.SemaphoreType.DMA((len(blocks) + 1,)),
+        ],
         compiler_params=pltpu.CompilerParams(vmem_limit_bytes=VMEM),
         cost_estimate=HIDDEN,
     )(*grads, *blocks, early, weight)
@@ -199,25 +253,29 @@
 def on_device(numerator, push_weight, norm_gain, activations, cotangent, step_index):
     count = lax.axis_size("fsdp")
     me = lax.axis_index("fsdp")
-    core = me % 2
-    ahead, back, far = ((me + step * (1 - 2 * core) + count) % count for step in (2, -2, 4))
+    chip, core, chips = me // 2, me % 2, count // 2
+    ahead, back, far = ((chip + step * (1 - 2 * core) + chips) % chips for step in (1, -1, 2))
     numer_t = numerator[0].T
     weight_t = (numer_t.astype(jnp.float32) / push_weight[0]).astype(jnp.bfloat16)
-    own = norm(activations.reshape(-1, DW), norm_gain)
-    first = to_chip(own, 1)
-    third = to_chip(first, 1)
     packed = pack_cotangent(cotangent.reshape(-1, cotangent.shape[2]).T, count)
-    packed = lax.all_to_all(packed, "fsdp", split_axis=0, concat_axis=0, tiled=True)
-    second = to_chip(copy_after(own, packed), -1)
-    blocks, grads = [], []
-    for sources, block in (((me, me ^ 1), own), ((back, ahead ^ 1), first), ((ahead, back ^ 1), second)):
-        pair = (block, to_core(block))
-        blocks += pair
-        grads.append(grad_out(weight_t, packed, sources, pair))
-    early, token = early_blocks(grads, blocks, numer_t)
+    tokens = activations.reshape(-1, DW)
+    to_ahead, to_back, own = prepare(tokens, norm_gain, packed, (far, ahead, back, chip))
+    grad_of = partial(grad_out, weight_t, core, tokens.shape[0])
+    first = to_chip(to_ahead, 1)
+    third, first = pass_on(first)
+    third = to_chip(third, 1)
+    blocks = [own, to_core(own)]
+    grad_own, token = grad_of(blocks)
+    second = to_chip(once_there(to_back, token), -1)
+    grad_first, token = grad_of([first])
+    first = once_there(first, token)
+    received = [to_core(first), second, to_core(second)]
+    grad_received, _ = grad_of(received)
+    blocks += [first] + received
+    early, token = early_blocks([grad_own, grad_first, grad_received], blocks, numer_t)
     third = once_there(third, token)
     blocks = [third, to_core(third)]
-    grads = [grad_out(weight_t, packed, (s,), (b,)) for s, b in zip((far, far ^ 1), blocks)]
+    grads = [grad_of([block])[0] for block in blocks]
     mixed_t, new_weight = per_hop(step_index, mix_with, grads, blocks, early, push_weight)
     return mixed_t.T[None], new_weight
 

time: 161 us -> 165 us (1.025)
  waiting for transfers between devices: 68 us -> 76.8 us
  Pallas kernels: 29.9 us -> 23.3 us
  starting transfers between devices: 51.5 us -> 55.7 us
  other arithmetic: 3.81 us -> 1.3 us
    ppermute x3, waiting for transfers between devices: 21.4 us -> 51.3 us  [to_chip(): return lax.ppermute(values, 'fsdp', route)]
    all_to_all x1 -> x0, waiting for transfers between devices: 14.6 us -> none  [on_device(): lax.all_to_all(packed, 'fsdp', split_axis=0, concat_axis=0, tiled=True)]
    ppermute x4, starting transfers between devices: 11.8 us -> 25.3 us  [to_core(): lax.ppermute(values, 'fsdp', [(i, i ^ 1) for i in range(lax.axis_size('fs...]
    all_to_all x1 -> x0, starting transfers between devices: 11.8 us -> none  [on_device(): lax.all_to_all(packed, 'fsdp', split_axis=0, concat_axis=0, tiled=True)]
    ppermute x4, waiting for transfers between devices: 31.9 us -> 22.3 us  [mix_with(): partner = lax.ppermute(local, 'rep', route(hop_size))]
    pallas_call x5, Pallas kernels: 12.1 us -> 8.08 us  [grad_out(): pl.pallas_call(grad_out_kernel, in_specs=[pl.BlockSpec(memory_space=pltpu...]
    ppermute x4, waiting for transfers between devices: 0.01 us -> 3.16 us  [to_core(): lax.ppermute(values, 'fsdp', [(i, i ^ 1) for i in range(lax.axis_size('fs...]
    pallas_call x1, Pallas kernels: 6.7 us -> 4.4 us  [early_blocks(): pl.pallas_call(partial(early_kernel, len(grads)), in_specs=[vmem] * (len(...]
  transfers between devices with their start and end apart: 13 -> 12, of which waited for: 6 -> 8; matrix products, arithmetic and copies ran while one was open for 2% -> 1% of each run, Pallas kernels for 16% -> 11%
where the time goes in v6:
time: 165 us
  waiting for transfers between devices  76.8 us (47%)
  starting transfers between devices  55.7 us (34%)
  Pallas kernels  23.3 us (14%)
  between operations  4.03 us (2%)
  local copies, waits for them, and re-layouts  3.41 us (2%)
    ppermute x3, waiting for transfers between devices, to_chip(): return lax.ppermute(values, 'fsdp', route)  51.3 us
    ppermute x4, starting transfers between devices, to_core(): lax.ppermute(values, 'fsdp', [(i, i ^ 1) for i in range(lax.axis_size('fs...  25.3 us
    ppermute x4, waiting for transfers between devices, mix_with(): partner = lax.ppermute(local, 'rep', route(hop_size))  22.3 us
    ppermute x4, starting transfers between devices, mix_with(): partner = lax.ppermute(local, 'rep', route(hop_size))  13.7 us
    ppermute x3, starting transfers between devices, to_chip(): return lax.ppermute(values, 'fsdp', route)  11.9 us
    pallas_call x4, Pallas kernels, late_chunk(): pl.pallas_call(partial(late_kernel, len(grads), first), in_specs=[vmem] *...  8.65 us
    pallas_call x5, Pallas kernels, grad_out(): pl.pallas_call(grad_out_kernel, in_specs=[pl.BlockSpec(memory_space=pltpu...  8.08 us
    ppermute x1, starting transfers between devices, mix_with(): lax.ppermute(weights[1], 'rep', route(hop_size))  4.68 us
  transfers between devices with their start and end apart: 12, of which 8 were waited for; matrix products, arithmetic and copies ran while one was open for 1% of the time, Pallas kernels for 11%

profile of v6, /device:TPU:1, one launch (start us, length us, event | category | flops | bytes accessed | tf_op | source)
XLA Modules:
  0.0 164.7 jit_solution(11875001599277039237)
XLA Ops:
  5.4 8.8 %collective-permute-start.32 = (bf16[224,2560]{1,0:T(8,128)(2,1)S(1)}, bf16[224,2560]{1,0:T(8,128)(2,1)S(1)}, u32[]{:S(2)}, u32[]{:S(2)}) collective-permute-start(bf16[224,2560]{1,0:T(8,128)(2,1)S(1)} %get-tuple-element.163.refs_0_.refs_3_), channel_id=1, source_target_pairs={{0,1},{1,0},{2,3},{3,2},{4,5},{5,4},{6,7},{7,6},{8,9},{9,8},{10,11... | collective-permute-start | bytes 3440648 | tf_op jit(solution)/shard_map/ppermute | solution.py:116
  14.2 5.3 %collective-permute-start.30 = (bf16[272,2560]{1,0:T(8,128)(2,1)S(1)}, bf16[272,2560]{1,0:T(8,128)(2,1)S(1)}, u32[]{:S(2)}, u32[]{:S(2)}) collective-permute-start(bf16[272,2560]{1,0:T(8,128)(2,1)S(1)} %get-tuple-element.161), channel_id=1, source_target_pairs={{0,2},{1,7},{2,4},{3,1},{4,6},{5,3},{6,0},{7,5},{8,10},{9,15},{10,... | collective-permute-start | bytes 4177928 | tf_op jit(solution)/shard_map/ppermute | solution.py:112
  21.7 1.9 %collective-permute-start.34 = (bf16[224,2560]{1,0:T(8,128)(2,1)S(1)}, bf16[224,2560]{1,0:T(8,128)(2,1)S(1)}, u32[]{:S(2)}, u32[]{:S(2)}) collective-permute-start(bf16[224,2560]{1,0:T(8,128)(2,1)S(1)} %shard_map.82), channel_id=1, source_target_pairs={{0,6},{1,3},{2,0},{3,5},{4,2},{5,7},{6,4},{7,1},{8,14},{9,11},{10,... | collective-permute-start | bytes 3440648 | tf_op jit(solution)/shard_map/ppermute | solution.py:112
  23.7 48.8 %collective-permute-done.30.message_ref = bf16[272,2560]{1,0:T(8,128)(2,1)S(1)} collective-permute-done((bf16[272,2560]{1,0:T(8,128)(2,1)S(1)}, bf16[272,2560]{1,0:T(8,128)(2,1)S(1)}, u32[]{:S(2)}, u32[]{:S(2)}) %collective-permute-start.30) | collective-permute-done | bytes 1392672 | tf_op jit(solution)/shard_map/ppermute | solution.py:112
  73.3 4.7 %collective-permute-start.31 = (bf16[240,2560]{1,0:T(8,128)(2,1)S(1)}, bf16[240,2560]{1,0:T(8,128)(2,1)S(1)}, u32[]{:S(2)}, u32[]{:S(2)}) collective-permute-start(bf16[240,2560]{1,0:T(8,128)(2,1)S(1)} %get-tuple-element.162), channel_id=1, source_target_pairs={{0,2},{1,7},{2,4},{3,1},{4,6},{5,3},{6,0},{7,5},{8,10},{9,15},{10,... | collective-permute-start | bytes 3686408 | tf_op jit(solution)/shard_map/ppermute | solution.py:112
  80.8 2.4 %collective-permute-start.35 = (bf16[224,2560]{1,0:T(8,128)(2,1)S(1)}, bf16[224,2560]{1,0:T(8,128)(2,1)S(1)}, u32[]{:S(2)}, u32[]{:S(2)}) collective-permute-start(bf16[224,2560]{1,0:T(8,128)(2,1)S(1)} %collective-permute-done.34.refs_1_.refs_7_), channel_id=1, source_target_pairs={{0,1},{1,0},{2,3},{3,2},{4,5},{5,4},{6,7},{7,6},{8,9},{9,8},{10,11... | collective-permute-start | bytes 3440648 | tf_op jit(solution)/shard_map/ppermute | solution.py:116
  83.6 2.1 %collective-permute-done.35.refs_2_.refs_8_ = bf16[224,2560]{1,0:T(8,128)(2,1)S(1)} collective-permute-done((bf16[224,2560]{1,0:T(8,128)(2,1)S(1)}, bf16[224,2560]{1,0:T(8,128)(2,1)S(1)}, u32[]{:S(2)}, u32[]{:S(2)}) %collective-permute-start.35) | collective-permute-done | bytes 1146912 | tf_op jit(solution)/shard_map/ppermute | solution.py:116
  85.6 2.3 %shard_map.83 = (bf16[3,320,176]{2,1,0:T(8,128)(2,1)S(1)}, f32[8,128]{1,0:T(8,128)}) custom-call(s32[1]{0:T(128)} %bitcast.core_ref, bf16[320,2560]{1,0:T(8,128)(2,1)S(1)} %divide_convert_fusion.weight_ref, bf16[224,2560]{1,0:T(8,128)(2,1)S(1)} %collective-permute-done.33.refs_0_.refs_6_, bf16[224,2560]{1,0:T(8,128)(2,1)S(1)} %collective-permute-done.34.refs_1_.refs_7_, ...), custom_call_target="tpu_custom_call" | custom-call | flops 1 | bytes 1 | tf_op jit(solution)/shard_map/pallas_call | solution.py:144
  87.9 4.4 %shard_map.84 = (f32[320,2560]{1,0:T(8,128)}, f32[8,128]{1,0:T(8,128)S(1)}) custom-call(bf16[2,320,176]{2,1,0:T(8,128)(2,1)S(1)} %get-tuple-element.164.refs_0_, bf16[1,320,176]{2,1,0:T(8,128)(2,1)S(1)} %get-tuple-element.166.refs_1_, bf16[3,320,176]{2,1,0:T(8,128)(2,1)S(1)} %get-tuple-element.170.refs_2_, ...), custom_call_target="tpu_custom_call" | custom-call | flops 1 | bytes 1 | tf_op jit(solution)/shard_map/pallas_call | solution.py:176
  92.3 2.5 %collective-permute-done.31.refs_0_ = bf16[240,2560]{1,0:T(8,128)(2,1)S(1)} collective-permute-done((bf16[240,2560]{1,0:T(8,128)(2,1)S(1)}, bf16[240,2560]{1,0:T(8,128)(2,1)S(1)}, u32[]{:S(2)}, u32[]{:S(2)}) %collective-permute-start.31) | collective-permute-done | bytes 1228832 | tf_op jit(solution)/shard_map/ppermute | solution.py:112
  94.8 12.2 %collective-permute-start.36 = (bf16[240,2560]{1,0:T(8,128)(2,1)S(1)}, bf16[240,2560]{1,0:T(8,128)(2,1)}, u32[]{:S(2)}, u32[]{:S(2)}) collective-permute-start(bf16[240,2560]{1,0:T(8,128)(2,1)S(1)} %shard_map.85.refs_0_), channel_id=1, source_target_pairs={{0,1},{1,0},{2,3},{3,2},{4,5},{5,4},{6,7},{7,6},{8,9},{9,8},{10,11... | collective-permute-start | bytes 3686408 | tf_op jit(solution)/shard_map/ppermute | solution.py:116
  109.7 2.5 %shard_map.87 = (bf16[1,320,176]{2,1,0:T(8,128)(2,1)S(1)}, f32[8,128]{1,0:T(8,128)}) custom-call(s32[1]{0:T(128)} %bitcast.core_ref, bf16[320,2560]{1,0:T(8,128)(2,1)S(1)} %divide_convert_fusion.weight_ref, bf16[240,2560]{1,0:T(8,128)(2,1)} %collective-permute-done.36.refs_0_), custom_call_target="tpu_custom_call" | custom-call | flops 1 | bytes 1 | tf_op jit(solution)/shard_map/pallas_call | solution.py:144
  112.2 50.2 %conditional.1 = (bf16[320,2560]{1,0:T(8,128)(2,1)S(1)}, f32[1]{0:T(128)}, f32[1]{0:T(128)}, f32[1]{0:T(128)}) conditional(s32[]{:T(128)} %clamp.3, (bf16[1,320,176]{2,1,0:T(8,128)(2,1)S(1)}, bf16[1,320,176]{2,1,0:T(8,128)(2,1)S(1)}, bf16[240,2560]{1,0:T(8,128)(2,1)S(1)}, bf16[240,2560]{1,0:T(8,128)(2,1)}, ...), branch_computations={%region_0.1_spmd, %region_1.2_spmd, %region_2.3_spmd, %region_3.4_... | conditional | flops 10649604 | bytes 14745852 | solution.py:250
  112.2 2.1 %branch_1_fun.4 = (bf16[320,512]{1,0:T(8,128)(2,1)S(1)}, f32[1]{0:T(128)}) custom-call(bf16[1,320,176]{2,1,0:T(8,128)(2,1)S(1)} %get-tuple-element.87.refs_0_, bf16[1,320,176]{2,1,0:T(8,128)(2,1)S(1)} %get-tuple-element.88.refs_1_, bf16[240,2560]{1,0:T(8,128)(2,1)S(1)} %get-tuple-element.89.refs_2_, bf16[240,2560]{1,0:T(8,128)(2,1)} %get-tuple-element.90.refs_3_, ...), custom_call_target="tpu_custom_call" | custom-call | flops 1 | bytes 1 | tf_op jit(solution)/shard_map/cond/branch_1_fun/pallas_call | solution.py:213
  114.3 2.8 %collective-permute-start.5 = (bf16[320,512]{1,0:T(8,128)(2,1)S(1)}, bf16[320,512]{1,0:T(8,128)(2,1)S(1)}, u32[]{:S(2)}, u32[]{:S(2)}) collective-permute-start(bf16[320,512]{1,0:T(8,128)(2,1)S(1)} %get-tuple-element.93), channel_id=1, source_target_pairs={{496,0},{504,8},{0,16},{8,24},{16,32},{24,40},{32,48},{40,56},{48,... | collective-permute-start | bytes 983048 | tf_op jit(solution)/shard_map/cond/branch_1_fun/ppermute | solution.py:241
  117.1 2.1 %branch_1_fun.7 = (bf16[320,512]{1,0:T(8,128)(2,1)S(1)}, f32[1]{0:T(128)}) custom-call(bf16[1,320,176]{2,1,0:T(8,128)(2,1)S(1)} %get-tuple-element.87.refs_0_, bf16[1,320,176]{2,1,0:T(8,128)(2,1)S(1)} %get-tuple-element.88.refs_1_, bf16[240,2560]{1,0:T(8,128)(2,1)S(1)} %get-tuple-element.89.refs_2_, bf16[240,2560]{1,0:T(8,128)(2,1)} %get-tuple-element.90.refs_3_, ...), custom_call_target="tpu_custom_call" | custom-call | flops 1 | bytes 1 | tf_op jit(solution)/shard_map/cond/branch_1_fun/pallas_call | solution.py:213
  119.3 3.2 %collective-permute-start.8 = (bf16[320,512]{1,0:T(8,128)(2,1)S(1)}, bf16[320,512]{1,0:T(8,128)(2,1)S(1)}, u32[]{:S(2)}, u32[]{:S(2)}) collective-permute-start(bf16[320,512]{1,0:T(8,128)(2,1)S(1)} %get-tuple-element.96), channel_id=1, source_target_pairs={{496,0},{504,8},{0,16},{8,24},{16,32},{24,40},{32,48},{40,56},{48,... | collective-permute-start | bytes 983048 | tf_op jit(solution)/shard_map/cond/branch_1_fun/ppermute | solution.py:241
  122.5 2.2 %branch_1_fun.6 = (bf16[320,768]{1,0:T(8,128)(2,1)S(1)}, f32[1]{0:T(128)}) custom-call(bf16[1,320,176]{2,1,0:T(8,128)(2,1)S(1)} %get-tuple-element.87.refs_0_, bf16[1,320,176]{2,1,0:T(8,128)(2,1)S(1)} %get-tuple-element.88.refs_1_, bf16[240,2560]{1,0:T(8,128)(2,1)S(1)} %get-tuple-element.89.refs_2_, bf16[240,2560]{1,0:T(8,128)(2,1)} %get-tuple-element.90.refs_3_, ...), custom_call_target="tpu_custom_call" | custom-call | flops 1 | bytes 1 | tf_op jit(solution)/shard_map/cond/branch_1_fun/pallas_call | solution.py:213
  124.6 4.7 %collective-permute-start.7 = (bf16[320,768]{1,0:T(8,128)(2,1)S(1)}, bf16[320,768]{1,0:T(8,128)(2,1)S(1)}, u32[]{:S(2)}, u32[]{:S(2)}) collective-permute-start(bf16[320,768]{1,0:T(8,128)(2,1)S(1)} %get-tuple-element.95), channel_id=1, source_target_pairs={{496,0},{504,8},{0,16},{8,24},{16,32},{24,40},{32,48},{40,56},{48,... | collective-permute-start | bytes 1474568 | tf_op jit(solution)/shard_map/cond/branch_1_fun/ppermute | solution.py:241
  129.3 2.2 %branch_1_fun.5 = (bf16[320,768]{1,0:T(8,128)(2,1)S(1)}, f32[1]{0:T(128)}) custom-call(bf16[1,320,176]{2,1,0:T(8,128)(2,1)S(1)} %get-tuple-element.87.refs_0_, bf16[1,320,176]{2,1,0:T(8,128)(2,1)S(1)} %get-tuple-element.88.refs_1_, bf16[240,2560]{1,0:T(8,128)(2,1)S(1)} %get-tuple-element.89.refs_2_, bf16[240,2560]{1,0:T(8,128)(2,1)} %get-tuple-element.90.refs_3_, ...), custom_call_target="tpu_custom_call" | custom-call | flops 1 | bytes 1 | tf_op jit(solution)/shard_map/cond/branch_1_fun/pallas_call | solution.py:213
  131.5 3.1 %collective-permute-start.6 = (bf16[320,768]{1,0:T(8,128)(2,1)S(1)}, bf16[320,768]{1,0:T(8,128)(2,1)S(1)}, u32[]{:S(2)}, u32[]{:S(2)}) collective-permute-start(bf16[320,768]{1,0:T(8,128)(2,1)S(1)} %get-tuple-element.94), channel_id=1, source_target_pairs={{496,0},{504,8},{0,16},{8,24},{16,32},{24,40},{32,48},{40,56},{48,... | collective-permute-start | bytes 1474568 | tf_op jit(solution)/shard_map/cond/branch_1_fun/ppermute | solution.py:241
  134.6 4.7 %collective-permute-start.9 = (f32[1]{0:T(128)}, f32[1]{0:T(128)}, u32[]{:S(2)}, u32[]{:S(2)}) collective-permute-start(f32[1]{0:T(128)} %get-tuple-element.97), channel_id=1, source_target_pairs={{496,0},{504,8},{0,16},{8,24},{16,32},{24,40},{32,48},{40,56},{48,... | collective-permute-start | bytes 20 | tf_op jit(solution)/shard_map/cond/branch_1_fun/ppermute | solution.py:244
  141.0 10.4 %collective-permute-done.7 = bf16[320,768]{1,0:T(8,128)(2,1)S(1)} collective-permute-done((bf16[320,768]{1,0:T(8,128)(2,1)S(1)}, bf16[320,768]{1,0:T(8,128)(2,1)S(1)}, u32[]{:S(2)}, u32[]{:S(2)}) %collective-permute-start.7) | collective-permute-done | bytes 491552 | tf_op jit(solution)/shard_map/cond/branch_1_fun/ppermute | solution.py:241
  151.6 10.4 %collective-permute-done.6 = bf16[320,768]{1,0:T(8,128)(2,1)S(1)} collective-permute-done((bf16[320,768]{1,0:T(8,128)(2,1)S(1)}, bf16[320,768]{1,0:T(8,128)(2,1)S(1)}, u32[]{:S(2)}, u32[]{:S(2)}) %collective-permute-start.6) | collective-permute-done | bytes 491552 | tf_op jit(solution)/shard_map/cond/branch_1_fun/ppermute | solution.py:241
  (40 shorter events, 14.6 us)
Async XLA Ops:
  2.2 0.7 copy-start.4
  2.9 1.2 copy-start.1
  3.2 17.0 %copy-start = (bf16[1,2560,320]{1,2,0:T(8,128)(2,1)S(1)}, bf16[1,2560,320]{1,2,0:T(8,128)(2,1)}, u32[]{:S(2)}) copy-start(bf16[1,2560,320]{1,2,0:T(8,128)(2,1)} %param.12) | copy-start | bytes 4915204
  5.4 15.0 %collective-permute-start.32 = (bf16[224,2560]{1,0:T(8,128)(2,1)S(1)}, bf16[224,2560]{1,0:T(8,128)(2,1)S(1)}, u32[]{:S(2)}, u32[]{:S(2)}) collective-permute-start(bf16[224,2560]{1,0:T(8,128)(2,1)S(1)} %get-tuple-element.163.refs_0_.refs_3_), channel_id=1, source_target_pairs={{0,1},{1,0},{2,3},{3,2},{4,5},{5,4},{6,7},{7,6},{8,9},{9,8},{10,11... | collective-permute-start | bytes 3440648 | tf_op jit(solution)/shard_map/ppermute | solution.py:116
  14.2 58.3 %collective-permute-start.30 = (bf16[272,2560]{1,0:T(8,128)(2,1)S(1)}, bf16[272,2560]{1,0:T(8,128)(2,1)S(1)}, u32[]{:S(2)}, u32[]{:S(2)}) collective-permute-start(bf16[272,2560]{1,0:T(8,128)(2,1)S(1)} %get-tuple-element.161), channel_id=1, source_target_pairs={{0,2},{1,7},{2,4},{3,1},{4,6},{5,3},{6,0},{7,5},{8,10},{9,15},{10,... | collective-permute-start | bytes 4177928 | tf_op jit(solution)/shard_map/ppermute | solution.py:112
  21.7 59.1 %collective-permute-start.34 = (bf16[224,2560]{1,0:T(8,128)(2,1)S(1)}, bf16[224,2560]{1,0:T(8,128)(2,1)S(1)}, u32[]{:S(2)}, u32[]{:S(2)}) collective-permute-start(bf16[224,2560]{1,0:T(8,128)(2,1)S(1)} %shard_map.82), channel_id=1, source_target_pairs={{0,6},{1,3},{2,0},{3,5},{4,2},{5,7},{6,4},{7,1},{8,14},{9,11},{10,... | collective-permute-start | bytes 3440648 | tf_op jit(solution)/shard_map/ppermute | solution.py:112
  73.3 21.4 %collective-permute-start.31 = (bf16[240,2560]{1,0:T(8,128)(2,1)S(1)}, bf16[240,2560]{1,0:T(8,128)(2,1)S(1)}, u32[]{:S(2)}, u32[]{:S(2)}) collective-permute-start(bf16[240,2560]{1,0:T(8,128)(2,1)S(1)} %get-tuple-element.162), channel_id=1, source_target_pairs={{0,2},{1,7},{2,4},{3,1},{4,6},{5,3},{6,0},{7,5},{8,10},{9,15},{10,... | collective-permute-start | bytes 3686408 | tf_op jit(solution)/shard_map/ppermute | solution.py:112
  78.9 4.7 %collective-permute-start.33 = (bf16[224,2560]{1,0:T(8,128)(2,1)S(1)}, bf16[224,2560]{1,0:T(8,128)(2,1)S(1)}, u32[]{:S(2)}, u32[]{:S(2)}) collective-permute-start(bf16[224,2560]{1,0:T(8,128)(2,1)S(1)} %shard_map.81.refs_5_), channel_id=1, source_target_pairs={{0,1},{1,0},{2,3},{3,2},{4,5},{5,4},{6,7},{7,6},{8,9},{9,8},{10,11... | collective-permute-start | bytes 3440648 | tf_op jit(solution)/shard_map/ppermute | solution.py:116
  80.8 4.8 %collective-permute-start.35 = (bf16[224,2560]{1,0:T(8,128)(2,1)S(1)}, bf16[224,2560]{1,0:T(8,128)(2,1)S(1)}, u32[]{:S(2)}, u32[]{:S(2)}) collective-permute-start(bf16[224,2560]{1,0:T(8,128)(2,1)S(1)} %collective-permute-done.34.refs_1_.refs_7_), channel_id=1, source_target_pairs={{0,1},{1,0},{2,3},{3,2},{4,5},{5,4},{6,7},{7,6},{8,9},{9,8},{10,11... | collective-permute-start | bytes 3440648 | tf_op jit(solution)/shard_map/ppermute | solution.py:116
  94.8 14.9 %collective-permute-start.36 = (bf16[240,2560]{1,0:T(8,128)(2,1)S(1)}, bf16[240,2560]{1,0:T(8,128)(2,1)}, u32[]{:S(2)}, u32[]{:S(2)}) collective-permute-start(bf16[240,2560]{1,0:T(8,128)(2,1)S(1)} %shard_map.85.refs_0_), channel_id=1, source_target_pairs={{0,1},{1,0},{2,3},{3,2},{4,5},{5,4},{6,7},{7,6},{8,9},{9,8},{10,11... | collective-permute-start | bytes 3686408 | tf_op jit(solution)/shard_map/ppermute | solution.py:116
  107.7 4.5 %copy-start.2 = (f32[320,2560]{1,0:T(8,128)S(1)}, f32[320,2560]{1,0:T(8,128)}, u32[]{:S(2)}) copy-start(f32[320,2560]{1,0:T(8,128)} %get-tuple-element.174) | copy-start | bytes 9830404
  114.3 25.0 %collective-permute-start.5 = (bf16[320,512]{1,0:T(8,128)(2,1)S(1)}, bf16[320,512]{1,0:T(8,128)(2,1)S(1)}, u32[]{:S(2)}, u32[]{:S(2)}) collective-permute-start(bf16[320,512]{1,0:T(8,128)(2,1)S(1)} %get-tuple-element.93), channel_id=1, source_target_pairs={{496,0},{504,8},{0,16},{8,24},{16,32},{24,40},{32,48},{40,56},{48,... | collective-permute-start | bytes 983048 | tf_op jit(solution)/shard_map/cond/branch_1_fun/ppermute | solution.py:241
  119.3 21.6 %collective-permute-start.8 = (bf16[320,512]{1,0:T(8,128)(2,1)S(1)}, bf16[320,512]{1,0:T(8,128)(2,1)S(1)}, u32[]{:S(2)}, u32[]{:S(2)}) collective-permute-start(bf16[320,512]{1,0:T(8,128)(2,1)S(1)} %get-tuple-element.96), channel_id=1, source_target_pairs={{496,0},{504,8},{0,16},{8,24},{16,32},{24,40},{32,48},{40,56},{48,... | collective-permute-start | bytes 983048 | tf_op jit(solution)/shard_map/cond/branch_1_fun/ppermute | solution.py:241
  124.6 26.8 %collective-permute-start.7 = (bf16[320,768]{1,0:T(8,128)(2,1)S(1)}, bf16[320,768]{1,0:T(8,128)(2,1)S(1)}, u32[]{:S(2)}, u32[]{:S(2)}) collective-permute-start(bf16[320,768]{1,0:T(8,128)(2,1)S(1)} %get-tuple-element.95), channel_id=1, source_target_pairs={{496,0},{504,8},{0,16},{8,24},{16,32},{24,40},{32,48},{40,56},{48,... | collective-permute-start | bytes 1474568 | tf_op jit(solution)/shard_map/cond/branch_1_fun/ppermute | solution.py:241
  131.5 30.4 %collective-permute-start.6 = (bf16[320,768]{1,0:T(8,128)(2,1)S(1)}, bf16[320,768]{1,0:T(8,128)(2,1)S(1)}, u32[]{:S(2)}, u32[]{:S(2)}) collective-permute-start(bf16[320,768]{1,0:T(8,128)(2,1)S(1)} %get-tuple-element.94), channel_id=1, source_target_pairs={{496,0},{504,8},{0,16},{8,24},{16,32},{24,40},{32,48},{40,56},{48,... | collective-permute-start | bytes 1474568 | tf_op jit(solution)/shard_map/cond/branch_1_fun/ppermute | solution.py:241
  134.6 27.6 %collective-permute-start.9 = (f32[1]{0:T(128)}, f32[1]{0:T(128)}, u32[]{:S(2)}, u32[]{:S(2)}) collective-permute-start(f32[1]{0:T(128)} %get-tuple-element.97), channel_id=1, source_target_pairs={{496,0},{504,8},{0,16},{8,24},{16,32},{24,40},{32,48},{40,56},{48,... | collective-permute-start | bytes 20 | tf_op jit(solution)/shard_map/cond/branch_1_fun/ppermute | solution.py:244
  162.4 1.2 copy-start.3

commit v7 on v6

--- a/solution.py
+++ b/solution.py
@@ -33,77 +33,66 @@
     wide = tokens_ref[...].astype(jnp.float32)
     mean_square = jnp.mean(wide * wide, axis=-1, keepdims=True)
     normed = (wide * lax.rsqrt(mean_square + EPSILON) * gain_ref[...]).astype(jnp.bfloat16)
-    place = 0
+    for place in range(ids_ref.shape[0]):
+        out_ref, chip = out_refs[place], ids_ref[place]
+        pieces = packed_ref.shape[1] // COT_ROWS
+        for part in range(2 * pieces):
+            core, rows = divmod(part, pieces)
+            out_ref[:COT_ROWS, part * LANES : (part + 1) * LANES] = packed_ref[
+                2 * chip + core, rows * COT_ROWS : (rows + 1) * COT_ROWS, :
+            ]
     for out_ref in out_refs:
-        cots = out_ref.shape[0] // COT_ROWS - tokens_ref.shape[0] // COT_ROWS
-        for slot in range(cots):
-            chip = ids_ref[place]
-            place += 1
-            for part in range(packed_ref.shape[1] // COT_ROWS * 2):
-                core, rows = divmod(part, packed_ref.shape[1] // COT_ROWS)
-                out_ref[slot * COT_ROWS : (slot + 1) * COT_ROWS, part * LANES : (part + 1) * LANES] = packed_ref[
-                    2 * chip + core, rows * COT_ROWS : (rows + 1) * COT_ROWS, :
-                ]
-        out_ref[cots * COT_ROWS :, :] = normed
+        if out_ref.shape[0] > COT_ROWS:
+            out_ref[-normed.shape[0] :, :] = normed
 
 
 def prepare(tokens, gain, packed, chips):
     vmem = pl.BlockSpec(memory_space=pltpu.VMEM)
-    rows = [tokens.shape[0] + cots * COT_ROWS for cots in (2, 1, 1)]
+    count = tokens.shape[0]
+    rows = (COT_ROWS + count, COT_ROWS + count, COT_ROWS, COT_ROWS, count)
     return pl.pallas_call(
         prepare_kernel,
         in_specs=[pl.BlockSpec(memory_space=pltpu.SMEM)] + [vmem] * 3,
-        out_specs=[vmem] * 3,
+        out_specs=[vmem] * len(rows),
         out_shape=[jax.ShapeDtypeStruct((r, DW), jnp.bfloat16) for r in rows],
         compiler_params=pltpu.CompilerParams(vmem_limit_bytes=VMEM),
         cost_estimate=HIDDEN,
     )(jnp.stack(chips), tokens, gain[None], packed)
 
 
-def pass_on_kernel(message_ref, on_ref, kept_ref, sems):
-    spare = on_ref.shape[0] - kept_ref.shape[0]
-    tokens = message_ref.at[pl.ds(2 * COT_ROWS, message_ref.shape[0] - 2 * COT_ROWS)]
-    moves = (
-        (message_ref.at[pl.ds(0, COT_ROWS)], on_ref.at[pl.ds(spare, COT_ROWS)]),
-        (tokens, on_ref.at[pl.ds(spare + COT_ROWS, tokens.shape[0])]),
-        (message_ref.at[pl.ds(COT_ROWS, kept_ref.shape[0])], kept_ref),
-    )
-    copies = [pltpu.make_async_copy(*move, sems.at[i]) for i, move in enumerate(moves)]
-    copies.append(pltpu.make_async_copy(message_ref.at[pl.ds(0, spare)], on_ref.at[pl.ds(0, spare)], sems.at[3]))
-    for copy in copies:
-        copy.start()
-    for copy in copies:
-        copy.wait()
-
-
-def pass_on(message, spare=16):
-    rows = message.shape[0] - COT_ROWS
+def once_there(array, token):
     whole = pl.BlockSpec(memory_space=pl.ANY)
-    return pl.pallas_call(
-        pass_on_kernel,
-        in_specs=[whole],
-        out_specs=(whole, whole),
-        out_shape=(
-            jax.ShapeDtypeStruct((rows + spare, DW), message.dtype),
-            jax.ShapeDtypeStruct((rows, DW), message.dtype),
-        ),
-        scratch_shapes=[pltpu.SemaphoreType.DMA((4,))],
-        compiler_params=pltpu.CompilerParams(vmem_limit_bytes=VMEM),
-        cost_estimate=HIDDEN,
-    )(message)
-
-
-def once_there(array, *tokens):
-    whole = pl.BlockSpec(memory_space=pl.ANY)
+    corner = (1,) * (token.ndim - 2) + (min(16, token.shape[-2]), LANES)
     return pl.pallas_call(
         lambda *refs: None,
-        in_specs=[whole] + [pl.BlockSpec(memory_space=pltpu.VMEM)] * len(tokens),
+        grid=(1,),
+        in_specs=[whole, pl.BlockSpec(corner, lambda i: (0,) * token.ndim)],
         out_specs=whole,
         out_shape=jax.ShapeDtypeStruct(array.shape, array.dtype),
         input_output_aliases={0: 0},
         compiler_params=pltpu.CompilerParams(vmem_limit_bytes=VMEM),
         cost_estimate=HIDDEN,
-    )(array, *tokens)
+    )(array, token)
+
+
+def tail_kernel(array_ref, token_ref, out_ref, sem):
+    rows = out_ref.shape[0]
+    copy = pltpu.make_async_copy(array_ref.at[pl.ds(array_ref.shape[0] - rows, rows)], out_ref, sem)
+    copy.start()
+    copy.wait()
+
+
+def tail_after(array, rows, token):
+    whole = pl.BlockSpec(memory_space=pl.ANY)
+    return pl.pallas_call(
+        tail_kernel,
+        in_specs=[whole, pl.BlockSpec(memory_space=pltpu.VMEM)],
+        out_specs=whole,
+        out_shape=jax.ShapeDtypeStruct((rows, array.shape[1]), array.dtype),
+        scratch_shapes=[pltpu.SemaphoreType.DMA],
+        compiler_params=pltpu.CompilerParams(vmem_limit_bytes=VMEM),
+        cost_estimate=HIDDEN,
+    )(array, token)
 
 
 def to_chip(values, step):
@@ -116,21 +105,20 @@
     return lax.ppermute(values, "fsdp", [(i, i ^ 1) for i in range(lax.axis_size("fsdp"))])
 
 
-def grad_out_kernel(core_ref, weight_ref, *refs):
-    messages, (out_ref, token_ref) = refs[:-2], refs[-2:]
+def grad_out_kernel(plan, core_ref, weight_ref, *refs):
+    arrays, (out_ref, token_ref) = refs[:-2], refs[-2:]
     _, cols, tokens = out_ref.shape
     half, rest = cols // 2, tokens - LANES
     token_ref[...] = jnp.zeros(token_ref.shape, token_ref.dtype)
     mine = pl.ds(pl.multiple_of(core_ref[0] * (DW // 2), LANES), DW // 2)
-    for i, message in enumerate(messages):
+    for i, (message, columns, at) in enumerate(plan):
         pre_act = SCALE * lax.dot_general(
-            weight_ref[...], message[-tokens:, :], (((1,), (1,)), ((), ())), preferred_element_type=jnp.float32
+            weight_ref[...], arrays[message][-tokens:, :], (((1,), (1,)), ((), ())), preferred_element_type=jnp.float32
         )
         sig = jax.nn.sigmoid(pre_act)
         slope = sig * (1.0 + pre_act * (1.0 - sig))
-        at = message.shape[0] - tokens - COT_ROWS
-        cot = message[at : at + COT_ROWS, mine]
-        cot = jnp.concatenate([cot[:, at : at + LANES] for at in range(0, DW // 2, LANES)], axis=0)
+        cot = arrays[columns][at : at + COT_ROWS, mine]
+        cot = jnp.concatenate([cot[:, lane : lane + LANES] for lane in range(0, DW // 2, LANES)], axis=0)
         head = cot[:cols].astype(jnp.float32)
         tail = cot[cols:].astype(jnp.float32)
         out_ref[i, :, :LANES] = (head * slope[:, :LANES]).astype(jnp.bfloat16)
@@ -138,20 +126,27 @@
         out_ref[i, half:, LANES:] = (tail[:, rest : 2 * rest] * slope[half:, LANES:]).astype(jnp.bfloat16)
 
 
-def grad_out(weight_t, core, tokens, messages):
+def grad_out(weight_t, core, tokens, pairs):
     cols = weight_t.shape[0]
+    arrays, plan = [], []
+    for message, columns, at in pairs:
+        for array in (message, columns):
+            if not any(array is other for other in arrays):
+                arrays.append(array)
+        place = [next(i for i, other in enumerate(arrays) if other is array) for array in (message, columns)]
+        plan.append((*place, at))
     vmem = pl.BlockSpec(memory_space=pltpu.VMEM)
     return pl.pallas_call(
-        grad_out_kernel,
-        in_specs=[pl.BlockSpec(memory_space=pltpu.SMEM)] + [vmem] * (1 + len(messages)),
+        partial(grad_out_kernel, plan),
+        in_specs=[pl.BlockSpec(memory_space=pltpu.SMEM)] + [vmem] * (1 + len(arrays)),
         out_specs=(vmem, vmem),
         out_shape=(
-            jax.ShapeDtypeStruct((len(messages), cols, tokens), jnp.bfloat16),
+            jax.ShapeDtypeStruct((len(pairs), cols, tokens), jnp.bfloat16),
             jax.ShapeDtypeStruct((8, LANES), jnp.float32),
         ),
         compiler_params=pltpu.CompilerParams(vmem_limit_bytes=VMEM),
         cost_estimate=HIDDEN,
-    )(core[None], weight_t, *messages)
+    )(core[None], weight_t, *arrays)
 
 
 def products(grads, blocks, columns):
@@ -259,23 +254,26 @@
     weight_t = (numer_t.astype(jnp.float32) / push_weight[0]).astype(jnp.bfloat16)
     packed = pack_cotangent(cotangent.reshape(-1, cotangent.shape[2]).T, count)
     tokens = activations.reshape(-1, DW)
-    to_ahead, to_back, own = prepare(tokens, norm_gain, packed, (far, ahead, back, chip))
+    own, to_far, cot_ahead, cot_back, plain = prepare(tokens, norm_gain, packed, (chip, far, ahead, back))
     grad_of = partial(grad_out, weight_t, core, tokens.shape[0])
-    first = to_chip(to_ahead, 1)
-    third, first = pass_on(first)
-    third = to_chip(third, 1)
-    blocks = [own, to_core(own)]
-    grad_own, token = grad_of(blocks)
-    second = to_chip(once_there(to_back, token), -1)
-    grad_first, token = grad_of([first])
-    first = once_there(first, token)
-    received = [to_core(first), second, to_core(second)]
-    grad_received, _ = grad_of(received)
-    blocks += [first] + received
+    first = to_chip(to_far, 1)
+    third = to_chip(first, 1)
+    cot_ahead = to_chip(cot_ahead, 1)
+    cot_back = to_chip(cot_back, -1)
+    cots = jnp.concatenate([cot_ahead, cot_back])
+    twin_cots = to_core(cots)
+    twin = to_core(own)
+    grad_own, _ = grad_of([(own, own, 0), (twin, twin, 0)])
+    second = to_chip(once_there(plain, twin_cots), -1)
+    grad_first, token = grad_of([(first, cot_ahead, 0)])
+    first = tail_after(first, tokens.shape[0], token)
+    twin_first, twin_second = to_core(first), to_core(second)
+    grad_received, _ = grad_of([(twin_first, twin_cots, 0), (second, cots, COT_ROWS), (twin_second, twin_cots, COT_ROWS)])
+    blocks = [own, twin, first, twin_first, second, twin_second]
     early, token = early_blocks([grad_own, grad_first, grad_received], blocks, numer_t)
     third = once_there(third, token)
     blocks = [third, to_core(third)]
-    grads = [grad_of([block])[0] for block in blocks]
+    grads = [grad_of([(block, block, 0)])[0] for block in blocks]
     mixed_t, new_weight = per_hop(step_index, mix_with, grads, blocks, early, push_weight)
     return mixed_t.T[None], new_weight
 

time: 165 us -> 159 us (0.964)
  waiting for transfers between devices: 76.8 us -> 38.9 us
  starting transfers between devices: 55.7 us -> 87.8 us
    ppermute x3 -> x5, waiting for transfers between devices: 51.3 us -> 16.2 us  [to_chip(): return lax.ppermute(values, 'fsdp', route)]
    ppermute x4 -> x5, starting transfers between devices: 25.3 us -> 42.5 us  [to_core(): lax.ppermute(values, 'fsdp', [(i, i ^ 1) for i in range(lax.axis_size('fs...]
    ppermute x3 -> x5, starting transfers between devices: 11.9 us -> 28.4 us  [to_chip(): return lax.ppermute(values, 'fsdp', route)]
    ppermute x4, waiting for transfers between devices: 22.3 us -> 19.6 us  [mix_with(): partner = lax.ppermute(local, 'rep', route(hop_size))]
    pallas_call x9 -> x8, Pallas kernels: 8.91 us -> 8.72 us  [the longest x5 8.51 us: grad_out(): pl.pallas_call(partial(grad_out_kernel, plan), in_specs=[pl.BlockSpec(mem...]
  transfers between devices with their start and end apart: 12 -> 15, of which waited for: 8 -> 8; matrix products, arithmetic and copies ran while one was open for 1% -> 1% of each run, Pallas kernels for 11% -> 11%
where the time goes in v7:
time: 159 us; the launch traced here: 158 us
  starting transfers between devices  87.8 us (55%)
  waiting for transfers between devices  38.9 us (24%)
  Pallas kernels  23.1 us (15%)
  between operations  4.03 us (3%)
  local copies, waits for them, and re-layouts  2.9 us (2%)
    ppermute x5, starting transfers between devices, to_core(): lax.ppermute(values, 'fsdp', [(i, i ^ 1) for i in range(lax.axis_size('fs...  42.5 us
    ppermute x5, starting transfers between devices, to_chip(): return lax.ppermute(values, 'fsdp', route)  28.4 us
    ppermute x4, waiting for transfers between devices, mix_with(): partner = lax.ppermute(local, 'rep', route(hop_size))  19.6 us
    ppermute x5, waiting for transfers between devices, to_chip(): return lax.ppermute(values, 'fsdp', route)  16.2 us
    ppermute x4, starting transfers between devices, mix_with(): partner = lax.ppermute(local, 'rep', route(hop_size))  12.2 us
    pallas_call x4, Pallas kernels, late_chunk(): pl.pallas_call(partial(late_kernel, len(grads), first), in_specs=[vmem] *...  8.65 us
    pallas_call x5, Pallas kernels, grad_out(): pl.pallas_call(partial(grad_out_kernel, plan), in_specs=[pl.BlockSpec(mem...  8.51 us
    ppermute x1, starting transfers between devices, mix_with(): lax.ppermute(weights[1], 'rep', route(hop_size))  4.65 us
  transfers between devices with their start and end apart: 15, of which 8 were waited for; matrix products, arithmetic and copies ran while one was open for 1% of the time, Pallas kernels for 11%

profile of v7, /device:TPU:1, one launch (start us, length us, event | category | flops | bytes accessed | tf_op | source)
XLA Modules:
  0.0 158.2 jit_solution(3737123788088428208)
XLA Ops:
  4.8 11.6 %collective-permute-start.33 = (bf16[48,2560]{1,0:T(8,128)(2,1)S(1)}, bf16[48,2560]{1,0:T(8,128)(2,1)S(1)}, u32[]{:S(2)}, u32[]{:S(2)}) collective-permute-start(bf16[48,2560]{1,0:T(8,128)(2,1)S(1)} %get-tuple-element.163), channel_id=1, source_target_pairs={{0,2},{1,7},{2,4},{3,1},{4,6},{5,3},{6,0},{7,5},{8,10},{9,15},{10,... | collective-permute-start | bytes 737288 | tf_op jit(solution)/shard_map/ppermute | solution.py:101
  16.5 1.9 %collective-permute-start.35 = (bf16[48,2560]{1,0:T(8,128)(2,1)S(1)}, bf16[48,2560]{1,0:T(8,128)(2,1)S(1)}, u32[]{:S(2)}, u32[]{:S(2)}) collective-permute-start(bf16[48,2560]{1,0:T(8,128)(2,1)S(1)} %get-tuple-element.166), channel_id=1, source_target_pairs={{0,6},{1,3},{2,0},{3,5},{4,2},{5,7},{6,4},{7,1},{8,14},{9,11},{10,... | collective-permute-start | bytes 737288 | tf_op jit(solution)/shard_map/ppermute | solution.py:101
  18.4 5.5 %collective-permute-start.30 = (bf16[224,2560]{1,0:T(8,128)(2,1)S(1)}, bf16[224,2560]{1,0:T(8,128)(2,1)S(1)}, u32[]{:S(2)}, u32[]{:S(2)}) collective-permute-start(bf16[224,2560]{1,0:T(8,128)(2,1)S(1)} %get-tuple-element.160), channel_id=1, source_target_pairs={{0,2},{1,7},{2,4},{3,1},{4,6},{5,3},{6,0},{7,5},{8,10},{9,15},{10,... | collective-permute-start | bytes 3440648 | tf_op jit(solution)/shard_map/ppermute | solution.py:101
  24.9 6.6 %collective-permute-done.35 = bf16[48,2560]{1,0:T(8,128)(2,1)S(1)} collective-permute-done((bf16[48,2560]{1,0:T(8,128)(2,1)S(1)}, bf16[48,2560]{1,0:T(8,128)(2,1)S(1)}, u32[]{:S(2)}, u32[]{:S(2)}) %collective-permute-start.35) | collective-permute-done | bytes 245792 | tf_op jit(solution)/shard_map/ppermute | solution.py:101
  35.3 3.1 %collective-permute-start.37 = (bf16[176,2560]{1,0:T(8,128)(2,1)S(1)}, bf16[176,2560]{1,0:T(8,128)(2,1)S(1)}, u32[]{:S(2)}, u32[]{:S(2)}) collective-permute-start(bf16[176,2560]{1,0:T(8,128)(2,1)S(1)} %shard_map.81), channel_id=1, source_target_pairs={{0,6},{1,3},{2,0},{3,5},{4,2},{5,7},{6,4},{7,1},{8,14},{9,11},{10,... | collective-permute-start | bytes 2703368 | tf_op jit(solution)/shard_map/ppermute | solution.py:101
  38.4 5.5 %collective-permute-start.32 = (bf16[224,2560]{1,0:T(8,128)(2,1)S(1)}, bf16[224,2560]{1,0:T(8,128)(2,1)S(1)}, u32[]{:S(2)}, u32[]{:S(2)}) collective-permute-start(bf16[224,2560]{1,0:T(8,128)(2,1)S(1)} %get-tuple-element.161.refs_0_.refs_3_), channel_id=1, source_target_pairs={{0,1},{1,0},{2,3},{3,2},{4,5},{5,4},{6,7},{7,6},{8,9},{9,8},{10,11... | collective-permute-start | bytes 3440648 | tf_op jit(solution)/shard_map/ppermute | solution.py:105
  44.5 8.5 %collective-permute-done.30.refs_0_.array_ref = bf16[224,2560]{1,0:T(8,128)(2,1)S(1)} collective-permute-done((bf16[224,2560]{1,0:T(8,128)(2,1)S(1)}, bf16[224,2560]{1,0:T(8,128)(2,1)S(1)}, u32[]{:S(2)}, u32[]{:S(2)}) %collective-permute-start.30) | collective-permute-done | bytes 1146912 | tf_op jit(solution)/shard_map/ppermute | solution.py:101
  53.0 6.3 %collective-permute-start.31 = (bf16[224,2560]{1,0:T(8,128)(2,1)S(1)}, bf16[224,2560]{1,0:T(8,128)(2,1)S(1)}, u32[]{:S(2)}, u32[]{:S(2)}) collective-permute-start(bf16[224,2560]{1,0:T(8,128)(2,1)S(1)} %collective-permute-done.30.refs_0_.array_ref), channel_id=1, source_target_pairs={{0,2},{1,7},{2,4},{3,1},{4,6},{5,3},{6,0},{7,5},{8,10},{9,15},{10,... | collective-permute-start | bytes 3440648 | tf_op jit(solution)/shard_map/ppermute | solution.py:101
  60.6 27.9 %collective-permute-start.34 = (bf16[176,2560]{1,0:T(8,128)(2,1)S(1)}, bf16[176,2560]{1,0:T(8,128)(2,1)S(1)}, u32[]{:S(2)}, u32[]{:S(2)}) collective-permute-start(bf16[176,2560]{1,0:T(8,128)(2,1)S(1)} %shard_map.80.refs_5_), channel_id=1, source_target_pairs={{0,1},{1,0},{2,3},{3,2},{4,5},{5,4},{6,7},{7,6},{8,9},{9,8},{10,11... | collective-permute-start | bytes 2703368 | tf_op jit(solution)/shard_map/ppermute | solution.py:105
  92.9 2.2 %shard_map.82 = (bf16[3,320,176]{2,1,0:T(8,128)(2,1)S(1)}, f32[8,128]{1,0:T(8,128)}) custom-call(s32[1]{0:T(128)} %bitcast.core_ref, bf16[320,2560]{1,0:T(8,128)(2,1)S(1)} %divide_convert_fusion.weight_ref, bf16[176,2560]{1,0:T(8,128)(2,1)S(1)} %collective-permute-done.34.refs_0_.refs_6_, bf16[96,2560]{1,0:T(8,128)(2,1)S(1)} %collective-permute-done.36.refs_1_, ...), custom_call_target="tpu_custom_call" | custom-call | flops 1 | bytes 1 | tf_op jit(solution)/shard_map/pallas_call | solution.py:139
  95.1 4.4 %shard_map.83 = (f32[320,2560]{1,0:T(8,128)}, f32[8,128]{1,0:T(8,128)S(1)}) custom-call(bf16[2,320,176]{2,1,0:T(8,128)(2,1)S(1)} %get-tuple-element.162.refs_0_, bf16[1,320,176]{2,1,0:T(8,128)(2,1)S(1)} %get-tuple-element.164.refs_1_, bf16[3,320,176]{2,1,0:T(8,128)(2,1)S(1)} %get-tuple-element.168.refs_2_, ...), custom_call_target="tpu_custom_call" | custom-call | flops 1 | bytes 1 | tf_op jit(solution)/shard_map/pallas_call | solution.py:171
  99.5 5.3 %collective-permute-start.39 = (bf16[224,2560]{1,0:T(8,128)(2,1)S(1)}, bf16[224,2560]{1,0:T(8,128)(2,1)}, u32[]{:S(2)}, u32[]{:S(2)}) collective-permute-start(bf16[224,2560]{1,0:T(8,128)(2,1)S(1)} %shard_map.84.refs_0_), channel_id=1, source_target_pairs={{0,1},{1,0},{2,3},{3,2},{4,5},{5,4},{6,7},{7,6},{8,9},{9,8},{10,11... | collective-permute-start | bytes 3440648 | tf_op jit(solution)/shard_map/ppermute | solution.py:105
  107.4 2.5 %shard_map.86 = (bf16[1,320,176]{2,1,0:T(8,128)(2,1)S(1)}, f32[8,128]{1,0:T(8,128)}) custom-call(s32[1]{0:T(128)} %bitcast.core_ref, bf16[320,2560]{1,0:T(8,128)(2,1)S(1)} %divide_convert_fusion.weight_ref, bf16[224,2560]{1,0:T(8,128)(2,1)} %collective-permute-done.39.refs_0_), custom_call_target="tpu_custom_call" | custom-call | flops 1 | bytes 1 | tf_op jit(solution)/shard_map/pallas_call | solution.py:139
  109.9 46.0 %conditional.1 = (bf16[320,2560]{1,0:T(8,128)(2,1)S(1)}, f32[1]{0:T(128)}, f32[1]{0:T(128)}, f32[1]{0:T(128)}) conditional(s32[]{:T(128)} %clamp.3, (bf16[1,320,176]{2,1,0:T(8,128)(2,1)S(1)}, bf16[1,320,176]{2,1,0:T(8,128)(2,1)S(1)}, bf16[224,2560]{1,0:T(8,128)(2,1)S(1)}, bf16[224,2560]{1,0:T(8,128)(2,1)}, ...), branch_computations={%region_0.1_spmd, %region_1.2_spmd, %region_2.3_spmd, %region_3.4_... | conditional | flops 10649604 | bytes 14745852 | solution.py:245
  109.9 2.1 %branch_1_fun.4 = (bf16[320,512]{1,0:T(8,128)(2,1)S(1)}, f32[1]{0:T(128)}) custom-call(bf16[1,320,176]{2,1,0:T(8,128)(2,1)S(1)} %get-tuple-element.87.refs_0_, bf16[1,320,176]{2,1,0:T(8,128)(2,1)S(1)} %get-tuple-element.88.refs_1_, bf16[224,2560]{1,0:T(8,128)(2,1)S(1)} %get-tuple-element.89.refs_2_, bf16[224,2560]{1,0:T(8,128)(2,1)} %get-tuple-element.90.refs_3_, ...), custom_call_target="tpu_custom_call" | custom-call | flops 1 | bytes 1 | tf_op jit(solution)/shard_map/cond/branch_1_fun/pallas_call | solution.py:208
  114.0 2.1 %branch_1_fun.7 = (bf16[320,512]{1,0:T(8,128)(2,1)S(1)}, f32[1]{0:T(128)}) custom-call(bf16[1,320,176]{2,1,0:T(8,128)(2,1)S(1)} %get-tuple-element.87.refs_0_, bf16[1,320,176]{2,1,0:T(8,128)(2,1)S(1)} %get-tuple-element.88.refs_1_, bf16[224,2560]{1,0:T(8,128)(2,1)S(1)} %get-tuple-element.89.refs_2_, bf16[224,2560]{1,0:T(8,128)(2,1)} %get-tuple-element.90.refs_3_, ...), custom_call_target="tpu_custom_call" | custom-call | flops 1 | bytes 1 | tf_op jit(solution)/shard_map/cond/branch_1_fun/pallas_call | solution.py:208
  116.1 2.5 %collective-permute-start.8 = (bf16[320,512]{1,0:T(8,128)(2,1)S(1)}, bf16[320,512]{1,0:T(8,128)(2,1)S(1)}, u32[]{:S(2)}, u32[]{:S(2)}) collective-permute-start(bf16[320,512]{1,0:T(8,128)(2,1)S(1)} %get-tuple-element.96), channel_id=1, source_target_pairs={{496,0},{504,8},{0,16},{8,24},{16,32},{24,40},{32,48},{40,56},{48,... | collective-permute-start | bytes 983048 | tf_op jit(solution)/shard_map/cond/branch_1_fun/ppermute | solution.py:236
  118.6 2.2 %branch_1_fun.6 = (bf16[320,768]{1,0:T(8,128)(2,1)S(1)}, f32[1]{0:T(128)}) custom-call(bf16[1,320,176]{2,1,0:T(8,128)(2,1)S(1)} %get-tuple-element.87.refs_0_, bf16[1,320,176]{2,1,0:T(8,128)(2,1)S(1)} %get-tuple-element.88.refs_1_, bf16[224,2560]{1,0:T(8,128)(2,1)S(1)} %get-tuple-element.89.refs_2_, bf16[224,2560]{1,0:T(8,128)(2,1)} %get-tuple-element.90.refs_3_, ...), custom_call_target="tpu_custom_call" | custom-call | flops 1 | bytes 1 | tf_op jit(solution)/shard_map/cond/branch_1_fun/pallas_call | solution.py:208
  120.8 4.6 %collective-permute-start.7 = (bf16[320,768]{1,0:T(8,128)(2,1)S(1)}, bf16[320,768]{1,0:T(8,128)(2,1)S(1)}, u32[]{:S(2)}, u32[]{:S(2)}) collective-permute-start(bf16[320,768]{1,0:T(8,128)(2,1)S(1)} %get-tuple-element.95), channel_id=1, source_target_pairs={{496,0},{504,8},{0,16},{8,24},{16,32},{24,40},{32,48},{40,56},{48,... | collective-permute-start | bytes 1474568 | tf_op jit(solution)/shard_map/cond/branch_1_fun/ppermute | solution.py:236
  125.4 2.2 %branch_1_fun.5 = (bf16[320,768]{1,0:T(8,128)(2,1)S(1)}, f32[1]{0:T(128)}) custom-call(bf16[1,320,176]{2,1,0:T(8,128)(2,1)S(1)} %get-tuple-element.87.refs_0_, bf16[1,320,176]{2,1,0:T(8,128)(2,1)S(1)} %get-tuple-element.88.refs_1_, bf16[224,2560]{1,0:T(8,128)(2,1)S(1)} %get-tuple-element.89.refs_2_, bf16[224,2560]{1,0:T(8,128)(2,1)} %get-tuple-element.90.refs_3_, ...), custom_call_target="tpu_custom_call" | custom-call | flops 1 | bytes 1 | tf_op jit(solution)/shard_map/cond/branch_1_fun/pallas_call | solution.py:208
  127.6 3.2 %collective-permute-start.6 = (bf16[320,768]{1,0:T(8,128)(2,1)S(1)}, bf16[320,768]{1,0:T(8,128)(2,1)S(1)}, u32[]{:S(2)}, u32[]{:S(2)}) collective-permute-start(bf16[320,768]{1,0:T(8,128)(2,1)S(1)} %get-tuple-element.94), channel_id=1, source_target_pairs={{496,0},{504,8},{0,16},{8,24},{16,32},{24,40},{32,48},{40,56},{48,... | collective-permute-start | bytes 1474568 | tf_op jit(solution)/shard_map/cond/branch_1_fun/ppermute | solution.py:236
  130.8 4.7 %collective-permute-start.9 = (f32[1]{0:T(128)}, f32[1]{0:T(128)}, u32[]{:S(2)}, u32[]{:S(2)}) collective-permute-start(f32[1]{0:T(128)} %get-tuple-element.97), channel_id=1, source_target_pairs={{496,0},{504,8},{0,16},{8,24},{16,32},{24,40},{32,48},{40,56},{48,... | collective-permute-start | bytes 20 | tf_op jit(solution)/shard_map/cond/branch_1_fun/ppermute | solution.py:239
  135.7 9.2 %collective-permute-done.7 = bf16[320,768]{1,0:T(8,128)(2,1)S(1)} collective-permute-done((bf16[320,768]{1,0:T(8,128)(2,1)S(1)}, bf16[320,768]{1,0:T(8,128)(2,1)S(1)}, u32[]{:S(2)}, u32[]{:S(2)}) %collective-permute-start.7) | collective-permute-done | bytes 491552 | tf_op jit(solution)/shard_map/cond/branch_1_fun/ppermute | solution.py:236
  145.1 10.4 %collective-permute-done.6 = bf16[320,768]{1,0:T(8,128)(2,1)S(1)} collective-permute-done((bf16[320,768]{1,0:T(8,128)(2,1)S(1)}, bf16[320,768]{1,0:T(8,128)(2,1)S(1)}, u32[]{:S(2)}, u32[]{:S(2)}) %collective-permute-start.6) | collective-permute-done | bytes 491552 | tf_op jit(solution)/shard_map/cond/branch_1_fun/ppermute | solution.py:236
  (47 shorter events, 19.3 us)
Async XLA Ops:
  0.7 1.8 %copy-start.4 = (f32[2560]{0:T(1024)S(1)}, f32[2560]{0:T(1024)}, u32[]{:S(2)}) copy-start(f32[2560]{0:T(1024)} %param.14) | copy-start | bytes 30724
  2.4 1.2 copy-start.1
  4.8 54.5 %copy-start = (bf16[1,2560,320]{1,2,0:T(8,128)(2,1)S(1)}, bf16[1,2560,320]{1,2,0:T(8,128)(2,1)}, u32[]{:S(2)}) copy-start(bf16[1,2560,320]{1,2,0:T(8,128)(2,1)} %param.12) | copy-start | bytes 4915204
  4.8 20.1 %collective-permute-start.33 = (bf16[48,2560]{1,0:T(8,128)(2,1)S(1)}, bf16[48,2560]{1,0:T(8,128)(2,1)S(1)}, u32[]{:S(2)}, u32[]{:S(2)}) collective-permute-start(bf16[48,2560]{1,0:T(8,128)(2,1)S(1)} %get-tuple-element.163), channel_id=1, source_target_pairs={{0,2},{1,7},{2,4},{3,1},{4,6},{5,3},{6,0},{7,5},{8,10},{9,15},{10,... | collective-permute-start | bytes 737288 | tf_op jit(solution)/shard_map/ppermute | solution.py:101
  16.5 15.1 %collective-permute-start.35 = (bf16[48,2560]{1,0:T(8,128)(2,1)S(1)}, bf16[48,2560]{1,0:T(8,128)(2,1)S(1)}, u32[]{:S(2)}, u32[]{:S(2)}) collective-permute-start(bf16[48,2560]{1,0:T(8,128)(2,1)S(1)} %get-tuple-element.166), channel_id=1, source_target_pairs={{0,6},{1,3},{2,0},{3,5},{4,2},{5,7},{6,4},{7,1},{8,14},{9,11},{10,... | collective-permute-start | bytes 737288 | tf_op jit(solution)/shard_map/ppermute | solution.py:101
  18.4 34.6 %collective-permute-start.30 = (bf16[224,2560]{1,0:T(8,128)(2,1)S(1)}, bf16[224,2560]{1,0:T(8,128)(2,1)S(1)}, u32[]{:S(2)}, u32[]{:S(2)}) collective-permute-start(bf16[224,2560]{1,0:T(8,128)(2,1)S(1)} %get-tuple-element.160), channel_id=1, source_target_pairs={{0,2},{1,7},{2,4},{3,1},{4,6},{5,3},{6,0},{7,5},{8,10},{9,15},{10,... | collective-permute-start | bytes 3440648 | tf_op jit(solution)/shard_map/ppermute | solution.py:101
  31.5 3.8 %collective-permute-start.36 = (bf16[96,2560]{1,0:T(8,128)(2,1)S(1)}, bf16[96,2560]{1,0:T(8,128)(2,1)S(1)}, u32[]{:S(2)}, u32[]{:S(2)}) collective-permute-start(bf16[96,2560]{1,0:T(8,128)(2,1)S(1)} %constant_dynamic-update-slice_fusion.refs_3_), channel_id=1, source_target_pairs={{0,1},{1,0},{2,3},{3,2},{4,5},{5,4},{6,7},{7,6},{8,9},{9,8},{10,11... | collective-permute-start | bytes 1474568 | tf_op jit(solution)/shard_map/ppermute | solution.py:105
  35.3 53.2 %collective-permute-start.37 = (bf16[176,2560]{1,0:T(8,128)(2,1)S(1)}, bf16[176,2560]{1,0:T(8,128)(2,1)S(1)}, u32[]{:S(2)}, u32[]{:S(2)}) collective-permute-start(bf16[176,2560]{1,0:T(8,128)(2,1)S(1)} %shard_map.81), channel_id=1, source_target_pairs={{0,6},{1,3},{2,0},{3,5},{4,2},{5,7},{6,4},{7,1},{8,14},{9,11},{10,... | collective-permute-start | bytes 2703368 | tf_op jit(solution)/shard_map/ppermute | solution.py:101
  38.4 52.1 %collective-permute-start.32 = (bf16[224,2560]{1,0:T(8,128)(2,1)S(1)}, bf16[224,2560]{1,0:T(8,128)(2,1)S(1)}, u32[]{:S(2)}, u32[]{:S(2)}) collective-permute-start(bf16[224,2560]{1,0:T(8,128)(2,1)S(1)} %get-tuple-element.161.refs_0_.refs_3_), channel_id=1, source_target_pairs={{0,1},{1,0},{2,3},{3,2},{4,5},{5,4},{6,7},{7,6},{8,9},{9,8},{10,11... | collective-permute-start | bytes 3440648 | tf_op jit(solution)/shard_map/ppermute | solution.py:105
  53.0 46.5 %collective-permute-start.31 = (bf16[224,2560]{1,0:T(8,128)(2,1)S(1)}, bf16[224,2560]{1,0:T(8,128)(2,1)S(1)}, u32[]{:S(2)}, u32[]{:S(2)}) collective-permute-start(bf16[224,2560]{1,0:T(8,128)(2,1)S(1)} %collective-permute-done.30.refs_0_.array_ref), channel_id=1, source_target_pairs={{0,2},{1,7},{2,4},{3,1},{4,6},{5,3},{6,0},{7,5},{8,10},{9,15},{10,... | collective-permute-start | bytes 3440648 | tf_op jit(solution)/shard_map/ppermute | solution.py:101
  60.6 31.6 %collective-permute-start.34 = (bf16[176,2560]{1,0:T(8,128)(2,1)S(1)}, bf16[176,2560]{1,0:T(8,128)(2,1)S(1)}, u32[]{:S(2)}, u32[]{:S(2)}) collective-permute-start(bf16[176,2560]{1,0:T(8,128)(2,1)S(1)} %shard_map.80.refs_5_), channel_id=1, source_target_pairs={{0,1},{1,0},{2,3},{3,2},{4,5},{5,4},{6,7},{7,6},{8,9},{9,8},{10,11... | collective-permute-start | bytes 2703368 | tf_op jit(solution)/shard_map/ppermute | solution.py:105
  88.5 4.3 %collective-permute-start.38 = (bf16[176,2560]{1,0:T(8,128)(2,1)S(1)}, bf16[176,2560]{1,0:T(8,128)(2,1)S(1)}, u32[]{:S(2)}, u32[]{:S(2)}) collective-permute-start(bf16[176,2560]{1,0:T(8,128)(2,1)S(1)} %collective-permute-done.37.refs_2_.refs_7_), channel_id=1, source_target_pairs={{0,1},{1,0},{2,3},{3,2},{4,5},{5,4},{6,7},{7,6},{8,9},{9,8},{10,11... | collective-permute-start | bytes 2703368 | tf_op jit(solution)/shard_map/ppermute | solution.py:105
  99.5 7.9 %collective-permute-start.39 = (bf16[224,2560]{1,0:T(8,128)(2,1)S(1)}, bf16[224,2560]{1,0:T(8,128)(2,1)}, u32[]{:S(2)}, u32[]{:S(2)}) collective-permute-start(bf16[224,2560]{1,0:T(8,128)(2,1)S(1)} %shard_map.84.refs_0_), channel_id=1, source_target_pairs={{0,1},{1,0},{2,3},{3,2},{4,5},{5,4},{6,7},{7,6},{8,9},{9,8},{10,11... | collective-permute-start | bytes 3440648 | tf_op jit(solution)/shard_map/ppermute | solution.py:105
  105.5 4.4 %copy-start.2 = (f32[320,2560]{1,0:T(8,128)S(1)}, f32[320,2560]{1,0:T(8,128)}, u32[]{:S(2)}) copy-start(f32[320,2560]{1,0:T(8,128)} %get-tuple-element.172) | copy-start | bytes 9830404
  112.1 23.4 %collective-permute-start.5 = (bf16[320,512]{1,0:T(8,128)(2,1)S(1)}, bf16[320,512]{1,0:T(8,128)(2,1)S(1)}, u32[]{:S(2)}, u32[]{:S(2)}) collective-permute-start(bf16[320,512]{1,0:T(8,128)(2,1)S(1)} %get-tuple-element.93), channel_id=1, source_target_pairs={{496,0},{504,8},{0,16},{8,24},{16,32},{24,40},{32,48},{40,56},{48,... | collective-permute-start | bytes 983048 | tf_op jit(solution)/shard_map/cond/branch_1_fun/ppermute | solution.py:236
  116.1 19.4 %collective-permute-start.8 = (bf16[320,512]{1,0:T(8,128)(2,1)S(1)}, bf16[320,512]{1,0:T(8,128)(2,1)S(1)}, u32[]{:S(2)}, u32[]{:S(2)}) collective-permute-start(bf16[320,512]{1,0:T(8,128)(2,1)S(1)} %get-tuple-element.96), channel_id=1, source_target_pairs={{496,0},{504,8},{0,16},{8,24},{16,32},{24,40},{32,48},{40,56},{48,... | collective-permute-start | bytes 983048 | tf_op jit(solution)/shard_map/cond/branch_1_fun/ppermute | solution.py:236
  120.8 24.2 %collective-permute-start.7 = (bf16[320,768]{1,0:T(8,128)(2,1)S(1)}, bf16[320,768]{1,0:T(8,128)(2,1)S(1)}, u32[]{:S(2)}, u32[]{:S(2)}) collective-permute-start(bf16[320,768]{1,0:T(8,128)(2,1)S(1)} %get-tuple-element.95), channel_id=1, source_target_pairs={{496,0},{504,8},{0,16},{8,24},{16,32},{24,40},{32,48},{40,56},{48,... | collective-permute-start | bytes 1474568 | tf_op jit(solution)/shard_map/cond/branch_1_fun/ppermute | solution.py:236
  127.6 27.8 %collective-permute-start.6 = (bf16[320,768]{1,0:T(8,128)(2,1)S(1)}, bf16[320,768]{1,0:T(8,128)(2,1)S(1)}, u32[]{:S(2)}, u32[]{:S(2)}) collective-permute-start(bf16[320,768]{1,0:T(8,128)(2,1)S(1)} %get-tuple-element.94), channel_id=1, source_target_pairs={{496,0},{504,8},{0,16},{8,24},{16,32},{24,40},{32,48},{40,56},{48,... | collective-permute-start | bytes 1474568 | tf_op jit(solution)/shard_map/cond/branch_1_fun/ppermute | solution.py:236
  130.8 25.0 %collective-permute-start.9 = (f32[1]{0:T(128)}, f32[1]{0:T(128)}, u32[]{:S(2)}, u32[]{:S(2)}) collective-permute-start(f32[1]{0:T(128)} %get-tuple-element.97), channel_id=1, source_target_pairs={{496,0},{504,8},{0,16},{8,24},{16,32},{24,40},{32,48},{40,56},{48,... | collective-permute-start | bytes 20 | tf_op jit(solution)/shard_map/cond/branch_1_fun/ppermute | solution.py:239
  155.9 1.2 copy-start.3

commit v8 on v5

--- a/solution.py
+++ b/solution.py
@@ -28,47 +28,38 @@
     return jnp.concatenate([cot_t[:, :, :LANES], folded], axis=1)
 
 
-def norm_kernel(tokens_ref, gain_ref, out_ref):
+def norm_kernel(tokens_ref, gain_ref, *out_refs):
     wide = tokens_ref[...].astype(jnp.float32)
     mean_square = jnp.mean(wide * wide, axis=-1, keepdims=True)
-    out_ref[...] = (wide * lax.rsqrt(mean_square + EPSILON) * gain_ref[...]).astype(jnp.bfloat16)
+    normed = (wide * lax.rsqrt(mean_square + EPSILON) * gain_ref[...]).astype(jnp.bfloat16)
+    for out_ref in out_refs:
+        out_ref[...] = normed
 
 
 def norm(tokens, gain):
+    vmem = pl.BlockSpec(memory_space=pltpu.VMEM)
     return pl.pallas_call(
         norm_kernel,
-        out_shape=jax.ShapeDtypeStruct(tokens.shape, jnp.bfloat16),
+        in_specs=[vmem, vmem],
+        out_specs=(vmem, vmem),
+        out_shape=(jax.ShapeDtypeStruct(tokens.shape, jnp.bfloat16),) * 2,
         compiler_params=pltpu.CompilerParams(vmem_limit_bytes=VMEM),
         cost_estimate=pl.CostEstimate(flops=8 * tokens.size, bytes_accessed=4 * tokens.size, transcendentals=0),
     )(tokens, gain[None])
 
 
 def corner(array):
-    return pl.BlockSpec((1,) * (array.ndim - 2) + (16, LANES), lambda i: (0,) * array.ndim)
-
-
-def copy_kernel(array_ref, token_ref, out_ref):
-    out_ref[...] = array_ref[...]
-
-
-def copy_after(array, token):
-    whole = pl.BlockSpec(array.shape, lambda i: (0,) * array.ndim)
-    return pl.pallas_call(
-        copy_kernel,
-        grid=(1,),
-        in_specs=[whole, corner(token)],
-        out_specs=whole,
-        out_shape=jax.ShapeDtypeStruct(array.shape, array.dtype),
-        compiler_params=pltpu.CompilerParams(vmem_limit_bytes=VMEM),
-        cost_estimate=HIDDEN,
-    )(array, token)
+    return pl.BlockSpec(
+        (1,) * (array.ndim - 2) + (min(16, array.shape[-2]), LANES), lambda i: (0,) * array.ndim
+    )
 
 
 def once_there(array, *tokens):
     whole = pl.BlockSpec(memory_space=pl.ANY)
     return pl.pallas_call(
         lambda *refs: None,
-        in_specs=[whole] + [pl.BlockSpec(memory_space=pltpu.VMEM)] * len(tokens),
+        grid=(1,),
+        in_specs=[whole] + [corner(token) for token in tokens],
         out_specs=whole,
         out_shape=jax.ShapeDtypeStruct(array.shape, array.dtype),
         input_output_aliases={0: 0},
@@ -121,7 +112,8 @@
 def products(grads, blocks, columns):
     terms = [grad_ref[i] for grad_ref in grads for i in range(grad_ref.shape[0])]
     return sum(
-        jnp.dot(term, block[:, columns], preferred_element_type=jnp.float32) for term, block in zip(terms, blocks)
+        jnp.dot(term, block[-term.shape[1] :, columns], preferred_element_type=jnp.float32)
+        for term, block in zip(terms, blocks)
     )
 
 
@@ -150,25 +142,42 @@
 
 
 def late_kernel(groups, first, *refs):
-    grads, blocks = refs[:groups], refs[groups:-4]
-    early_ref, weight_ref, out_ref, weight_out_ref = refs[-4:]
+    grads, blocks = refs[:groups], refs[groups:-7]
+    early_ref, weight_ref, out_ref, weight_out_ref, held, early, sems = refs[-7:]
+    tokens, width = held.shape[1:]
+    columns = pl.ds(first, width)
+    copies = [
+        pltpu.make_async_copy(block.at[pl.ds(block.shape[0] - tokens, tokens), columns], held.at[i], sems.at[i])
+        for i, block in enumerate(blocks)
+    ]
+    copies.append(pltpu.make_async_copy(early_ref.at[:, columns], early, sems.at[len(blocks)]))
+    for copy in copies:
+        copy.start()
     weight_out_ref[0] = weight_ref[0]
-    for at in range(0, out_ref.shape[1], TILE):
-        part = slice(first + at, first + at + TILE)
-        update = LEARN_RATE * (SCALE * products(grads, blocks, part))
-        out_ref[:, at : at + TILE] = (early_ref[:, part] - update).astype(jnp.bfloat16)
+    for copy in copies:
+        copy.wait()
+    for at in range(0, width, TILE):
+        part = slice(at, at + TILE)
+        update = LEARN_RATE * (SCALE * products(grads, [held.at[i] for i in range(len(blocks))], part))
+        out_ref[:, part] = (early[:, part] - update).astype(jnp.bfloat16)
 
 
 def late_chunk(grads, blocks, early, weight, first, width):
     vmem, smem = pl.BlockSpec(memory_space=pltpu.VMEM), pl.BlockSpec(memory_space=pltpu.SMEM)
+    whole = pl.BlockSpec(memory_space=pl.ANY)
     return pl.pallas_call(
         partial(late_kernel, len(grads), first),
-        in_specs=[vmem] * (len(grads) + len(blocks) + 1) + [smem],
+        in_specs=[vmem] * len(grads) + [whole] * (len(blocks) + 1) + [smem],
         out_specs=(vmem, smem),
         out_shape=(
             jax.ShapeDtypeStruct((early.shape[0], width), jnp.bfloat16),
             jax.ShapeDtypeStruct(weight.shape, weight.dtype),
         ),
+        scratch_shapes=[
+            pltpu.VMEM((len(blocks), grads[0].shape[2], width), jnp.bfloat16),
+            pltpu.VMEM((early.shape[0], width), jnp.float32),
+            pltpu.SemaphoreType.DMA((len(blocks) + 1,)),
+        ],
         compiler_params=pltpu.CompilerParams(vmem_limit_bytes=VMEM),
         cost_estimate=HIDDEN,
     )(*grads, *blocks, early, weight)
@@ -203,12 +212,12 @@
     ahead, back, far = ((me + step * (1 - 2 * core) + count) % count for step in (2, -2, 4))
     numer_t = numerator[0].T
     weight_t = (numer_t.astype(jnp.float32) / push_weight[0]).astype(jnp.bfloat16)
-    own = norm(activations.reshape(-1, DW), norm_gain)
+    own, plain = norm(activations.reshape(-1, DW), norm_gain)
     first = to_chip(own, 1)
     third = to_chip(first, 1)
     packed = pack_cotangent(cotangent.reshape(-1, cotangent.shape[2]).T, count)
     packed = lax.all_to_all(packed, "fsdp", split_axis=0, concat_axis=0, tiled=True)
-    second = to_chip(copy_after(own, packed), -1)
+    second = to_chip(once_there(plain, packed), -1)
     blocks, grads = [], []
     for sources, block in (((me, me ^ 1), own), ((back, ahead ^ 1), first), ((ahead, back ^ 1), second)):
         pair = (block, to_core(block))

time: 161 us -> 191 us (1.19)
  waiting for transfers between devices: 68 us -> 82 us
  starting transfers between devices: 51.5 us -> 65.3 us
  local copies, waits for them, and re-layouts: 2.49 us -> 5.7 us
  Pallas kernels: 29.9 us -> 27.6 us
    ppermute x4, waiting for transfers between devices: 31.9 us -> 49.5 us  [mix_with(): partner = lax.ppermute(local, 'rep', route(hop_size))]
    ppermute x4, starting transfers between devices: 12.2 us -> 24.5 us  [mix_with(): partner = lax.ppermute(local, 'rep', route(hop_size))]
    unnamed x10 -> x14, local copies, waits for them, and re-layouts: 0.63 us -> 3.84 us
    all_to_all x1, waiting for transfers between devices: 14.6 us -> 12.7 us  [on_device(): lax.all_to_all(packed, 'fsdp', split_axis=0, concat_axis=0, tiled=True)]
  transfers between devices with their start and end apart: 13 -> 13, of which waited for: 6 -> 5; matrix products, arithmetic and copies ran while one was open for 2% -> 1% of each run, Pallas kernels for 16% -> 13%
where the time goes in v8:
time: 191 us; the launch traced here: 188 us
  waiting for transfers between devices  82 us (43%)
  starting transfers between devices  65.3 us (34%)
  Pallas kernels  27.6 us (14%)
  local copies, waits for them, and re-layouts  5.7 us (3%)
  between operations  3.97 us (2%)
  other arithmetic  3.82 us (2%)
    ppermute x4, waiting for transfers between devices, mix_with(): partner = lax.ppermute(local, 'rep', route(hop_size))  49.5 us
    ppermute x4, starting transfers between devices, mix_with(): partner = lax.ppermute(local, 'rep', route(hop_size))  24.5 us
    ppermute x3, waiting for transfers between devices, to_chip(): return lax.ppermute(values, 'fsdp', route)  19.8 us
    all_to_all x1, waiting for transfers between devices, on_device(): lax.all_to_all(packed, 'fsdp', split_axis=0, concat_axis=0, tiled=True)  12.7 us
    ppermute x4, starting transfers between devices, to_core(): lax.ppermute(values, 'fsdp', [(i, i ^ 1) for i in range(lax.axis_size('fs...  12.4 us
    ppermute x3, starting transfers between devices, to_chip(): return lax.ppermute(values, 'fsdp', route)  12.4 us
    all_to_all x1, starting transfers between devices, on_device(): lax.all_to_all(packed, 'fsdp', split_axis=0, concat_axis=0, tiled=True)  11.8 us
    pallas_call x5, Pallas kernels, grad_out(): pl.pallas_call(grad_out_kernel, in_specs=[pl.BlockSpec(memory_space=pltpu...  10.8 us
  transfers between devices with their start and end apart: 13, of which 5 were waited for; matrix products, arithmetic and copies ran while one was open for 1% of the time, Pallas kernels for 13%

profile of v8, /device:TPU:1, one launch (start us, length us, event | category | flops | bytes accessed | tf_op | source)
XLA Modules:
  0.0 188.5 jit_solution(3907530382711526036)
XLA Ops:
  3.8 11.8 %all-to-all-start = ((bf16[8,480,128]{2,1,0:T(8,128)(2,1)}), bf16[8,480,128]{2,1,0:T(8,128)(2,1)S(1)}, u32[]{:S(2)}, u32[]{:S(2)}) async-start(bf16[8,480,128]{2,1,0:T(8,128)(2,1)} %maximum_maximum_fusion), calls=%async_computation | async-start | bytes 1966080 | tf_op jit(solution)/shard_map/all_to_all | solution.py:219
  18.1 5.4 %collective-permute-start.30 = (bf16[176,2560]{1,0:T(8,128)(2,1)}, bf16[176,2560]{1,0:T(8,128)(2,1)S(1)}, u32[]{:S(2)}, u32[]{:S(2)}) collective-permute-start(bf16[176,2560]{1,0:T(8,128)(2,1)} %get-tuple-element.151.refs_0_.refs_3_), channel_id=1, source_target_pairs={{0,2},{1,7},{2,4},{3,1},{4,6},{5,3},{6,0},{7,5},{8,10},{9,15},{10,... | collective-permute-start | bytes 2703368 | tf_op jit(solution)/shard_map/ppermute | solution.py:74
  23.5 12.7 %all-to-all-done.cot_ref.refs_1_ = bf16[8,480,128]{2,1,0:T(8,128)(2,1)S(1)} async-done(((bf16[8,480,128]{2,1,0:T(8,128)(2,1)}), bf16[8,480,128]{2,1,0:T(8,128)(2,1)S(1)}, u32[]{:S(2)}, u32[]{:S(2)}) %all-to-all-start) | async-done | bytes 983072 | tf_op jit(solution)/shard_map/all_to_all | solution.py:219
  37.3 3.6 %collective-permute-start.34 = (bf16[176,2560]{1,0:T(8,128)(2,1)S(1)}, bf16[176,2560]{1,0:T(8,128)(2,1)}, u32[]{:S(2)}, u32[]{:S(2)}) collective-permute-start(bf16[176,2560]{1,0:T(8,128)(2,1)S(1)} %shard_map.80), channel_id=1, source_target_pairs={{0,6},{1,3},{2,0},{3,5},{4,2},{5,7},{6,4},{7,1},{8,14},{9,11},{10,... | collective-permute-start | bytes 2703368 | tf_op jit(solution)/shard_map/ppermute | solution.py:74
  40.9 3.3 %collective-permute-start.32 = (bf16[176,2560]{1,0:T(8,128)(2,1)}, bf16[176,2560]{1,0:T(8,128)(2,1)}, u32[]{:S(2)}, u32[]{:S(2)}) collective-permute-start(bf16[176,2560]{1,0:T(8,128)(2,1)} %get-tuple-element.151.refs_0_.refs_3_), channel_id=1, source_target_pairs={{0,1},{1,0},{2,3},{3,2},{4,5},{5,4},{6,7},{7,6},{8,9},{9,8},{10,11... | collective-permute-start | bytes 2703368 | tf_op jit(solution)/shard_map/ppermute | solution.py:78
  44.3 19.8 %collective-permute-done.30.refs_0_.refs_5_ = bf16[176,2560]{1,0:T(8,128)(2,1)S(1)} collective-permute-done((bf16[176,2560]{1,0:T(8,128)(2,1)}, bf16[176,2560]{1,0:T(8,128)(2,1)S(1)}, u32[]{:S(2)}, u32[]{:S(2)}) %collective-permute-start.30) | collective-permute-done | bytes 901152 | tf_op jit(solution)/shard_map/ppermute | solution.py:74
  66.1 3.4 %collective-permute-start.31 = (bf16[176,2560]{1,0:T(8,128)(2,1)S(1)}, bf16[176,2560]{1,0:T(8,128)(2,1)}, u32[]{:S(2)}, u32[]{:S(2)}) collective-permute-start(bf16[176,2560]{1,0:T(8,128)(2,1)S(1)} %collective-permute-done.30.refs_0_.refs_5_), channel_id=1, source_target_pairs={{0,2},{1,7},{2,4},{3,1},{4,6},{5,3},{6,0},{7,5},{8,10},{9,15},{10,... | collective-permute-start | bytes 2703368 | tf_op jit(solution)/shard_map/ppermute | solution.py:74
  69.5 5.0 %collective-permute-start.35 = (bf16[176,2560]{1,0:T(8,128)(2,1)}, bf16[176,2560]{1,0:T(8,128)(2,1)}, u32[]{:S(2)}, u32[]{:S(2)}) collective-permute-start(bf16[176,2560]{1,0:T(8,128)(2,1)} %collective-permute-done.34.refs_0_.refs_7_), channel_id=1, source_target_pairs={{0,1},{1,0},{2,3},{3,2},{4,5},{5,4},{6,7},{7,6},{8,9},{9,8},{10,11... | collective-permute-start | bytes 2703368 | tf_op jit(solution)/shard_map/ppermute | solution.py:78
  77.1 2.8 %shard_map.78.refs_0_ = bf16[2,320,176]{2,1,0:T(8,128)(2,1)S(1)} custom-call(s32[2]{0:T(128)S(1)} %pad_add_fusion.ids_ref, bf16[320,2560]{1,0:T(8,128)(2,1)S(1)} %divide_convert_fusion.weight_ref, bf16[8,480,128]{2,1,0:T(8,128)(2,1)S(1)} %all-to-all-done.cot_ref.refs_1_, bf16[176,2560]{1,0:T(8,128)(2,1)} %get-tuple-element.151.refs_0_.refs_3_, ...), custom_call_target="tpu_custom_call" | custom-call | flops 1 | bytes 1 | tf_op jit(solution)/shard_map/pallas_call | solution.py:102
  79.8 2.5 %shard_map.79.refs_1_ = bf16[2,320,176]{2,1,0:T(8,128)(2,1)S(1)} custom-call(s32[2]{0:T(128)S(1)} %pad_add_fusion.1.ids_ref, bf16[320,2560]{1,0:T(8,128)(2,1)S(1)} %divide_convert_fusion.weight_ref, bf16[8,480,128]{2,1,0:T(8,128)(2,1)S(1)} %all-to-all-done.cot_ref.refs_1_, bf16[176,2560]{1,0:T(8,128)(2,1)S(1)} %collective-permute-done.30.refs_0_.refs_5_, ...), custom_call_target="tpu_custom_call" | custom-call | flops 1 | bytes 1 | tf_op jit(solution)/shard_map/pallas_call | solution.py:102
  82.3 2.9 %shard_map.81.refs_2_ = bf16[2,320,176]{2,1,0:T(8,128)(2,1)S(1)} custom-call(s32[2]{0:T(128)S(1)} %pad_add_fusion.2.ids_ref, bf16[320,2560]{1,0:T(8,128)(2,1)S(1)} %divide_convert_fusion.weight_ref, bf16[8,480,128]{2,1,0:T(8,128)(2,1)S(1)} %all-to-all-done.cot_ref.refs_1_, bf16[176,2560]{1,0:T(8,128)(2,1)} %collective-permute-done.34.refs_0_.refs_7_, ...), custom_call_target="tpu_custom_call" | custom-call | flops 1 | bytes 1 | tf_op jit(solution)/shard_map/pallas_call | solution.py:102
  85.2 6.7 %shard_map.82 = (f32[320,2560]{1,0:T(8,128)}, f32[8,128]{1,0:T(8,128)S(1)}) custom-call(bf16[2,320,176]{2,1,0:T(8,128)(2,1)S(1)} %shard_map.78.refs_0_, bf16[2,320,176]{2,1,0:T(8,128)(2,1)S(1)} %shard_map.79.refs_1_, bf16[2,320,176]{2,1,0:T(8,128)(2,1)S(1)} %shard_map.81.refs_2_, bf16[176,2560]{1,0:T(8,128)(2,1)} %get-tuple-element.151.refs_0_.refs_3_, ...), custom_call_target="tpu_custom_call" | custom-call | flops 1 | bytes 1 | tf_op jit(solution)/shard_map/pallas_call | solution.py:131
  91.9 2.2 %collective-permute-start.36 = (bf16[176,2560]{1,0:T(8,128)(2,1)}, bf16[176,2560]{1,0:T(8,128)(2,1)S(1)}, u32[]{:S(2)}, u32[]{:S(2)}) collective-permute-start(bf16[176,2560]{1,0:T(8,128)(2,1)} %shard_map.83.refs_0_), channel_id=1, source_target_pairs={{0,1},{1,0},{2,3},{3,2},{4,5},{5,4},{6,7},{7,6},{8,9},{9,8},{10,11... | collective-permute-start | bytes 2703368 | tf_op jit(solution)/shard_map/ppermute | solution.py:78
  98.7 87.5 %conditional.1 = (bf16[320,2560]{1,0:T(8,128)(2,1)S(1)}, f32[1]{0:T(128)}, f32[1]{0:T(128)}, f32[1]{0:T(128)}) conditional(s32[]{:T(128)} %clamp.3, (bf16[1,320,176]{2,1,0:T(8,128)(2,1)S(1)}, bf16[1,320,176]{2,1,0:T(8,128)(2,1)S(1)}, bf16[176,2560]{1,0:T(8,128)(2,1)}, bf16[176,2560]{1,0:T(8,128)(2,1)S(1)}, ...), branch_computations={%region_0.1_spmd, %region_1.2_spmd, %region_2.3_spmd, %region_3.4_... | conditional | flops 10649604 | bytes 14745852 | solution.py:205
  100.8 4.2 %collective-permute-start.15 = (bf16[320,512]{1,0:T(8,128)(2,1)S(1)}, bf16[320,512]{1,0:T(8,128)(2,1)S(1)}, u32[]{:S(2)}, u32[]{:S(2)}) collective-permute-start(bf16[320,512]{1,0:T(8,128)(2,1)S(1)} %get-tuple-element.115), channel_id=1, source_target_pairs={{448,0},{456,8},{464,16},{472,24},{480,32},{488,40},{496,48},{504,... | collective-permute-start | bytes 983048 | tf_op jit(solution)/shard_map/cond/branch_3_fun/ppermute | solution.py:196
  107.2 5.4 %collective-permute-start.18 = (bf16[320,512]{1,0:T(8,128)(2,1)S(1)}, bf16[320,512]{1,0:T(8,128)(2,1)S(1)}, u32[]{:S(2)}, u32[]{:S(2)}) collective-permute-start(bf16[320,512]{1,0:T(8,128)(2,1)S(1)} %get-tuple-element.118), channel_id=1, source_target_pairs={{448,0},{456,8},{464,16},{472,24},{480,32},{488,40},{496,48},{504,... | collective-permute-start | bytes 983048 | tf_op jit(solution)/shard_map/cond/branch_3_fun/ppermute | solution.py:196
  112.6 2.2 %branch_3_fun.6 = (bf16[320,768]{1,0:T(8,128)(2,1)S(1)}, f32[1]{0:T(128)}) custom-call(bf16[1,320,176]{2,1,0:T(8,128)(2,1)S(1)} %get-tuple-element.109.refs_0_, bf16[1,320,176]{2,1,0:T(8,128)(2,1)S(1)} %get-tuple-element.110.refs_1_, bf16[176,2560]{1,0:T(8,128)(2,1)} %get-tuple-element.111.refs_2_, bf16[176,2560]{1,0:T(8,128)(2,1)S(1)} %get-tuple-element.112.refs_3_, ...), custom_call_target="tpu_custom_call" | custom-call | flops 1 | bytes 1 | tf_op jit(solution)/shard_map/cond/branch_3_fun/pallas_call | solution.py:168
  114.8 2.4 %collective-permute-start.17 = (bf16[320,768]{1,0:T(8,128)(2,1)S(1)}, bf16[320,768]{1,0:T(8,128)(2,1)S(1)}, u32[]{:S(2)}, u32[]{:S(2)}) collective-permute-start(bf16[320,768]{1,0:T(8,128)(2,1)S(1)} %get-tuple-element.117), channel_id=1, source_target_pairs={{448,0},{456,8},{464,16},{472,24},{480,32},{488,40},{496,48},{504,... | collective-permute-start | bytes 1474568 | tf_op jit(solution)/shard_map/cond/branch_3_fun/ppermute | solution.py:196
  117.2 2.2 %branch_3_fun.5 = (bf16[320,768]{1,0:T(8,128)(2,1)S(1)}, f32[1]{0:T(128)}) custom-call(bf16[1,320,176]{2,1,0:T(8,128)(2,1)S(1)} %get-tuple-element.109.refs_0_, bf16[1,320,176]{2,1,0:T(8,128)(2,1)S(1)} %get-tuple-element.110.refs_1_, bf16[176,2560]{1,0:T(8,128)(2,1)} %get-tuple-element.111.refs_2_, bf16[176,2560]{1,0:T(8,128)(2,1)S(1)} %get-tuple-element.112.refs_3_, ...), custom_call_target="tpu_custom_call" | custom-call | flops 1 | bytes 1 | tf_op jit(solution)/shard_map/cond/branch_3_fun/pallas_call | solution.py:168
  119.4 12.4 %collective-permute-start.16 = (bf16[320,768]{1,0:T(8,128)(2,1)S(1)}, bf16[320,768]{1,0:T(8,128)(2,1)S(1)}, u32[]{:S(2)}, u32[]{:S(2)}) collective-permute-start(bf16[320,768]{1,0:T(8,128)(2,1)S(1)} %get-tuple-element.116), channel_id=1, source_target_pairs={{448,0},{456,8},{464,16},{472,24},{480,32},{488,40},{496,48},{504,... | collective-permute-start | bytes 1474568 | tf_op jit(solution)/shard_map/cond/branch_3_fun/ppermute | solution.py:196
  131.8 4.2 %collective-permute-start.19 = (f32[1]{0:T(128)}, f32[1]{0:T(128)}, u32[]{:S(2)}, u32[]{:S(2)}) collective-permute-start(f32[1]{0:T(128)} %get-tuple-element.119), channel_id=1, source_target_pairs={{448,0},{456,8},{464,16},{472,24},{480,32},{488,40},{496,48},{504,... | collective-permute-start | bytes 20 | tf_op jit(solution)/shard_map/cond/branch_3_fun/ppermute | solution.py:199
  136.2 6.2 %collective-permute-done.18 = bf16[320,512]{1,0:T(8,128)(2,1)S(1)} collective-permute-done((bf16[320,512]{1,0:T(8,128)(2,1)S(1)}, bf16[320,512]{1,0:T(8,128)(2,1)S(1)}, u32[]{:S(2)}, u32[]{:S(2)}) %collective-permute-start.18) | collective-permute-done | bytes 327712 | tf_op jit(solution)/shard_map/cond/branch_3_fun/ppermute | solution.py:196
  142.5 20.6 %collective-permute-done.17 = bf16[320,768]{1,0:T(8,128)(2,1)S(1)} collective-permute-done((bf16[320,768]{1,0:T(8,128)(2,1)S(1)}, bf16[320,768]{1,0:T(8,128)(2,1)S(1)}, u32[]{:S(2)}, u32[]{:S(2)}) %collective-permute-start.17) | collective-permute-done | bytes 491552 | tf_op jit(solution)/shard_map/cond/branch_3_fun/ppermute | solution.py:196
  163.2 22.6 %collective-permute-done.16 = bf16[320,768]{1,0:T(8,128)(2,1)S(1)} collective-permute-done((bf16[320,768]{1,0:T(8,128)(2,1)S(1)}, bf16[320,768]{1,0:T(8,128)(2,1)S(1)}, u32[]{:S(2)}, u32[]{:S(2)}) %collective-permute-start.16) | collective-permute-done | bytes 491552 | tf_op jit(solution)/shard_map/cond/branch_3_fun/ppermute | solution.py:196
  (46 shorter events, 19.9 us)
Async XLA Ops:
  2.5 13.1 %copy-start.6 = (f32[2560]{0:T(1024)S(1)}, f32[2560]{0:T(1024)}, u32[]{:S(2)}) copy-start(f32[2560]{0:T(1024)} %param.14) | copy-start | bytes 30724
  2.5 13.1 %copy-start.1 = (bf16[2,88,2560]{2,1,0:T(8,128)(2,1)S(1)}, bf16[2,88,2560]{2,1,0:T(8,128)(2,1)}, u32[]{:S(2)}) copy-start(bf16[2,88,2560]{2,1,0:T(8,128)(2,1)} %param.15) | copy-start | bytes 2703364
  3.8 32.3 %all-to-all-start = ((bf16[8,480,128]{2,1,0:T(8,128)(2,1)}), bf16[8,480,128]{2,1,0:T(8,128)(2,1)S(1)}, u32[]{:S(2)}, u32[]{:S(2)}) async-start(bf16[8,480,128]{2,1,0:T(8,128)(2,1)} %maximum_maximum_fusion), calls=%async_computation | async-start | bytes 1966080 | tf_op jit(solution)/shard_map/all_to_all | solution.py:219
  17.1 1.0 copy-start.2
  18.1 46.1 %collective-permute-start.30 = (bf16[176,2560]{1,0:T(8,128)(2,1)}, bf16[176,2560]{1,0:T(8,128)(2,1)S(1)}, u32[]{:S(2)}, u32[]{:S(2)}) collective-permute-start(bf16[176,2560]{1,0:T(8,128)(2,1)} %get-tuple-element.151.refs_0_.refs_3_), channel_id=1, source_target_pairs={{0,2},{1,7},{2,4},{3,1},{4,6},{5,3},{6,0},{7,5},{8,10},{9,15},{10,... | collective-permute-start | bytes 2703368 | tf_op jit(solution)/shard_map/ppermute | solution.py:74
  36.1 1.2 copy-start.3
  37.3 32.2 %collective-permute-start.34 = (bf16[176,2560]{1,0:T(8,128)(2,1)S(1)}, bf16[176,2560]{1,0:T(8,128)(2,1)}, u32[]{:S(2)}, u32[]{:S(2)}) collective-permute-start(bf16[176,2560]{1,0:T(8,128)(2,1)S(1)} %shard_map.80), channel_id=1, source_target_pairs={{0,6},{1,3},{2,0},{3,5},{4,2},{5,7},{6,4},{7,1},{8,14},{9,11},{10,... | collective-permute-start | bytes 2703368 | tf_op jit(solution)/shard_map/ppermute | solution.py:74
  40.9 36.1 %collective-permute-start.32 = (bf16[176,2560]{1,0:T(8,128)(2,1)}, bf16[176,2560]{1,0:T(8,128)(2,1)}, u32[]{:S(2)}, u32[]{:S(2)}) collective-permute-start(bf16[176,2560]{1,0:T(8,128)(2,1)} %get-tuple-element.151.refs_0_.refs_3_), channel_id=1, source_target_pairs={{0,1},{1,0},{2,3},{3,2},{4,5},{5,4},{6,7},{7,6},{8,9},{9,8},{10,11... | collective-permute-start | bytes 2703368 | tf_op jit(solution)/shard_map/ppermute | solution.py:78
  64.2 15.7 %collective-permute-start.33 = (bf16[176,2560]{1,0:T(8,128)(2,1)S(1)}, bf16[176,2560]{1,0:T(8,128)(2,1)}, u32[]{:S(2)}, u32[]{:S(2)}) collective-permute-start(bf16[176,2560]{1,0:T(8,128)(2,1)S(1)} %collective-permute-done.30.refs_0_.refs_5_), channel_id=1, source_target_pairs={{0,1},{1,0},{2,3},{3,2},{4,5},{5,4},{6,7},{7,6},{8,9},{9,8},{10,11... | collective-permute-start | bytes 2703368 | tf_op jit(solution)/shard_map/ppermute | solution.py:78
  66.1 25.8 %collective-permute-start.31 = (bf16[176,2560]{1,0:T(8,128)(2,1)S(1)}, bf16[176,2560]{1,0:T(8,128)(2,1)}, u32[]{:S(2)}, u32[]{:S(2)}) collective-permute-start(bf16[176,2560]{1,0:T(8,128)(2,1)S(1)} %collective-permute-done.30.refs_0_.refs_5_), channel_id=1, source_target_pairs={{0,2},{1,7},{2,4},{3,1},{4,6},{5,3},{6,0},{7,5},{8,10},{9,15},{10,... | collective-permute-start | bytes 2703368 | tf_op jit(solution)/shard_map/ppermute | solution.py:74
  69.5 12.8 %collective-permute-start.35 = (bf16[176,2560]{1,0:T(8,128)(2,1)}, bf16[176,2560]{1,0:T(8,128)(2,1)}, u32[]{:S(2)}, u32[]{:S(2)}) collective-permute-start(bf16[176,2560]{1,0:T(8,128)(2,1)} %collective-permute-done.34.refs_0_.refs_7_), channel_id=1, source_target_pairs={{0,1},{1,0},{2,3},{3,2},{4,5},{5,4},{6,7},{7,6},{8,9},{9,8},{10,11... | collective-permute-start | bytes 2703368 | tf_op jit(solution)/shard_map/ppermute | solution.py:78
  82.3 2.9 %copy-start = (bf16[1,2560,320]{1,2,0:T(8,128)(2,1)S(1)}, bf16[1,2560,320]{1,2,0:T(8,128)(2,1)}, u32[]{:S(2)}) copy-start(bf16[1,2560,320]{1,2,0:T(8,128)(2,1)} %param.12) | copy-start | bytes 4915204
  91.9 4.9 %collective-permute-start.36 = (bf16[176,2560]{1,0:T(8,128)(2,1)}, bf16[176,2560]{1,0:T(8,128)(2,1)S(1)}, u32[]{:S(2)}, u32[]{:S(2)}) collective-permute-start(bf16[176,2560]{1,0:T(8,128)(2,1)} %shard_map.83.refs_0_), channel_id=1, source_target_pairs={{0,1},{1,0},{2,3},{3,2},{4,5},{5,4},{6,7},{7,6},{8,9},{9,8},{10,11... | collective-permute-start | bytes 2703368 | tf_op jit(solution)/shard_map/ppermute | solution.py:78
  96.8 1.9 %copy-start.4 = (f32[320,2560]{1,0:T(8,128)S(1)}, f32[320,2560]{1,0:T(8,128)}, u32[]{:S(2)}) copy-start(f32[320,2560]{1,0:T(8,128)} %get-tuple-element.154) | copy-start | bytes 9830404
  100.8 35.2 %collective-permute-start.15 = (bf16[320,512]{1,0:T(8,128)(2,1)S(1)}, bf16[320,512]{1,0:T(8,128)(2,1)S(1)}, u32[]{:S(2)}, u32[]{:S(2)}) collective-permute-start(bf16[320,512]{1,0:T(8,128)(2,1)S(1)} %get-tuple-element.115), channel_id=1, source_target_pairs={{448,0},{456,8},{464,16},{472,24},{480,32},{488,40},{496,48},{504,... | collective-permute-start | bytes 983048 | tf_op jit(solution)/shard_map/cond/branch_3_fun/ppermute | solution.py:196
  107.2 35.2 %collective-permute-start.18 = (bf16[320,512]{1,0:T(8,128)(2,1)S(1)}, bf16[320,512]{1,0:T(8,128)(2,1)S(1)}, u32[]{:S(2)}, u32[]{:S(2)}) collective-permute-start(bf16[320,512]{1,0:T(8,128)(2,1)S(1)} %get-tuple-element.118), channel_id=1, source_target_pairs={{448,0},{456,8},{464,16},{472,24},{480,32},{488,40},{496,48},{504,... | collective-permute-start | bytes 983048 | tf_op jit(solution)/shard_map/cond/branch_3_fun/ppermute | solution.py:196
  114.8 48.3 %collective-permute-start.17 = (bf16[320,768]{1,0:T(8,128)(2,1)S(1)}, bf16[320,768]{1,0:T(8,128)(2,1)S(1)}, u32[]{:S(2)}, u32[]{:S(2)}) collective-permute-start(bf16[320,768]{1,0:T(8,128)(2,1)S(1)} %get-tuple-element.117), channel_id=1, source_target_pairs={{448,0},{456,8},{464,16},{472,24},{480,32},{488,40},{496,48},{504,... | collective-permute-start | bytes 1474568 | tf_op jit(solution)/shard_map/cond/branch_3_fun/ppermute | solution.py:196
  119.4 66.5 %collective-permute-start.16 = (bf16[320,768]{1,0:T(8,128)(2,1)S(1)}, bf16[320,768]{1,0:T(8,128)(2,1)S(1)}, u32[]{:S(2)}, u32[]{:S(2)}) collective-permute-start(bf16[320,768]{1,0:T(8,128)(2,1)S(1)} %get-tuple-element.116), channel_id=1, source_target_pairs={{448,0},{456,8},{464,16},{472,24},{480,32},{488,40},{496,48},{504,... | collective-permute-start | bytes 1474568 | tf_op jit(solution)/shard_map/cond/branch_3_fun/ppermute | solution.py:196
  131.8 54.3 %collective-permute-start.19 = (f32[1]{0:T(128)}, f32[1]{0:T(128)}, u32[]{:S(2)}, u32[]{:S(2)}) collective-permute-start(f32[1]{0:T(128)} %get-tuple-element.119), channel_id=1, source_target_pairs={{448,0},{456,8},{464,16},{472,24},{480,32},{488,40},{496,48},{504,... | collective-permute-start | bytes 20 | tf_op jit(solution)/shard_map/cond/branch_3_fun/ppermute | solution.py:199
  186.2 1.2 copy-start.5
